TPU v7x, 256 devices: a whole 4x4x8 slice. The times are simulated.
256 devices in a mesh: lat: 16 (over y, x_hi, core), lon: 16 (over x_lo, z).
Axes of the slice: x: 4 (x_hi: 2, x_lo: 2; x = x_hi * 2 + x_lo), y: 4, z: 8, core: 2. Of those that a mesh axis runs over, the one named last changes fastest.
Arguments:
- atmos: bfloat16 [2, 5, 512, 4096], P(None, None, 'lat', 'lon'), may hold values from -6 to 6
- orography: bfloat16 [512, 4096], P('lat', 'lon'), may hold values from -6 to 6
- land_sea: int32 [512, 4096], P('lat', 'lon'), may hold values 0 or 1
- embed_weight: bfloat16 [12, 12, 6, 512], replicated, may hold values from -0.21875 to 0.21875
- level_embed: float32 [2, 512], replicated, may hold values from -6 to 6
- land_embed: float32 [512], replicated, may hold values from -6 to 6
- norm_gain: float32 [2, 512], replicated, may hold values from 0.1 to 1.9
- w_query: bfloat16 [2, 512, 512], replicated, may hold values from -12 to 12
- w_keyval: bfloat16 [2, 512, 1024], replicated, may hold values from -1 to 1
- w_out: bfloat16 [2, 512, 512], replicated, may hold values from -0.25 to 0.25
- merge_gain: float32 [2048], replicated, may hold values from 0.1 to 1.9
- merge_weight: bfloat16 [2048, 1024], replicated, may hold values from -0.125 to 0.125
Outputs:
- merged: bfloat16 [2, 64, 512, 1024], P(None, 'lat', 'lon')
All inputs are finite; a program needn't handle non-finite values. No bound on the sum of `land_sea` on one device may be relied on, other than what follows from the above.
Results may differ from a plain program's by a relative error of at most 0.015.
Values may be sent and summed in bfloat16 or wider, within the bound.
No kernel may reach another device: no remote copies, remote signals or barrier semaphores. Data moves between devices by JAX's collectives and lax.ppermute only.
A program may use at most 64 MiB of HBM per device.

v0:
```python
import math

import jax
import jax.numpy as jnp
from jax import lax
from jax.experimental import pallas as pl
from jax.experimental.pallas import tpu as pltpu
from jax.sharding import PartitionSpec as P

BF = jnp.bfloat16
F32 = jnp.float32
D = 512
HEAD_DIM = 64
WINS = 10
SCALE = HEAD_DIM ** (-0.5) * math.log2(math.e)
VMEM_LIMIT = 56 * 1024 * 1024


def iota(shape, dim):
    return lax.broadcasted_iota(jnp.int32, shape, dim)


def one_hot(cond):
    return jnp.where(cond, 1.0, 0.0).astype(BF)


def mm(a, b):
    return jnp.dot(a, b, preferred_element_type=F32)


def mm_t(a, b):
    return lax.dot_general(a, b, (((1,), (1,)), ((), ())), preferred_element_type=F32)


def params():
    return pltpu.CompilerParams(vmem_limit_bytes=VMEM_LIMIT)


def patch_kernel(par_ref, atmos_ref, oro_ref, land_ref, band_ref, edge_ref):
    par = par_ref[0]
    cells = jnp.concatenate(
        [
            atmos_ref[...].reshape(320, 256),
            oro_ref[...],
            land_ref[...].astype(F32).astype(BF),
        ],
        axis=0,
    )
    row, src = iota((1024, 384), 0), iota((1024, 384), 1)
    i, ch, r = row // 128, (row % 32) // 4, row % 4
    channel = jnp.where(ch < 5, ch, jnp.where(ch == 5, 10, jnp.where(ch == 6, 11, 9)))
    main = mm(one_hot(src == channel * 32 + i * 4 + r), cells)
    channel = 5 + (row % 16) // 4
    aux = mm(one_hot(src == channel * 32 + i * 4 + r), cells)
    row, col = iota((1024, 256), 0), iota((1024, 256), 1)
    c, half = (row % 128) // 32, (row % 32) // 16
    main = jnp.where(col % 4 == c, main, 0.0).astype(BF)
    aux = jnp.where((col % 4 == c) & (col // 128 == half), aux, 0.0).astype(BF)
    j, col = iota((64, 256), 0), iota((64, 256), 1)
    main = mm_t(one_hot(col // 4 == j), main).astype(BF)
    j, col = iota((32, 256), 0), iota((32, 256), 1)
    aux = mm_t(one_hot((col % 128) // 4 == j), aux).astype(BF)
    for i in range(8):
        band_ref[par + i, 0:64, :] = main[:, i * 128 : i * 128 + 128]
        band_ref[par + i, 64:96, :] = aux[:, i * 128 : i * 128 + 128]
    edge_ref[...] = band_ref[pl.ds(par + 7 * (1 - par), 1)]


def patches(par, atmos, orography, land_sea):
    return pl.pallas_call(
        patch_kernel,
        out_shape=(
            jax.ShapeDtypeStruct((9, 96, 128), BF),
            jax.ShapeDtypeStruct((1, 96, 128), BF),
        ),
        in_specs=[pl.BlockSpec(memory_space=pltpu.SMEM)] + [pl.BlockSpec(memory_space=pltpu.VMEM)] * 3,
        out_specs=(pl.BlockSpec(memory_space=pltpu.VMEM),) * 2,
        compiler_params=params(),
        cost_estimate=pl.CostEstimate(flops=10**9, bytes_accessed=10**6, transcendentals=0),
    )(par, atmos, orography, land_sea)


def unpack_kernel(par_ref, band_ref, far_ref, full_ref, low_ref, high_ref, packed):
    par = par_ref[0]
    packed[pl.ds(9 * (1 - par), 9)] = band_ref[...]
    packed[pl.ds(9 * par, 9)] = far_ref[...]
    k, n = iota((256, 256), 0), iota((256, 256), 1)
    ch, lane = (n % 32) // 4, n % 128
    from_main0 = jnp.where(ch == 7, lane - 4, lane)
    from_main1 = jnp.where(ch == 7, lane - 4, jnp.where(ch == 4, lane + 12, lane))
    aux = packed[:, 64:96, :]
    for half in range(2):
        from_one = jnp.where(ch < 4, 128 + lane + 16 * half, from_main1)
        pick = one_hot(k == jnp.where(n < 128, from_main0, from_one))
        both = jnp.concatenate([packed[:, half * 32 : half * 32 + 32, :], aux], axis=2)
        got = mm(both.reshape(18 * 32, 256), pick).astype(BF).reshape(18, 32, 256)
        for level in range(2):
            tile = got[:, :, level * 128 : level * 128 + 128]
            full_ref[level, :, half * 32 : half * 32 + 32, :] = tile
            if half == 0:
                low_ref[level] = tile[:, :16, :]
            else:
                high_ref[level] = tile[:, 16:, :]


def unpack(par, band, far):
    return pl.pallas_call(
        unpack_kernel,
        out_shape=(
            jax.ShapeDtypeStruct((2, 18, 64, 128), BF),
            jax.ShapeDtypeStruct((2, 18, 16, 128), BF),
            jax.ShapeDtypeStruct((2, 18, 16, 128), BF),
        ),
        in_specs=[pl.BlockSpec(memory_space=pltpu.SMEM)] + [pl.BlockSpec(memory_space=pltpu.VMEM)] * 2,
        out_specs=(pl.BlockSpec(memory_space=pltpu.VMEM),) * 3,
        scratch_shapes=[pltpu.VMEM((18, 96, 128), BF)],
        compiler_params=params(),
        cost_estimate=pl.CostEstimate(flops=10**9, bytes_accessed=10**6, transcendentals=0),
    )(par, band, far)


def normalize(x, gain):
    mean = jnp.mean(x, axis=-1, keepdims=True)
    x = x - mean
    var = jnp.mean(x * x, axis=-1, keepdims=True)
    return x * lax.rsqrt(var + 1e-05) * gain


def attend(q, k, v, bias):
    left = iota((128, 128), 1) < HEAD_DIM
    ones_left, ones_right = one_hot(left), one_hot(~left)
    zero = jnp.zeros((128, 128), BF)
    out = []
    for pair in range(4):
        at = slice(pair * 128, pair * 128 + 128)
        kp, vp = k[:, at], v[:, at]
        keys = jnp.concatenate([jnp.where(left, kp, zero), jnp.where(left, zero, kp)], axis=0)
        s = mm_t(q[:, at], keys)
        if bias is not None:
            s = s + bias
        s0, s1 = s[:, :128], s[:, 128:]
        p0 = jnp.exp2(s0 - jnp.max(s0, axis=-1, keepdims=True))
        p1 = jnp.exp2(s1 - jnp.max(s1, axis=-1, keepdims=True))
        p = jnp.concatenate([p0, p1], axis=1).astype(BF)
        vals = jnp.concatenate(
            [
                jnp.concatenate([jnp.where(left, vp, zero), ones_left], axis=1),
                jnp.concatenate([jnp.where(left, zero, vp), ones_right], axis=1),
            ],
            axis=0,
        )
        o = mm(p, vals)
        out.append((o[:, :128] / o[:, 128:]).astype(BF))
    return jnp.concatenate(out, axis=1)


def first_kernel(
    par_ref, full_ref, low_ref, high_ref, wemb_ref, lev_ref, gain_ref, wq_any, wkv_any, wo_any,
    x1_ref, send_ref,
    wide, gathered, x0, normed, query, keyval, heads, wq, wkv, wo, sems,
):
    par = par_ref[0]
    loads = [
        pltpu.make_async_copy(wq_any.at[0], wq, sems.at[0]),
        pltpu.make_async_copy(wkv_any.at[0], wkv, sems.at[1]),
        pltpu.make_async_copy(wo_any.at[0], wo, sems.at[2]),
    ]
    for load in loads:
        load.start()
    wide[:, :, 0:16, :] = low_ref[...].astype(F32)
    wide[:, :, 16:80, :] = full_ref[...].astype(F32)
    wide[:, :, 80:96, :] = high_ref[...].astype(F32)
    for dj in range(3):
        gathered[:, :, :, dj * 128 : dj * 128 + 128] = wide[:, :, 7 + dj : 87 + dj, :].astype(BF)
    gain = gain_ref[0:1, :]

    def embed(part):
        def one(t, carry):
            level, pair = t // 4, t % 4
            at = part * 8 + pair * 2
            lhs = jnp.concatenate(
                [gathered[level, pl.ds(at + di, 2)].reshape(160, 384) for di in range(3)], axis=1
            )
            x = mm(lhs, wemb_ref[...]) + lev_ref[pl.ds(level, 1), :]
            x0[level, pl.ds(pair * 2, 2)] = x.reshape(2, 80, D)
            return carry

        lax.fori_loop(0, 8, one, 0)

    def norm(w, carry):
        x = x0[:, :, pl.ds(pl.multiple_of(w * 8, 8), 8), :].reshape(128, D)
        normed[w] = normalize(x, gain).astype(BF).reshape(2, 4, 16, D)
        return carry

    def project_kv(w, carry):
        n = normed[pl.ds(w * 2, 2)].reshape(256, D)
        keyval[pl.ds(w * 2, 2)] = mm(n, wkv[...]).astype(BF).reshape(2, 128, 1024)
        return carry

    def store(w, rows_from, rows, out_from, value):
        old = x0[:, pl.ds(rows_from, rows), pl.ds(pl.multiple_of(w * 8, 8), 8), :]
        new = old + value.reshape(2, rows, 8, D)
        x1_ref[:, pl.ds(out_from, rows), pl.ds(pl.multiple_of(w * 8, 8), 8), :] = new

    embed(1 - par)
    lax.fori_loop(0, WINS, norm, 0)
    loads[0].wait()
    loads[1].wait()
    lax.fori_loop(0, WINS // 2, project_kv, 0)

    def own_query(w, carry):
        n = normed[pl.ds(w * 2, 2)].reshape(256, D)
        query[pl.ds(w * 4, 4)] = (mm(n, wq[...]) * SCALE).astype(BF).reshape(4, 64, D)
        return carry

    lax.fori_loop(0, WINS // 2, own_query, 0)

    def own_attend(w, carry):
        q = query[pl.ds(w * 2, 2)].reshape(128, D)
        kv = keyval[w]
        heads[pl.ds(w * 2, 2)] = attend(q, kv[:, :D], kv[:, D:], None).reshape(2, 64, D)
        return carry

    lax.fori_loop(0, WINS, own_attend, 0)
    loads[2].wait()

    def own_out(w, carry):
        out = mm(heads[pl.ds(w * 4, 4)].reshape(256, D), wo[...])
        for u in range(2):
            store(w * 2 + u, 0, 8, 4 * (1 - par), out[u * 128 : u * 128 + 128])
        return carry

    lax.fori_loop(0, WINS // 2, own_out, 0)

    half = 1 - par
    embed(par)
    lax.fori_loop(0, WINS, norm, 0)
    lax.fori_loop(0, WINS // 2, project_kv, 0)

    def outer_query(w, carry):
        n = normed[pl.ds(w * 5, 5), :, pl.ds(half * 2, 2)].reshape(320, D)
        query[pl.ds(w * 5, 5)] = (mm(n, wq[...]) * SCALE).astype(BF).reshape(5, 64, D)
        return carry

    lax.fori_loop(0, 2, outer_query, 0)

    def outer_attend(w, carry):
        kv = keyval[w]
        heads[w] = attend(query[w], kv[:, :D], kv[:, D:], None)
        return carry

    lax.fori_loop(0, WINS, outer_attend, 0)

    def outer_out(w, carry):
        out = mm(heads[pl.ds(w * 5, 5)].reshape(320, D), wo[...])
        for u in range(5):
            store(w * 5 + u, 4 * half, 4, 8 * par, out[u * 64 : u * 64 + 64])
        return carry

    lax.fori_loop(0, 2, outer_out, 0)
    send_ref[...] = x1_ref[:, pl.ds(8 * (1 - par), 4)].astype(BF)


def first_block(par, full, low, high, wemb, level_embed, norm_gain, w_query, w_keyval, w_out):
    vmem = pl.BlockSpec(memory_space=pltpu.VMEM)
    hbm = pl.BlockSpec(memory_space=pl.ANY)
    return pl.pallas_call(
        first_kernel,
        out_shape=(
            jax.ShapeDtypeStruct((2, 12, 80, D), F32),
            jax.ShapeDtypeStruct((2, 4, 80, D), BF),
        ),
        in_specs=[pl.BlockSpec(memory_space=pltpu.SMEM)] + [vmem] * 6 + [hbm] * 3,
        out_specs=(vmem, vmem),
        scratch_shapes=[
            pltpu.VMEM((2, 18, 96, 128), F32),
            pltpu.VMEM((2, 18, 80, 384), BF),
            pltpu.VMEM((2, 8, 80, D), F32),
            pltpu.VMEM((WINS, 2, 4, 16, D), BF),
            pltpu.VMEM((2 * WINS, 64, D), BF),
            pltpu.VMEM((WINS, 128, 1024), BF),
            pltpu.VMEM((2 * WINS, 64, D), BF),
            pltpu.VMEM((D, D), BF),
            pltpu.VMEM((D, 1024), BF),
            pltpu.VMEM((D, D), BF),
            pltpu.SemaphoreType.DMA((3,)),
        ],
        compiler_params=params(),
        cost_estimate=pl.CostEstimate(flops=2 * 10**10, bytes_accessed=10**7, transcendentals=0),
    )(par, full, low, high, wemb, level_embed, norm_gain, w_query, w_keyval, w_out)


SHIFTED = WINS - 1


def second_kernel(
    par_ref, x1_any, near_ref, gain_ref, mgain_ref, wq_any, wkv_any, wo_any, wm_any,
    out_ref,
    x1, x2, normed, query, keyval, heads, wq, wkv, wo, wm, sems,
):
    par, first, last = par_ref[0], par_ref[1], par_ref[2]
    loads = [
        pltpu.make_async_copy(x1_any, x1.at[:, pl.ds(4 * par, 12)], sems.at[0]),
        pltpu.make_async_copy(wkv_any.at[1], wkv, sems.at[1]),
        pltpu.make_async_copy(wq_any.at[1], wq, sems.at[2]),
        pltpu.make_async_copy(wo_any.at[1], wo, sems.at[3]),
        pltpu.make_async_copy(wm_any, wm, sems.at[4]),
    ]
    for load in loads:
        load.start()
    x1[:, pl.ds(12 * (1 - par), 4)] = near_ref[...].astype(F32)
    gain = gain_ref[1:2, :]
    upper = iota((8, D), 0) >= 4
    loads[0].wait()

    def window(w, rows_from, rows):
        at = pl.multiple_of(w * 8, 8)
        a = x1[:, pl.ds(rows_from, rows), pl.ds(at, 8), :]
        b = x1[:, pl.ds(rows_from, rows), pl.ds(pl.multiple_of(at + 8, 8), 8), :]
        return jnp.where(upper, a, b)

    def norm(t, carry):
        s, w = t // SHIFTED, t % SHIFTED
        x = window(w, s * 8, 8).reshape(128, D)
        normed[t] = normalize(x, gain).astype(BF).reshape(2, 4, 16, D)
        return carry

    lax.fori_loop(0, 2 * SHIFTED, norm, 0)
    loads[1].wait()

    def project_kv(t, carry):
        n = normed[pl.ds(t * 2, 2)].reshape(256, D)
        keyval[pl.ds(t * 2, 2)] = mm(n, wkv[...]).astype(BF).reshape(2, 128, 1024)
        return carry

    lax.fori_loop(0, SHIFTED, project_kv, 0)
    loads[2].wait()

    def project_q(t, carry):
        s, part = t // 3, t % 3
        at = s * SHIFTED + part * 3
        n = normed[pl.ds(at, 3), :, pl.ds((1 - s) * 2, 2)].reshape(192, D)
        query[pl.ds(at, 3)] = (mm(n, wq[...]) * SCALE).astype(BF).reshape(3, 64, D)
        return carry

    lax.fori_loop(0, 6, project_q, 0)
    key_row = (iota((1, 256), 1) // 8) % 8
    below = jnp.where(key_row < 4, F32(-1e30), F32(0))
    above = jnp.where(key_row < 4, F32(0), F32(-1e30))

    def one_attend(t, carry):
        s = t // SHIFTED
        cut_low = jnp.where(s == 0, first, 0).astype(F32)
        cut_high = jnp.where(s == 0, 0, last).astype(F32)
        bias = below * cut_low + above * cut_high
        kv = keyval[t]
        heads[t] = attend(query[t], kv[:, :D], kv[:, D:], bias)
        return carry

    lax.fori_loop(0, 2 * SHIFTED, one_attend, 0)
    loads[3].wait()

    def one_out(t, carry):
        s, part = t // 3, t % 3
        out = mm(heads[pl.ds(s * SHIFTED + part * 3, 3)].reshape(192, D), wo[...])
        for u in range(3):
            w = part * 3 + u
            new = window(w, 4 + s * 4, 4) + out[u * 64 : u * 64 + 64].reshape(2, 4, 8, D)
            at = pl.multiple_of(w * 8, 8)
            rows, here, after = pl.ds(s * 4, 4), pl.ds(at, 8), pl.ds(pl.multiple_of(at + 8, 8), 8)
            for c in range(4):
                piece = new[..., c * 128 : c * 128 + 128]
                old = x2[c, :, rows, here, :]
                x2[c, :, rows, here, :] = jnp.where(upper[:, :128], piece, old)
                x2[c, :, rows, after, :] = piece
        return carry

    lax.fori_loop(0, 6, one_out, 0)
    loads[4].wait()

    def merge(t, carry):
        level, half = t // 2, t % 2
        parts = []
        for p in range(4):
            got = [
                jnp.concatenate(
                    [
                        x2[c, level, half * 4 + 2 * a + p % 2, pl.ds(8 + p // 2, 32, stride=2), :]
                        for c in range(4)
                    ],
                    axis=1,
                )
                for a in range(2)
            ]
            parts.append(jnp.concatenate(got, axis=0))
        x = jnp.concatenate(parts, axis=1)
        n = normalize(x, mgain_ref[...]).astype(BF)
        out = mm(n, wm[...]).astype(BF)
        out_ref[level, pl.ds(half * 2, 2)] = out.reshape(2, 32, 1024)
        return carry

    lax.fori_loop(0, 4, merge, 0)


def second_block(par, x1, near, norm_gain, merge_gain, w_query, w_keyval, w_out, merge_weight):
    vmem = pl.BlockSpec(memory_space=pltpu.VMEM)
    hbm = pl.BlockSpec(memory_space=pl.ANY)
    return pl.pallas_call(
        second_kernel,
        out_shape=jax.ShapeDtypeStruct((2, 4, 32, 1024), BF),
        in_specs=[pl.BlockSpec(memory_space=pltpu.SMEM), hbm] + [vmem] * 3 + [hbm] * 4,
        out_specs=vmem,
        scratch_shapes=[
            pltpu.VMEM((2, 16, 80, D), F32),
            pltpu.VMEM((4, 2, 8, 80, 128), F32),
            pltpu.VMEM((2 * SHIFTED, 2, 4, 16, D), BF),
            pltpu.VMEM((2 * SHIFTED, 64, D), BF),
            pltpu.VMEM((2 * SHIFTED, 128, 1024), BF),
            pltpu.VMEM((2 * SHIFTED, 64, D), BF),
            pltpu.VMEM((D, D), BF),
            pltpu.VMEM((D, 1024), BF),
            pltpu.VMEM((D, D), BF),
            pltpu.VMEM((4 * D, 1024), BF),
            pltpu.SemaphoreType.DMA((5,)),
        ],
        compiler_params=params(),
        cost_estimate=pl.CostEstimate(flops=10**10, bytes_accessed=10**7, transcendentals=0),
    )(par, x1, near, norm_gain, merge_gain, w_query, w_keyval, w_out, merge_weight)


def embedding_matrix(embed_weight, land_embed):
    w = embed_weight.reshape(3, 4, 3, 4, 6, D).transpose(0, 2, 3, 4, 1, 5)
    share = land_embed / 16
    high = lax.reduce_precision(share, 8, 7)
    terms = jnp.stack([high, share - high]).astype(BF)
    terms = jnp.broadcast_to(terms[None, :, None, :], (4, 2, 4, D))
    middle = (jnp.arange(9) == 4).reshape(3, 3, 1, 1, 1, 1)
    land = jnp.where(middle, terms, jnp.zeros((), BF))
    return jnp.concatenate([w, land], axis=3).reshape(9 * 128, D)


def swap(block, first):
    count = lax.axis_size("lat")
    pairs = []
    for i in range(first, count - 1, 2):
        pairs += [(i, i + 1), (i + 1, i)]
    return lax.ppermute(block, "lat", pairs)


def around(block, distance):
    count = lax.axis_size("lon")
    return lax.ppermute(block, "lon", [(i, (i + distance) % count) for i in range(count)])


def shards(
    atmos, orography, land_sea, embed_weight, level_embed, land_embed, norm_gain,
    w_query, w_keyval, w_out, merge_gain, merge_weight,
):
    lat = lax.axis_index("lat")
    par = lat % 2
    place = jnp.stack([par, lat == 0, lat == lax.axis_size("lat") - 1]).astype(jnp.int32)
    band, edge = patches(place, atmos, orography, land_sea)
    edge = swap(edge, 0)
    band = lax.dynamic_update_slice(band, edge, (8 * (1 - par), 0, 0))
    far = swap(band, 1)
    full, low, high = unpack(place, band, far)
    from_low, from_high = around(high, 1), around(low, -1)
    wemb = embedding_matrix(embed_weight, land_embed)
    x1, send = first_block(
        place, full, from_low, from_high, wemb, level_embed, norm_gain, w_query, w_keyval, w_out
    )
    near = swap(send, 0)
    return second_block(
        place, x1, near, norm_gain, merge_gain.reshape(1, -1), w_query, w_keyval, w_out, merge_weight
    )


def solution(mesh):
    in_specs = (P(None, None, "lat", "lon"), P("lat", "lon"), P("lat", "lon")) + (P(),) * 9
    out_specs = P(None, "lat", "lon", None)
    return jax.shard_map(shards, mesh=mesh, in_specs=in_specs, out_specs=out_specs, check_vma=False)
```

profile of v0, /device:TPU:25, one launch (start us, length us, event | category | flops | bytes accessed | tf_op | source)
XLA Modules:
  0.0 95.8 jit_solution(7143601030780124326)
XLA Ops:
  0.0 0.6 pad_add_fusion.par_ref
  0.6 0.0 copy-start.1
  0.6 2.9 %shard_map.118 = (bf16[9,96,128]{2,1,0:T(8,128)(2,1)}, bf16[1,96,128]{2,1,0:T(8,128)(2,1)}) custom-call(s32[3]{0:T(128)} %pad_add_fusion.par_ref, bf16[2,5,32,256]{3,2,1,0:T(8,128)(2,1)} %atmos_ref.1, bf16[32,256]{1,0:T(8,128)(2,1)} %oro_ref.1, s32[32,256]{1,0:T(8,128)} %land_ref.1), custom_call_target="tpu_custom_call" | custom-call | flops 1000000000 | bytes 1000000 | tf_op jit(solution)/shard_map/pallas_call | solution.py:70
  3.5 0.7 collective-permute-start
  4.1 0.0 copy-done.1
  4.2 1.0 %collective-permute-done = bf16[1,96,128]{2,1,0:T(8,128)(2,1)S(1)} collective-permute-done((bf16[1,96,128]{2,1,0:T(8,128)(2,1)}, bf16[1,96,128]{2,1,0:T(8,128)(2,1)S(1)}, u32[]{:S(2)}, u32[]{:S(2)}) %collective-permute-start) | collective-permute-done | bytes 24608 | tf_op jit(solution)/shard_map/ppermute | solution.py:447
  5.2 0.6 constant_dynamic-update-slice_fusion.band_ref
  5.8 4.9 %collective-permute-start.1 = (bf16[9,96,128]{2,1,0:T(8,128)(2,1)}, bf16[9,96,128]{2,1,0:T(8,128)(2,1)S(1)}, u32[]{:S(2)}, u32[]{:S(2)}) collective-permute-start(bf16[9,96,128]{2,1,0:T(8,128)(2,1)} %constant_dynamic-update-slice_fusion.band_ref), channel_id=1, source_target_pairs={{16,32},{32,16},{48,64},{64,48},{80,96},{96,80},{112,128},{128,112... | collective-permute-start | bytes 663560 | tf_op jit(solution)/shard_map/ppermute | solution.py:447
  10.7 0.0 copy-start
  10.7 5.0 %collective-permute-done.1.far_ref = bf16[9,96,128]{2,1,0:T(8,128)(2,1)S(1)} collective-permute-done((bf16[9,96,128]{2,1,0:T(8,128)(2,1)}, bf16[9,96,128]{2,1,0:T(8,128)(2,1)S(1)}, u32[]{:S(2)}, u32[]{:S(2)}) %collective-permute-start.1) | collective-permute-done | bytes 221216 | tf_op jit(solution)/shard_map/ppermute | solution.py:447
  15.8 0.0 copy-start.3
  15.8 0.7 copy-done.3
  16.5 2.3 %shard_map.119 = (bf16[2,18,64,128]{3,2,1,0:T(8,128)(2,1)}, bf16[2,18,16,128]{3,2,1,0:T(8,128)(2,1)}, bf16[2,18,16,128]{3,2,1,0:T(8,128)(2,1)}) custom-call(s32[3]{0:T(128)} %pad_add_fusion.par_ref, bf16[9,96,128]{2,1,0:T(8,128)(2,1)} %constant_dynamic-update-slice_fusion.band_ref, bf16[9,96,128]{2,1,0:T(8,128)(2,1)} %copy-done.3), custom_call_target="tpu_custom_call" | custom-call | flops 1000000000 | bytes 1000000 | tf_op jit(solution)/shard_map/pallas_call | solution.py:107
  18.8 1.6 %collective-permute-start.2 = (bf16[2,18,16,128]{3,2,1,0:T(8,128)(2,1)}, bf16[2,18,16,128]{3,2,1,0:T(8,128)(2,1)S(1)}, u32[]{:S(2)}, u32[]{:S(2)}) collective-permute-start(bf16[2,18,16,128]{3,2,1,0:T(8,128)(2,1)} %get-tuple-element.15), channel_id=1, source_target_pairs={{0,1},{1,2},{2,3},{3,4},{4,5},{5,6},{6,7},{7,8},{8,9},{9,10},{10,1... | collective-permute-start | bytes 442376 | tf_op jit(solution)/shard_map/ppermute | solution.py:452
  20.4 4.2 %collective-permute-start.3 = (bf16[2,18,16,128]{3,2,1,0:T(8,128)(2,1)}, bf16[2,18,16,128]{3,2,1,0:T(8,128)(2,1)S(1)}, u32[]{:S(2)}, u32[]{:S(2)}) collective-permute-start(bf16[2,18,16,128]{3,2,1,0:T(8,128)(2,1)} %get-tuple-element.16), channel_id=1, source_target_pairs={{0,15},{1,0},{2,1},{3,2},{4,3},{5,4},{6,5},{7,6},{8,7},{9,8},{10,9... | collective-permute-start | bytes 442376 | tf_op jit(solution)/shard_map/ppermute | solution.py:452
  24.6 0.1 broadcast_select_fusion
  24.7 0.0 copy-done
  24.8 0.7 copy.15
  25.5 0.8 pad_maximum_fusion
  26.2 1.2 %reshape.38.wemb_ref = bf16[1152,512]{1,0:T(8,128)(2,1)} reshape(bf16[3,3,4,8,4,512]{5,4,3,2,1,0:T(4,128)(2,1)S(1)} %pad_maximum_fusion) | data formatting | bytes 2359296 | tf_op jit(solution)/shard_map/reshape | solution.py:439
  27.4 0.0 collective-permute-done.2.low_ref
  27.4 0.0 copy-start.4
  27.4 0.0 collective-permute-done.3.high_ref
  27.4 0.0 copy-start.5
  27.4 0.6 copy-done.4
  28.1 0.0 copy-done.5
  28.1 33.0 %shard_map.120 = (f32[2,12,80,512]{3,2,1,0:T(8,128)}, bf16[2,4,80,512]{3,2,1,0:T(8,128)(2,1)}) custom-call(s32[3]{0:T(128)} %pad_add_fusion.par_ref, bf16[2,18,64,128]{3,2,1,0:T(8,128)(2,1)} %get-tuple-element.14.full_ref, bf16[2,18,16,128]{3,2,1,0:T(8,128)(2,1)} %copy-done.4, bf16[2,18,16,128]{3,2,1,0:T(8,128)(2,1)} %copy-done.5, ...), custom_call_target="tpu_custom_call" | custom-call | flops 20000000000 | bytes 10000000 | tf_op jit(solution)/shard_map/pallas_call | solution.py:267
  61.1 3.8 %collective-permute-start.4 = (bf16[2,4,80,512]{3,2,1,0:T(8,128)(2,1)}, bf16[2,4,80,512]{3,2,1,0:T(8,128)(2,1)S(1)}, u32[]{:S(2)}, u32[]{:S(2)}) collective-permute-start(bf16[2,4,80,512]{3,2,1,0:T(8,128)(2,1)} %get-tuple-element.18), channel_id=1, source_target_pairs={{0,16},{16,0},{32,48},{48,32},{64,80},{80,64},{96,112},{112,96},{1... | collective-permute-start | bytes 1966088 | tf_op jit(solution)/shard_map/ppermute | solution.py:447
  64.9 1.9 %collective-permute-done.4.near_ref = bf16[2,4,80,512]{3,2,1,0:T(8,128)(2,1)S(1)} collective-permute-done((bf16[2,4,80,512]{3,2,1,0:T(8,128)(2,1)}, bf16[2,4,80,512]{3,2,1,0:T(8,128)(2,1)S(1)}, u32[]{:S(2)}, u32[]{:S(2)}) %collective-permute-start.4) | collective-permute-done | bytes 655392 | tf_op jit(solution)/shard_map/ppermute | solution.py:447
  66.8 0.0 copy-start.2
  66.8 0.8 copy-done.2
  67.7 28.2 %shard_map.121 = bf16[2,4,32,1024]{3,2,1,0:T(8,128)(2,1)} custom-call(s32[3]{0:T(128)} %pad_add_fusion.par_ref, f32[2,12,80,512]{3,2,1,0:T(8,128)} %get-tuple-element.17.x1_any, bf16[2,4,80,512]{3,2,1,0:T(8,128)(2,1)} %copy-done.2, f32[2,512]{1,0:T(2,128)} %gain_ref.3, f32[1,2048]{1,0:T(1,128)} %bitcast.10, bf16[2,512,512]{2,1,0:T(8,128)(2,1)} %wq_any.3, ...), custom_call_target="tpu_custom_call" | custom-call | flops 10000000000 | bytes 10000000 | tf_op jit(solution)/shard_map/pallas_call | solution.py:408
  (5 shorter events, 0.0 us)
Async XLA Ops:
  0.6 3.5 %copy-start.1 = (f32[512]{0:T(512)S(1)}, f32[512]{0:T(512)}, u32[]{:S(2)}) copy-start(f32[512]{0:T(512)} %param.17) | copy-start | bytes 6148
  3.5 1.7 %collective-permute-start = (bf16[1,96,128]{2,1,0:T(8,128)(2,1)}, bf16[1,96,128]{2,1,0:T(8,128)(2,1)S(1)}, u32[]{:S(2)}, u32[]{:S(2)}) collective-permute-start(bf16[1,96,128]{2,1,0:T(8,128)(2,1)} %get-tuple-element.13), channel_id=1, source_target_pairs={{0,16},{16,0},{32,48},{48,32},{64,80},{80,64},{96,112},{112,96},{1... | collective-permute-start | bytes 73736 | tf_op jit(solution)/shard_map/ppermute | solution.py:447
  5.8 10.0 %collective-permute-start.1 = (bf16[9,96,128]{2,1,0:T(8,128)(2,1)}, bf16[9,96,128]{2,1,0:T(8,128)(2,1)S(1)}, u32[]{:S(2)}, u32[]{:S(2)}) collective-permute-start(bf16[9,96,128]{2,1,0:T(8,128)(2,1)} %constant_dynamic-update-slice_fusion.band_ref), channel_id=1, source_target_pairs={{16,32},{32,16},{48,64},{64,48},{80,96},{96,80},{112,128},{128,112... | collective-permute-start | bytes 663560 | tf_op jit(solution)/shard_map/ppermute | solution.py:447
  10.7 14.0 %copy-start = (bf16[12,12,6,512]{3,2,1,0:T(8,128)(2,1)S(1)}, bf16[12,12,6,512]{3,2,1,0:T(8,128)(2,1)}, u32[]{:S(2)}) copy-start(bf16[12,12,6,512]{3,2,1,0:T(8,128)(2,1)} %param.15) | copy-start | bytes 2654212
  15.8 0.7 copy-start.3
  18.8 8.6 %collective-permute-start.2 = (bf16[2,18,16,128]{3,2,1,0:T(8,128)(2,1)}, bf16[2,18,16,128]{3,2,1,0:T(8,128)(2,1)S(1)}, u32[]{:S(2)}, u32[]{:S(2)}) collective-permute-start(bf16[2,18,16,128]{3,2,1,0:T(8,128)(2,1)} %get-tuple-element.15), channel_id=1, source_target_pairs={{0,1},{1,2},{2,3},{3,4},{4,5},{5,6},{6,7},{7,8},{8,9},{9,10},{10,1... | collective-permute-start | bytes 442376 | tf_op jit(solution)/shard_map/ppermute | solution.py:452
  20.4 7.0 %collective-permute-start.3 = (bf16[2,18,16,128]{3,2,1,0:T(8,128)(2,1)}, bf16[2,18,16,128]{3,2,1,0:T(8,128)(2,1)S(1)}, u32[]{:S(2)}, u32[]{:S(2)}) collective-permute-start(bf16[2,18,16,128]{3,2,1,0:T(8,128)(2,1)} %get-tuple-element.16), channel_id=1, source_target_pairs={{0,15},{1,0},{2,1},{3,2},{4,3},{5,4},{6,5},{7,6},{8,7},{9,8},{10,9... | collective-permute-start | bytes 442376 | tf_op jit(solution)/shard_map/ppermute | solution.py:452
  27.4 0.7 copy-start.4
  27.4 0.7 copy-start.5
  61.1 5.8 %collective-permute-start.4 = (bf16[2,4,80,512]{3,2,1,0:T(8,128)(2,1)}, bf16[2,4,80,512]{3,2,1,0:T(8,128)(2,1)S(1)}, u32[]{:S(2)}, u32[]{:S(2)}) collective-permute-start(bf16[2,4,80,512]{3,2,1,0:T(8,128)(2,1)} %get-tuple-element.18), channel_id=1, source_target_pairs={{0,16},{16,0},{32,48},{48,32},{64,80},{80,64},{96,112},{112,96},{1... | collective-permute-start | bytes 1966088 | tf_op jit(solution)/shard_map/ppermute | solution.py:447
  66.8 0.8 copy-start.2
where the time goes:
time: 96.6 us; the launch traced here: 95.8 us
  Pallas kernels  66.3 us (69%)
  starting transfers between devices  15.2 us (16%)
  waiting for transfers between devices  8.01 us (8%)
  local copies, waits for them, and re-layouts  4.71 us (5%)
  other arithmetic  1.53 us (2%)
    pallas_call x1, Pallas kernels, first_block(): pl.pallas_call(first_kernel, out_shape=(jax.ShapeDtypeStruct((2, 12, 80,...  33 us
    pallas_call x1, Pallas kernels, second_block(): pl.pallas_call(second_kernel, out_shape=jax.ShapeDtypeStruct((2, 4, 32, 1...  28.2 us
    ppermute x3, starting transfers between devices, swap(): return lax.ppermute(block, 'lat', pairs)  9.37 us
    ppermute x3, waiting for transfers between devices, swap(): return lax.ppermute(block, 'lat', pairs)  8.01 us
    ppermute x2, starting transfers between devices, around(): lax.ppermute(block, 'lon', [(i, (i + distance) % count) for i in range(co...  5.8 us
    pallas_call x1, Pallas kernels, patches(): pl.pallas_call(patch_kernel, out_shape=(jax.ShapeDtypeStruct((9, 96, 128)...  2.86 us
    pallas_call x1, Pallas kernels, unpack(): pl.pallas_call(unpack_kernel, out_shape=(jax.ShapeDtypeStruct((2, 18, 64,...  2.34 us
    unnamed x12, local copies, waits for them, and re-layouts  2.23 us
  transfers between devices with their start and end apart: 5, of which 3 were waited for; matrix products, arithmetic and copies ran while one was open for 3% of the time, Pallas kernels for 0%

commit v1 on v0

--- a/solution.py
+++ b/solution.py
@@ -119,6 +119,11 @@
     )(par, band, far)
 
 
+def steps(count, body):
+    for t in range(count):
+        body(t)
+
+
 def normalize(x, gain):
     mean = jnp.mean(x, axis=-1, keepdims=True)
     x = x - mean
@@ -175,89 +180,80 @@
     gain = gain_ref[0:1, :]
 
     def embed(part):
-        def one(t, carry):
+        def one(t):
             level, pair = t // 4, t % 4
             at = part * 8 + pair * 2
             lhs = jnp.concatenate(
                 [gathered[level, pl.ds(at + di, 2)].reshape(160, 384) for di in range(3)], axis=1
             )
-            x = mm(lhs, wemb_ref[...]) + lev_ref[pl.ds(level, 1), :]
+            x = mm(lhs, wemb_ref[...]) + lev_ref[level : level + 1, :]
             x0[level, pl.ds(pair * 2, 2)] = x.reshape(2, 80, D)
-            return carry
-
-        lax.fori_loop(0, 8, one, 0)
-
-    def norm(w, carry):
-        x = x0[:, :, pl.ds(pl.multiple_of(w * 8, 8), 8), :].reshape(128, D)
+
+        steps(8, one)
+
+    def norm(w):
+        x = x0[:, :, pl.ds(w * 8, 8), :].reshape(128, D)
         normed[w] = normalize(x, gain).astype(BF).reshape(2, 4, 16, D)
-        return carry
-
-    def project_kv(w, carry):
+
+    def project_kv(w):
         n = normed[pl.ds(w * 2, 2)].reshape(256, D)
         keyval[pl.ds(w * 2, 2)] = mm(n, wkv[...]).astype(BF).reshape(2, 128, 1024)
-        return carry
 
     def store(w, rows_from, rows, out_from, value):
-        old = x0[:, pl.ds(rows_from, rows), pl.ds(pl.multiple_of(w * 8, 8), 8), :]
+        old = x0[:, pl.ds(rows_from, rows), pl.ds(w * 8, 8), :]
         new = old + value.reshape(2, rows, 8, D)
-        x1_ref[:, pl.ds(out_from, rows), pl.ds(pl.multiple_of(w * 8, 8), 8), :] = new
+        x1_ref[:, pl.ds(out_from, rows), pl.ds(w * 8, 8), :] = new
 
     embed(1 - par)
-    lax.fori_loop(0, WINS, norm, 0)
+    steps(WINS, norm)
     loads[0].wait()
     loads[1].wait()
-    lax.fori_loop(0, WINS // 2, project_kv, 0)
-
-    def own_query(w, carry):
+    steps(WINS // 2, project_kv)
+
+    def own_query(w):
         n = normed[pl.ds(w * 2, 2)].reshape(256, D)
         query[pl.ds(w * 4, 4)] = (mm(n, wq[...]) * SCALE).astype(BF).reshape(4, 64, D)
-        return carry
-
-    lax.fori_loop(0, WINS // 2, own_query, 0)
-
-    def own_attend(w, carry):
+
+    steps(WINS // 2, own_query)
+
+    def own_attend(w):
         q = query[pl.ds(w * 2, 2)].reshape(128, D)
         kv = keyval[w]
         heads[pl.ds(w * 2, 2)] = attend(q, kv[:, :D], kv[:, D:], None).reshape(2, 64, D)
-        return carry
-
-    lax.fori_loop(0, WINS, own_attend, 0)
+
+    steps(WINS, own_attend)
     loads[2].wait()
 
-    def own_out(w, carry):
+    def own_out(w):
         out = mm(heads[pl.ds(w * 4, 4)].reshape(256, D), wo[...])
         for u in range(2):
             store(w * 2 + u, 0, 8, 4 * (1 - par), out[u * 128 : u * 128 + 128])
-        return carry
-
-    lax.fori_loop(0, WINS // 2, own_out, 0)
+
+    steps(WINS // 2, own_out)
 
     half = 1 - par
     embed(par)
-    lax.fori_loop(0, WINS, norm, 0)
-    lax.fori_loop(0, WINS // 2, project_kv, 0)
-
-    def outer_query(w, carry):
+    steps(WINS, norm)
+    steps(WINS // 2, project_kv)
+
+    def outer_query(w):
         n = normed[pl.ds(w * 5, 5), :, pl.ds(half * 2, 2)].reshape(320, D)
         query[pl.ds(w * 5, 5)] = (mm(n, wq[...]) * SCALE).astype(BF).reshape(5, 64, D)
-        return carry
-
-    lax.fori_loop(0, 2, outer_query, 0)
-
-    def outer_attend(w, carry):
+
+    steps(2, outer_query)
+
+    def outer_attend(w):
         kv = keyval[w]
         heads[w] = attend(query[w], kv[:, :D], kv[:, D:], None)
-        return carry
-
-    lax.fori_loop(0, WINS, outer_attend, 0)
-
-    def outer_out(w, carry):
+
+    steps(WINS, outer_attend)
+
+    def outer_out(w):
         out = mm(heads[pl.ds(w * 5, 5)].reshape(320, D), wo[...])
         for u in range(5):
             store(w * 5 + u, 4 * half, 4, 8 * par, out[u * 64 : u * 64 + 64])
-        return carry
-
-    lax.fori_loop(0, 2, outer_out, 0)
+
+    steps(2, outer_out)
     send_ref[...] = x1_ref[:, pl.ds(8 * (1 - par), 4)].astype(BF)
 
 
@@ -314,71 +310,64 @@
     loads[0].wait()
 
     def window(w, rows_from, rows):
-        at = pl.multiple_of(w * 8, 8)
+        at = w * 8
         a = x1[:, pl.ds(rows_from, rows), pl.ds(at, 8), :]
-        b = x1[:, pl.ds(rows_from, rows), pl.ds(pl.multiple_of(at + 8, 8), 8), :]
+        b = x1[:, pl.ds(rows_from, rows), pl.ds(at + 8, 8), :]
         return jnp.where(upper, a, b)
 
-    def norm(t, carry):
+    def norm(t):
         s, w = t // SHIFTED, t % SHIFTED
         x = window(w, s * 8, 8).reshape(128, D)
         normed[t] = normalize(x, gain).astype(BF).reshape(2, 4, 16, D)
-        return carry
-
-    lax.fori_loop(0, 2 * SHIFTED, norm, 0)
+
+    steps(2 * SHIFTED, norm)
     loads[1].wait()
 
-    def project_kv(t, carry):
+    def project_kv(t):
         n = normed[pl.ds(t * 2, 2)].reshape(256, D)
         keyval[pl.ds(t * 2, 2)] = mm(n, wkv[...]).astype(BF).reshape(2, 128, 1024)
-        return carry
-
-    lax.fori_loop(0, SHIFTED, project_kv, 0)
+
+    steps(SHIFTED, project_kv)
     loads[2].wait()
 
-    def project_q(t, carry):
+    def project_q(t):
         s, part = t // 3, t % 3
         at = s * SHIFTED + part * 3
         n = normed[pl.ds(at, 3), :, pl.ds((1 - s) * 2, 2)].reshape(192, D)
         query[pl.ds(at, 3)] = (mm(n, wq[...]) * SCALE).astype(BF).reshape(3, 64, D)
-        return carry
-
-    lax.fori_loop(0, 6, project_q, 0)
+
+    steps(6, project_q)
     key_row = (iota((1, 256), 1) // 8) % 8
     below = jnp.where(key_row < 4, F32(-1e30), F32(0))
     above = jnp.where(key_row < 4, F32(0), F32(-1e30))
 
-    def one_attend(t, carry):
+    def one_attend(t):
         s = t // SHIFTED
-        cut_low = jnp.where(s == 0, first, 0).astype(F32)
-        cut_high = jnp.where(s == 0, 0, last).astype(F32)
-        bias = below * cut_low + above * cut_high
+        bias = above * last.astype(F32) if s else below * first.astype(F32)
         kv = keyval[t]
         heads[t] = attend(query[t], kv[:, :D], kv[:, D:], bias)
-        return carry
-
-    lax.fori_loop(0, 2 * SHIFTED, one_attend, 0)
+
+    steps(2 * SHIFTED, one_attend)
     loads[3].wait()
 
-    def one_out(t, carry):
+    def one_out(t):
         s, part = t // 3, t % 3
         out = mm(heads[pl.ds(s * SHIFTED + part * 3, 3)].reshape(192, D), wo[...])
         for u in range(3):
             w = part * 3 + u
             new = window(w, 4 + s * 4, 4) + out[u * 64 : u * 64 + 64].reshape(2, 4, 8, D)
-            at = pl.multiple_of(w * 8, 8)
-            rows, here, after = pl.ds(s * 4, 4), pl.ds(at, 8), pl.ds(pl.multiple_of(at + 8, 8), 8)
+            at = w * 8
+            rows, here, after = pl.ds(s * 4, 4), pl.ds(at, 8), pl.ds(at + 8, 8)
             for c in range(4):
                 piece = new[..., c * 128 : c * 128 + 128]
                 old = x2[c, :, rows, here, :]
                 x2[c, :, rows, here, :] = jnp.where(upper[:, :128], piece, old)
                 x2[c, :, rows, after, :] = piece
-        return carry
-
-    lax.fori_loop(0, 6, one_out, 0)
+
+    steps(6, one_out)
     loads[4].wait()
 
-    def merge(t, carry):
+    def merge(t):
         level, half = t // 2, t % 2
         parts = []
         for p in range(4):
@@ -397,9 +386,8 @@
         n = normalize(x, mgain_ref[...]).astype(BF)
         out = mm(n, wm[...]).astype(BF)
         out_ref[level, pl.ds(half * 2, 2)] = out.reshape(2, 32, 1024)
-        return carry
-
-    lax.fori_loop(0, 4, merge, 0)
+
+    steps(4, merge)
 
 
 def second_block(par, x1, near, norm_gain, merge_gain, w_query, w_keyval, w_out, merge_weight):
@@ -463,9 +451,10 @@
     edge = swap(edge, 0)
     band = lax.dynamic_update_slice(band, edge, (8 * (1 - par), 0, 0))
     far = swap(band, 1)
+    wemb = embedding_matrix(embed_weight, land_embed)
+    far, wemb = lax.optimization_barrier((far, wemb))
     full, low, high = unpack(place, band, far)
     from_low, from_high = around(high, 1), around(low, -1)
-    wemb = embedding_matrix(embed_weight, land_embed)
     x1, send = first_block(
         place, full, from_low, from_high, wemb, level_embed, norm_gain, w_query, w_keyval, w_out
     )

time: 96.6 us -> 69.9 us (0.72)
  Pallas kernels: 66.3 us -> 39.4 us
    pallas_call x1, Pallas kernels: 33 us -> 17.3 us  [first_block(): pl.pallas_call(first_kernel, out_shape=(jax.ShapeDtypeStruct((2, 12, 80,...]
    pallas_call x1, Pallas kernels: 28.2 us -> 16.8 us  [second_block(): pl.pallas_call(second_kernel, out_shape=jax.ShapeDtypeStruct((2, 4, 32, 1...]
    ppermute x3, waiting for transfers between devices: 8.01 us -> 5.21 us  [swap(): return lax.ppermute(block, 'lat', pairs)]
    ppermute x2, waiting for transfers between devices: 0.01 us -> 2.74 us  [around(): lax.ppermute(block, 'lon', [(i, (i + distance) % count) for i in range(co...]
  transfers between devices with their start and end apart: 5 -> 5, of which waited for: 3 -> 4; matrix products, arithmetic and copies ran while one was open for 3% -> 4% of each run, Pallas kernels for 0% -> 0%
where the time goes in v1:
time: 69.9 us; the launch traced here: 69.1 us
  Pallas kernels  39.4 us (56%)
  starting transfers between devices  15.2 us (22%)
  waiting for transfers between devices  7.95 us (11%)
  local copies, waits for them, and re-layouts  4.72 us (7%)
  other arithmetic  1.53 us (2%)
    pallas_call x1, Pallas kernels, first_block(): pl.pallas_call(first_kernel, out_shape=(jax.ShapeDtypeStruct((2, 12, 80,...  17.3 us
    pallas_call x1, Pallas kernels, second_block(): pl.pallas_call(second_kernel, out_shape=jax.ShapeDtypeStruct((2, 4, 32, 1...  16.8 us
    ppermute x3, starting transfers between devices, swap(): return lax.ppermute(block, 'lat', pairs)  9.45 us
    ppermute x2, starting transfers between devices, around(): lax.ppermute(block, 'lon', [(i, (i + distance) % count) for i in range(co...  5.79 us
    ppermute x3, waiting for transfers between devices, swap(): return lax.ppermute(block, 'lat', pairs)  5.21 us
    pallas_call x1, Pallas kernels, patches(): pl.pallas_call(patch_kernel, out_shape=(jax.ShapeDtypeStruct((9, 96, 128)...  2.94 us
    ppermute x2, waiting for transfers between devices, around(): lax.ppermute(block, 'lon', [(i, (i + distance) % count) for i in range(co...  2.74 us
    pallas_call x1, Pallas kernels, unpack(): pl.pallas_call(unpack_kernel, out_shape=(jax.ShapeDtypeStruct((2, 18, 64,...  2.35 us
  transfers between devices with their start and end apart: 5, of which 4 were waited for; matrix products, arithmetic and copies ran while one was open for 4% of the time, Pallas kernels for 0%

profile of v1, /device:TPU:25, one launch (start us, length us, event | category | flops | bytes accessed | tf_op | source)
XLA Modules:
  0.0 69.1 jit_solution(14375152864490272805)
XLA Ops:
  0.0 0.6 pad_add_fusion.par_ref
  0.6 0.0 copy-start.1
  0.6 0.0 copy-start
  0.6 2.9 %shard_map.118 = (bf16[9,96,128]{2,1,0:T(8,128)(2,1)}, bf16[1,96,128]{2,1,0:T(8,128)(2,1)}) custom-call(s32[3]{0:T(128)} %pad_add_fusion.par_ref, bf16[2,5,32,256]{3,2,1,0:T(8,128)(2,1)} %atmos_ref.1, bf16[32,256]{1,0:T(8,128)(2,1)} %oro_ref.1, s32[32,256]{1,0:T(8,128)} %land_ref.1), custom_call_target="tpu_custom_call" | custom-call | flops 1000000000 | bytes 1000000 | tf_op jit(solution)/shard_map/pallas_call | solution.py:70
  3.5 0.7 collective-permute-start
  4.2 0.0 copy-done.1
  4.3 1.0 %collective-permute-done = bf16[1,96,128]{2,1,0:T(8,128)(2,1)S(1)} collective-permute-done((bf16[1,96,128]{2,1,0:T(8,128)(2,1)}, bf16[1,96,128]{2,1,0:T(8,128)(2,1)S(1)}, u32[]{:S(2)}, u32[]{:S(2)}) %collective-permute-start) | collective-permute-done | bytes 24608 | tf_op jit(solution)/shard_map/ppermute | solution.py:435
  5.3 0.6 constant_dynamic-update-slice_fusion.band_ref
  5.9 4.9 %collective-permute-start.1 = (bf16[9,96,128]{2,1,0:T(8,128)(2,1)}, bf16[9,96,128]{2,1,0:T(8,128)(2,1)S(1)}, u32[]{:S(2)}, u32[]{:S(2)}) collective-permute-start(bf16[9,96,128]{2,1,0:T(8,128)(2,1)} %constant_dynamic-update-slice_fusion.band_ref), channel_id=1, source_target_pairs={{16,32},{32,16},{48,64},{64,48},{80,96},{96,80},{112,128},{128,112... | collective-permute-start | bytes 663560 | tf_op jit(solution)/shard_map/ppermute | solution.py:435
  10.8 0.1 broadcast_select_fusion
  10.9 0.0 copy-done
  10.9 0.7 %copy.15 = bf16[3,4,3,4,6,512]{5,1,4,3,2,0:T(4,128)(2,1)S(1)} copy(bf16[3,4,3,4,6,512]{5,4,3,2,1,0:T(8,128)(2,1)S(1)} %bitcast.9) | data formatting | bytes 1769472 | tf_op jit(solution)/shard_map/reshape | solution.py:420
  11.6 0.8 %pad_maximum_fusion = bf16[3,3,4,8,4,512]{5,4,3,2,1,0:T(4,128)(2,1)S(1)} fusion(bf16[3,3,4,2,4,512]{5,4,3,2,1,0:T(4,128)(2,1)S(1)} %broadcast_select_fusion, bf16[3,3,4,6,4,512]{5,4,3,2,1,0:T(4,128)(2,1)S(1)} %bitcast.8), kind=kLoop, calls=%fused_computation | loop fusion | flops 589824 | bytes 2359296 | tf_op jit(solution)/shard_map/concatenate | solution.py:427
  12.4 1.2 %reshape.38.wemb_ref = bf16[1152,512]{1,0:T(8,128)(2,1)} reshape(bf16[3,3,4,8,4,512]{5,4,3,2,1,0:T(4,128)(2,1)S(1)} %pad_maximum_fusion) | data formatting | bytes 2359296 | tf_op jit(solution)/shard_map/reshape | solution.py:427
  13.6 2.3 %collective-permute-done.1.far_ref = bf16[9,96,128]{2,1,0:T(8,128)(2,1)S(1)} collective-permute-done((bf16[9,96,128]{2,1,0:T(8,128)(2,1)}, bf16[9,96,128]{2,1,0:T(8,128)(2,1)S(1)}, u32[]{:S(2)}, u32[]{:S(2)}) %collective-permute-start.1) | collective-permute-done | bytes 221216 | tf_op jit(solution)/shard_map/ppermute | solution.py:435
  15.9 0.0 copy-start.3
  15.9 0.7 copy-done.3
  16.5 2.4 %shard_map.119 = (bf16[2,18,64,128]{3,2,1,0:T(8,128)(2,1)}, bf16[2,18,16,128]{3,2,1,0:T(8,128)(2,1)}, bf16[2,18,16,128]{3,2,1,0:T(8,128)(2,1)}) custom-call(s32[3]{0:T(128)} %pad_add_fusion.par_ref, bf16[9,96,128]{2,1,0:T(8,128)(2,1)} %constant_dynamic-update-slice_fusion.band_ref, bf16[9,96,128]{2,1,0:T(8,128)(2,1)} %copy-done.3), custom_call_target="tpu_custom_call" | custom-call | flops 1000000000 | bytes 1000000 | tf_op jit(solution)/shard_map/pallas_call | solution.py:107
  18.9 1.6 %collective-permute-start.2 = (bf16[2,18,16,128]{3,2,1,0:T(8,128)(2,1)}, bf16[2,18,16,128]{3,2,1,0:T(8,128)(2,1)S(1)}, u32[]{:S(2)}, u32[]{:S(2)}) collective-permute-start(bf16[2,18,16,128]{3,2,1,0:T(8,128)(2,1)} %get-tuple-element.18), channel_id=1, source_target_pairs={{0,1},{1,2},{2,3},{3,4},{4,5},{5,6},{6,7},{7,8},{8,9},{9,10},{10,1... | collective-permute-start | bytes 442376 | tf_op jit(solution)/shard_map/ppermute | solution.py:440
  20.5 4.2 %collective-permute-start.3 = (bf16[2,18,16,128]{3,2,1,0:T(8,128)(2,1)}, bf16[2,18,16,128]{3,2,1,0:T(8,128)(2,1)S(1)}, u32[]{:S(2)}, u32[]{:S(2)}) collective-permute-start(bf16[2,18,16,128]{3,2,1,0:T(8,128)(2,1)} %get-tuple-element.19), channel_id=1, source_target_pairs={{0,15},{1,0},{2,1},{3,2},{4,3},{5,4},{6,5},{7,6},{8,7},{9,8},{10,9... | collective-permute-start | bytes 442376 | tf_op jit(solution)/shard_map/ppermute | solution.py:440
  24.7 2.7 %collective-permute-done.2.low_ref = bf16[2,18,16,128]{3,2,1,0:T(8,128)(2,1)S(1)} collective-permute-done((bf16[2,18,16,128]{3,2,1,0:T(8,128)(2,1)}, bf16[2,18,16,128]{3,2,1,0:T(8,128)(2,1)S(1)}, u32[]{:S(2)}, u32[]{:S(2)}) %collective-permute-start.2) | collective-permute-done | bytes 147488 | tf_op jit(solution)/shard_map/ppermute | solution.py:440
  27.4 0.0 copy-start.4
  27.4 0.0 collective-permute-done.3.high_ref
  27.4 0.0 copy-start.5
  27.4 0.7 copy-done.4
  28.1 0.0 copy-done.5
  28.1 17.3 %shard_map.120 = (f32[2,12,80,512]{3,2,1,0:T(8,128)}, bf16[2,4,80,512]{3,2,1,0:T(8,128)(2,1)}) custom-call(s32[3]{0:T(128)} %pad_add_fusion.par_ref, bf16[2,18,64,128]{3,2,1,0:T(8,128)(2,1)} %get-tuple-element.17.full_ref, bf16[2,18,16,128]{3,2,1,0:T(8,128)(2,1)} %copy-done.4, bf16[2,18,16,128]{3,2,1,0:T(8,128)(2,1)} %copy-done.5, ...), custom_call_target="tpu_custom_call" | custom-call | flops 20000000000 | bytes 10000000 | tf_op jit(solution)/shard_map/pallas_call | solution.py:263
  45.4 3.9 %collective-permute-start.4 = (bf16[2,4,80,512]{3,2,1,0:T(8,128)(2,1)}, bf16[2,4,80,512]{3,2,1,0:T(8,128)(2,1)S(1)}, u32[]{:S(2)}, u32[]{:S(2)}) collective-permute-start(bf16[2,4,80,512]{3,2,1,0:T(8,128)(2,1)} %get-tuple-element.22), channel_id=1, source_target_pairs={{0,16},{16,0},{32,48},{48,32},{64,80},{80,64},{96,112},{112,96},{1... | collective-permute-start | bytes 1966088 | tf_op jit(solution)/shard_map/ppermute | solution.py:435
  49.3 1.9 %collective-permute-done.4.near_ref = bf16[2,4,80,512]{3,2,1,0:T(8,128)(2,1)S(1)} collective-permute-done((bf16[2,4,80,512]{3,2,1,0:T(8,128)(2,1)}, bf16[2,4,80,512]{3,2,1,0:T(8,128)(2,1)S(1)}, u32[]{:S(2)}, u32[]{:S(2)}) %collective-permute-start.4) | collective-permute-done | bytes 655392 | tf_op jit(solution)/shard_map/ppermute | solution.py:435
  51.3 0.0 copy-start.2
  51.3 0.8 %copy-done.2 = bf16[2,4,80,512]{3,2,1,0:T(8,128)(2,1)} copy-done((bf16[2,4,80,512]{3,2,1,0:T(8,128)(2,1)}, bf16[2,4,80,512]{3,2,1,0:T(8,128)(2,1)S(1)}, u32[]{:S(2)}) %copy-start.2) | copy-done | bytes 655384
  52.1 16.8 %shard_map.121 = bf16[2,4,32,1024]{3,2,1,0:T(8,128)(2,1)} custom-call(s32[3]{0:T(128)} %pad_add_fusion.par_ref, f32[2,12,80,512]{3,2,1,0:T(8,128)} %get-tuple-element.21.x1_any, bf16[2,4,80,512]{3,2,1,0:T(8,128)(2,1)} %copy-done.2, f32[2,512]{1,0:T(2,128)} %gain_ref.3, f32[1,2048]{1,0:T(1,128)} %bitcast.10, bf16[2,512,512]{2,1,0:T(8,128)(2,1)} %wq_any.3, ...), custom_call_target="tpu_custom_call" | custom-call | flops 10000000000 | bytes 10000000 | tf_op jit(solution)/shard_map/pallas_call | solution.py:396
  (5 shorter events, 0.0 us)
Async XLA Ops:
  0.6 3.6 %copy-start.1 = (f32[512]{0:T(512)S(1)}, f32[512]{0:T(512)}, u32[]{:S(2)}) copy-start(f32[512]{0:T(512)} %param.17) | copy-start | bytes 6148
  0.6 10.3 %copy-start = (bf16[12,12,6,512]{3,2,1,0:T(8,128)(2,1)S(1)}, bf16[12,12,6,512]{3,2,1,0:T(8,128)(2,1)}, u32[]{:S(2)}) copy-start(bf16[12,12,6,512]{3,2,1,0:T(8,128)(2,1)} %param.15) | copy-start | bytes 2654212
  3.5 1.7 %collective-permute-start = (bf16[1,96,128]{2,1,0:T(8,128)(2,1)}, bf16[1,96,128]{2,1,0:T(8,128)(2,1)S(1)}, u32[]{:S(2)}, u32[]{:S(2)}) collective-permute-start(bf16[1,96,128]{2,1,0:T(8,128)(2,1)} %get-tuple-element.15), channel_id=1, source_target_pairs={{0,16},{16,0},{32,48},{48,32},{64,80},{80,64},{96,112},{112,96},{1... | collective-permute-start | bytes 73736 | tf_op jit(solution)/shard_map/ppermute | solution.py:435
  5.9 10.0 %collective-permute-start.1 = (bf16[9,96,128]{2,1,0:T(8,128)(2,1)}, bf16[9,96,128]{2,1,0:T(8,128)(2,1)S(1)}, u32[]{:S(2)}, u32[]{:S(2)}) collective-permute-start(bf16[9,96,128]{2,1,0:T(8,128)(2,1)} %constant_dynamic-update-slice_fusion.band_ref), channel_id=1, source_target_pairs={{16,32},{32,16},{48,64},{64,48},{80,96},{96,80},{112,128},{128,112... | collective-permute-start | bytes 663560 | tf_op jit(solution)/shard_map/ppermute | solution.py:435
  15.9 0.7 copy-start.3
  18.9 8.5 %collective-permute-start.2 = (bf16[2,18,16,128]{3,2,1,0:T(8,128)(2,1)}, bf16[2,18,16,128]{3,2,1,0:T(8,128)(2,1)S(1)}, u32[]{:S(2)}, u32[]{:S(2)}) collective-permute-start(bf16[2,18,16,128]{3,2,1,0:T(8,128)(2,1)} %get-tuple-element.18), channel_id=1, source_target_pairs={{0,1},{1,2},{2,3},{3,4},{4,5},{5,6},{6,7},{7,8},{8,9},{9,10},{10,1... | collective-permute-start | bytes 442376 | tf_op jit(solution)/shard_map/ppermute | solution.py:440
  20.5 6.9 %collective-permute-start.3 = (bf16[2,18,16,128]{3,2,1,0:T(8,128)(2,1)}, bf16[2,18,16,128]{3,2,1,0:T(8,128)(2,1)S(1)}, u32[]{:S(2)}, u32[]{:S(2)}) collective-permute-start(bf16[2,18,16,128]{3,2,1,0:T(8,128)(2,1)} %get-tuple-element.19), channel_id=1, source_target_pairs={{0,15},{1,0},{2,1},{3,2},{4,3},{5,4},{6,5},{7,6},{8,7},{9,8},{10,9... | collective-permute-start | bytes 442376 | tf_op jit(solution)/shard_map/ppermute | solution.py:440
  27.4 0.7 copy-start.4
  27.4 0.7 %copy-start.5 = (bf16[2,18,16,128]{3,2,1,0:T(8,128)(2,1)}, bf16[2,18,16,128]{3,2,1,0:T(8,128)(2,1)S(1)}, u32[]{:S(2)}) copy-start(bf16[2,18,16,128]{3,2,1,0:T(8,128)(2,1)S(1)} %collective-permute-done.3.high_ref) | copy-start | bytes 442372
  45.4 5.8 %collective-permute-start.4 = (bf16[2,4,80,512]{3,2,1,0:T(8,128)(2,1)}, bf16[2,4,80,512]{3,2,1,0:T(8,128)(2,1)S(1)}, u32[]{:S(2)}, u32[]{:S(2)}) collective-permute-start(bf16[2,4,80,512]{3,2,1,0:T(8,128)(2,1)} %get-tuple-element.22), channel_id=1, source_target_pairs={{0,16},{16,0},{32,48},{48,32},{64,80},{80,64},{96,112},{112,96},{1... | collective-permute-start | bytes 1966088 | tf_op jit(solution)/shard_map/ppermute | solution.py:435
  51.3 0.8 %copy-start.2 = (bf16[2,4,80,512]{3,2,1,0:T(8,128)(2,1)}, bf16[2,4,80,512]{3,2,1,0:T(8,128)(2,1)S(1)}, u32[]{:S(2)}) copy-start(bf16[2,4,80,512]{3,2,1,0:T(8,128)(2,1)S(1)} %collective-permute-done.4.near_ref) | copy-start | bytes 1966084

commit v2 on v1

v2 whole, which is shorter than its diff:
```python
import math

import jax
import jax.numpy as jnp
from jax import lax
from jax.experimental import pallas as pl
from jax.experimental.pallas import tpu as pltpu
from jax.sharding import PartitionSpec as P

BF = jnp.bfloat16
F32 = jnp.float32
D = 512
HEAD_DIM = 64
WINS = 10
SCALE = HEAD_DIM ** (-0.5) * math.log2(math.e)
VMEM_LIMIT = 32 * 1024 * 1024


def iota(shape, dim):
    return lax.broadcasted_iota(jnp.int32, shape, dim)


def one_hot(cond):
    return jnp.where(cond, 1.0, 0.0).astype(BF)


def mm(a, b):
    return jnp.dot(a, b, preferred_element_type=F32)


def mm_t(a, b):
    return lax.dot_general(a, b, (((1,), (1,)), ((), ())), preferred_element_type=F32)


def params():
    return pltpu.CompilerParams(vmem_limit_bytes=VMEM_LIMIT)


def patch_kernel(par_ref, atmos_ref, oro_ref, land_ref, band_ref, edge_ref):
    par = par_ref[0]
    cells = jnp.concatenate(
        [
            atmos_ref[...].reshape(320, 256),
            oro_ref[...],
            land_ref[...].astype(F32).astype(BF),
        ],
        axis=0,
    )
    row, src = iota((1024, 384), 0), iota((1024, 384), 1)
    i, ch, r = row // 128, (row % 32) // 4, row % 4
    channel = jnp.where(ch < 5, ch, jnp.where(ch == 5, 10, jnp.where(ch == 6, 11, 9)))
    main = mm(one_hot(src == channel * 32 + i * 4 + r), cells)
    channel = 5 + (row % 16) // 4
    aux = mm(one_hot(src == channel * 32 + i * 4 + r), cells)
    row, col = iota((1024, 256), 0), iota((1024, 256), 1)
    c, half = (row % 128) // 32, (row % 32) // 16
    main = jnp.where(col % 4 == c, main, 0.0).astype(BF)
    aux = jnp.where((col % 4 == c) & (col // 128 == half), aux, 0.0).astype(BF)
    j, col = iota((64, 256), 0), iota((64, 256), 1)
    main = mm_t(one_hot(col // 4 == j), main).astype(BF)
    j, col = iota((32, 256), 0), iota((32, 256), 1)
    aux = mm_t(one_hot((col % 128) // 4 == j), aux).astype(BF)
    for i in range(8):
        band_ref[par + i, 0:64, :] = main[:, i * 128 : i * 128 + 128]
        band_ref[par + i, 64:96, :] = aux[:, i * 128 : i * 128 + 128]
    edge_ref[...] = band_ref[pl.ds(par + 7 * (1 - par), 1)]


def patches(par, atmos, orography, land_sea):
    return pl.pallas_call(
        patch_kernel,
        out_shape=(
            jax.ShapeDtypeStruct((9, 96, 128), BF),
            jax.ShapeDtypeStruct((1, 96, 128), BF),
        ),
        in_specs=[pl.BlockSpec(memory_space=pltpu.SMEM)] + [pl.BlockSpec(memory_space=pltpu.VMEM)] * 3,
        out_specs=(pl.BlockSpec(memory_space=pltpu.VMEM),) * 2,
        compiler_params=params(),
        cost_estimate=pl.CostEstimate(flops=10**9, bytes_accessed=10**6, transcendentals=0),
    )(par, atmos, orography, land_sea)


def unpack_kernel(par_ref, band_ref, far_ref, full_ref, low_ref, high_ref, packed):
    par = par_ref[0]
    packed[pl.ds(9 * (1 - par), 9)] = band_ref[...]
    packed[pl.ds(9 * par, 9)] = far_ref[...]
    k, n = iota((256, 256), 0), iota((256, 256), 1)
    ch, lane = (n % 32) // 4, n % 128
    from_main0 = jnp.where(ch == 7, lane - 4, lane)
    from_main1 = jnp.where(ch == 7, lane - 4, jnp.where(ch == 4, lane + 12, lane))
    aux = packed[:, 64:96, :]
    for half in range(2):
        from_one = jnp.where(ch < 4, 128 + lane + 16 * half, from_main1)
        pick = one_hot(k == jnp.where(n < 128, from_main0, from_one))
        both = jnp.concatenate([packed[:, half * 32 : half * 32 + 32, :], aux], axis=2)
        got = mm(both.reshape(18 * 32, 256), pick).astype(BF).reshape(18, 32, 256)
        for level in range(2):
            tile = got[:, :, level * 128 : level * 128 + 128]
            full_ref[level, :, half * 32 : half * 32 + 32, :] = tile
            if half == 0:
                low_ref[level] = tile[:, :16, :]
            else:
                high_ref[level] = tile[:, 16:, :]


def unpack(par, band, far):
    return pl.pallas_call(
        unpack_kernel,
        out_shape=(
            jax.ShapeDtypeStruct((2, 18, 64, 128), BF),
            jax.ShapeDtypeStruct((2, 18, 16, 128), BF),
            jax.ShapeDtypeStruct((2, 18, 16, 128), BF),
        ),
        in_specs=[pl.BlockSpec(memory_space=pltpu.SMEM)] + [pl.BlockSpec(memory_space=pltpu.VMEM)] * 2,
        out_specs=(pl.BlockSpec(memory_space=pltpu.VMEM),) * 3,
        scratch_shapes=[pltpu.VMEM((18, 96, 128), BF)],
        compiler_params=params(),
        cost_estimate=pl.CostEstimate(flops=10**9, bytes_accessed=10**6, transcendentals=0),
    )(par, band, far)


def pipelined(stages, groups):
    for step in range(len(groups) + len(stages) - 1):
        for k in reversed(range(len(stages))):
            if 0 <= step - k < len(groups):
                stages[k](groups[step - k])


def normalize(x, gain):
    mean = jnp.mean(x, axis=-1, keepdims=True)
    x = x - mean
    var = jnp.mean(x * x, axis=-1, keepdims=True)
    return x * lax.rsqrt(var + 1e-05) * gain


def attend(q, k, v, bias):
    left = iota((128, 128), 1) < HEAD_DIM
    ones_left, ones_right = one_hot(left), one_hot(~left)
    zero = jnp.zeros((128, 128), BF)
    out = []
    for pair in range(4):
        at = slice(pair * 128, pair * 128 + 128)
        kp, vp = k[:, at], v[:, at]
        keys = jnp.concatenate([jnp.where(left, kp, zero), jnp.where(left, zero, kp)], axis=0)
        s = mm_t(q[:, at], keys)
        if bias is not None:
            s = s + bias
        s0, s1 = s[:, :128], s[:, 128:]
        p0 = jnp.exp2(s0 - jnp.max(s0, axis=-1, keepdims=True))
        p1 = jnp.exp2(s1 - jnp.max(s1, axis=-1, keepdims=True))
        p = jnp.concatenate([p0, p1], axis=1).astype(BF)
        vals = jnp.concatenate(
            [
                jnp.concatenate([jnp.where(left, vp, zero), ones_left], axis=1),
                jnp.concatenate([jnp.where(left, zero, vp), ones_right], axis=1),
            ],
            axis=0,
        )
        o = mm(p, vals)
        out.append((o[:, :128] / o[:, 128:]).astype(BF))
    return jnp.concatenate(out, axis=1)


def first_kernel(
    par_ref, full_ref, low_ref, high_ref, wemb_ref, lev_ref, gain_ref, wq_ref, wkv_ref, wo_ref,
    x1_ref, send_ref,
    wide, gathered, x0, normed, query, keyval, heads,
):
    par = par_ref[0]
    wide[:, :, 0:16, :] = low_ref[...].astype(F32)
    wide[:, :, 16:80, :] = full_ref[...].astype(F32)
    wide[:, :, 80:96, :] = high_ref[...].astype(F32)
    gain = gain_ref[0:1, :]
    half = 1 - par

    def embed(group):
        part, g = group
        slot = part * 5 + g
        base = 8 * (par if part else half)
        for dj in range(3):
            cols = slice(g * 16 + 7 + dj, g * 16 + 23 + dj)
            got = wide[:, pl.ds(base, 10), cols, :].astype(BF)
            gathered[slot, :, :, :, dj * 128 : dj * 128 + 128] = got
        for level in range(2):
            lhs = jnp.concatenate(
                [gathered[slot, level, di : di + 8].reshape(128, 384) for di in range(3)], axis=1
            )
            x = mm(lhs, wemb_ref[...]) + lev_ref[level : level + 1, :]
            x0[slot, level] = x.reshape(8, 16, D)

    def norm(group):
        slot = group[0] * 5 + group[1]
        for u in range(2):
            x = x0[slot, :, :, u * 8 : u * 8 + 8, :].reshape(128, D)
            normed[slot, u] = normalize(x, gain).astype(BF).reshape(2, 4, 16, D)

    def project(group):
        slot = group[0] * 5 + group[1]
        n = normed[slot].reshape(256, D)
        keyval[slot] = mm(n, wkv_ref[0]).astype(BF).reshape(2, 128, 1024)
        if group[0]:
            n = normed[slot, :, :, pl.ds(half * 2, 2)].reshape(128, D)
        q = (mm(n, wq_ref[0]) * SCALE).astype(BF)
        query[slot, :, : q.shape[0] // 2] = q.reshape(2, -1, D)

    def attention(group):
        slot = group[0] * 5 + group[1]
        count = 64 if group[0] else 128
        for u in range(2):
            kv = keyval[slot, u]
            heads[slot, u, :count] = attend(query[slot, u, :count], kv[:, :D], kv[:, D:], None)

    def project_out(group):
        part, g = group
        slot = part * 5 + g
        count = 64 if part else 128
        out = mm(heads[slot, :, :count].reshape(2 * count, D), wo_ref[0])
        for u in range(2):
            cols = slice(g * 16 + u * 8, g * 16 + u * 8 + 8)
            mine = slice(u * 8, u * 8 + 8)
            add = out[u * count : u * count + count].reshape(2, count // 16, 8, D)
            if part:
                x1_ref[:, 0:4, cols, :] = x0[slot, :, pl.ds(4 * half, 4), mine, :] + add
            else:
                for h in range(2):
                    to = pl.ds(4 + 4 * (par if h == 0 else half), 4)
                    rows = slice(4 * h, 4 * h + 4)
                    x1_ref[:, to, cols, :] = x0[slot, :, rows, mine, :] + add[:, rows]

    groups = [(part, g) for part in range(2) for g in range(5)]
    pipelined([embed, norm, project, attention, project_out], groups)
    send_ref[...] = x1_ref[:, 8:12].astype(BF)


def first_block(par, full, low, high, wemb, level_embed, norm_gain, w_query, w_keyval, w_out):
    vmem = pl.BlockSpec(memory_space=pltpu.VMEM)
    return pl.pallas_call(
        first_kernel,
        out_shape=(
            jax.ShapeDtypeStruct((2, 12, 80, D), F32),
            jax.ShapeDtypeStruct((2, 4, 80, D), BF),
        ),
        in_specs=[pl.BlockSpec(memory_space=pltpu.SMEM)] + [vmem] * 9,
        out_specs=(vmem, vmem),
        scratch_shapes=[
            pltpu.VMEM((2, 18, 96, 128), F32),
            pltpu.VMEM((10, 2, 10, 16, 384), BF),
            pltpu.VMEM((10, 2, 8, 16, D), F32),
            pltpu.VMEM((10, 2, 2, 4, 16, D), BF),
            pltpu.VMEM((10, 2, 128, D), BF),
            pltpu.VMEM((10, 2, 128, 1024), BF),
            pltpu.VMEM((10, 2, 128, D), BF),
        ],
        compiler_params=params(),
        cost_estimate=pl.CostEstimate(flops=2 * 10**10, bytes_accessed=10**7, transcendentals=0),
    )(par, full, low, high, wemb, level_embed, norm_gain, w_query, w_keyval, w_out)


SHIFTED = WINS - 1


def second_kernel(
    par_ref, x1_ref, near_ref, gain_ref, mgain_ref, wq_ref, wkv_ref, wo_ref, wm_ref,
    out_ref,
    near, x2, normed, query, keyval, heads,
):
    par, pole = par_ref[0], par_ref[1]
    near[...] = near_ref[...].astype(F32)
    gain = gain_ref[1:2, :]
    upper = iota((8, D), 0) >= 4
    key_row = (iota((1, 256), 1) // 8) % 8
    bias = jnp.where(key_row < 4, F32(-1e30), F32(0)) * pole.astype(F32)

    def window(ref, w, rows):
        a = ref[:, rows, w * 8 : w * 8 + 8, :]
        b = ref[:, rows, w * 8 + 8 : w * 8 + 16, :]
        return jnp.where(upper, a, b)

    def norm(group):
        s, g = group
        for w in range(g * 3, g * 3 + 3):
            if s == 0:
                x = window(x1_ref, w, slice(0, 8))
            else:
                x = jnp.concatenate(
                    [window(x1_ref, w, slice(8, 12)), window(near, w, slice(0, 4))], axis=1
                )
            n = normalize(x.reshape(128, D), gain).astype(BF)
            normed[s * SHIFTED + w] = n.reshape(2, 4, 16, D)

    def project(group):
        s, g = group
        at = slice(s * SHIFTED + g * 3, s * SHIFTED + g * 3 + 3)
        n = normed[at].reshape(384, D)
        keyval[at] = mm(n, wkv_ref[1]).astype(BF).reshape(3, 128, 1024)
        n = normed[at, :, 2 - 2 * s : 4 - 2 * s].reshape(192, D)
        query[at] = (mm(n, wq_ref[1]) * SCALE).astype(BF).reshape(3, 64, D)

    def attention(group):
        s, g = group
        for t in range(s * SHIFTED + g * 3, s * SHIFTED + g * 3 + 3):
            kv = keyval[t]
            heads[t] = attend(query[t], kv[:, :D], kv[:, D:], None if s else bias)

    def project_out(group):
        s, g = group
        at = slice(s * SHIFTED + g * 3, s * SHIFTED + g * 3 + 3)
        out = mm(heads[at].reshape(192, D), wo_ref[1])
        rows = slice(s * 4, s * 4 + 4)
        for u in range(3):
            w = g * 3 + u
            new = window(x1_ref, w, slice(4 + s * 4, 8 + s * 4))
            new = new + out[u * 64 : u * 64 + 64].reshape(2, 4, 8, D)
            for c in range(4):
                piece = new[..., c * 128 : c * 128 + 128]
                x2[c, :, rows, w * 8 + 4 : w * 8 + 8, :] = piece[:, :, 4:8, :]
                x2[c, :, rows, w * 8 + 8 : w * 8 + 12, :] = piece[:, :, 0:4, :]

    def merge(group):
        s, g = group
        if g < 2:
            return
        parts = []
        for p in range(4):
            got = [
                jnp.concatenate(
                    [
                        x2[c, level, s * 4 + 2 * a + p % 2, pl.ds(8 + p // 2, 32, stride=2), :]
                        for c in range(4)
                    ],
                    axis=1,
                )
                for level in range(2)
                for a in range(2)
            ]
            parts.append(jnp.concatenate(got, axis=0))
        n = normalize(jnp.concatenate(parts, axis=1), mgain_ref[...]).astype(BF)
        out = mm(n, wm_ref[...]).astype(BF)
        out_ref[:, pl.ds(2 * ((par + s) % 2), 2)] = out.reshape(2, 2, 32, 1024)

    groups = [(s, g) for s in range(2) for g in range(3)]
    pipelined([norm, project, attention, project_out, merge], groups)


def second_block(par, x1, near, norm_gain, merge_gain, w_query, w_keyval, w_out, merge_weight):
    vmem = pl.BlockSpec(memory_space=pltpu.VMEM)
    return pl.pallas_call(
        second_kernel,
        out_shape=jax.ShapeDtypeStruct((2, 4, 32, 1024), BF),
        in_specs=[pl.BlockSpec(memory_space=pltpu.SMEM)] + [vmem] * 8,
        out_specs=vmem,
        scratch_shapes=[
            pltpu.VMEM((2, 4, 80, D), F32),
            pltpu.VMEM((4, 2, 8, 80, 128), F32),
            pltpu.VMEM((2 * SHIFTED, 2, 4, 16, D), BF),
            pltpu.VMEM((2 * SHIFTED, 64, D), BF),
            pltpu.VMEM((2 * SHIFTED, 128, 1024), BF),
            pltpu.VMEM((2 * SHIFTED, 64, D), BF),
        ],
        compiler_params=params(),
        cost_estimate=pl.CostEstimate(flops=10**10, bytes_accessed=10**7, transcendentals=0),
    )(par, x1, near, norm_gain, merge_gain, w_query, w_keyval, w_out, merge_weight)


def embedding_matrix(embed_weight, land_embed):
    w = embed_weight.reshape(3, 4, 3, 4, 6, D).transpose(0, 2, 3, 4, 1, 5)
    share = land_embed / 16
    high = lax.reduce_precision(share, 8, 7)
    terms = jnp.stack([high, share - high]).astype(BF)
    terms = jnp.broadcast_to(terms[None, :, None, :], (4, 2, 4, D))
    middle = (jnp.arange(9) == 4).reshape(3, 3, 1, 1, 1, 1)
    land = jnp.where(middle, terms, jnp.zeros((), BF))
    return jnp.concatenate([w, land], axis=3).reshape(9 * 128, D)


def swap(block, first):
    count = lax.axis_size("lat")
    pairs = []
    for i in range(first, count - 1, 2):
        pairs += [(i, i + 1), (i + 1, i)]
    return lax.ppermute(block, "lat", pairs)


def around(block, distance):
    count = lax.axis_size("lon")
    return lax.ppermute(block, "lon", [(i, (i + distance) % count) for i in range(count)])


def shards(
    atmos, orography, land_sea, embed_weight, level_embed, land_embed, norm_gain,
    w_query, w_keyval, w_out, merge_gain, merge_weight,
):
    w_query, w_keyval, w_out, merge_weight = [
        pltpu.with_memory_space_constraint(w, pltpu.VMEM) for w in (w_query, w_keyval, w_out, merge_weight)
    ]
    lat = lax.axis_index("lat")
    par = lat % 2
    pole = (lat == 0) | (lat == lax.axis_size("lat") - 1)
    place = jnp.stack([par, pole]).astype(jnp.int32)
    band, edge = patches(place, atmos, orography, land_sea)
    edge = swap(edge, 0)
    band = lax.dynamic_update_slice(band, edge, (8 * (1 - par), 0, 0))
    far = swap(band, 1)
    wemb = embedding_matrix(embed_weight, land_embed)
    far, wemb = lax.optimization_barrier((far, wemb))
    full, low, high = unpack(place, band, far)
    from_low, from_high = around(high, 1), around(low, -1)
    x1, send = first_block(
        place, full, from_low, from_high, wemb, level_embed, norm_gain, w_query, w_keyval, w_out
    )
    near = swap(send, 0)
    return second_block(
        place, x1, near, norm_gain, merge_gain.reshape(1, -1), w_query, w_keyval, w_out, merge_weight
    )


def solution(mesh):
    in_specs = (P(None, None, "lat", "lon"), P("lat", "lon"), P("lat", "lon")) + (P(),) * 9
    out_specs = P(None, "lat", "lon", None)
    return jax.shard_map(shards, mesh=mesh, in_specs=in_specs, out_specs=out_specs, check_vma=False)
```

time: 69.9 us -> 57.9 us (0.83)
  Pallas kernels: 39.4 us -> 29.1 us
  waiting for transfers between devices: 7.95 us -> 4.78 us
  local copies, waits for them, and re-layouts: 4.72 us -> 6.88 us
  starting transfers between devices: 15.2 us -> 14.1 us
    pallas_call x1, Pallas kernels: 16.8 us -> 11.7 us  [second_block(): pl.pallas_call(second_kernel, out_shape=jax.ShapeDtypeStruct((2, 4, 32, 1...]
    ppermute x3, waiting for transfers between devices: 5.21 us -> 2.51 us  [swap(): return lax.ppermute(block, 'lat', pairs)]
    pallas_call x1, Pallas kernels: 17.3 us -> 14.8 us  [first_block(): pl.pallas_call(first_kernel, out_shape=(jax.ShapeDtypeStruct((2, 12, 80,...]
    pallas_call x1, Pallas kernels: 2.35 us -> 0.87 us  [unpack(): pl.pallas_call(unpack_kernel, out_shape=(jax.ShapeDtypeStruct((2, 18, 64,...]
    ppermute x3, starting transfers between devices: 9.45 us -> 8.12 us  [swap(): return lax.ppermute(block, 'lat', pairs)]
    reshape x1, local copies, waits for them, and re-layouts: 1.17 us -> 2.46 us  [embedding_matrix(): return jnp.concatenate([w, land], axis=3).reshape(9 * 128, D)]
    reshape x1, local copies, waits for them, and re-layouts: 0.69 us -> 1.96 us  [embedding_matrix(): w = embed_weight.reshape(3, 4, 3, 4, 6, D).transpose(0, 2, 3, 4, 1, 5)]
    pallas_call x1, Pallas kernels: 2.94 us -> 1.75 us  [patches(): pl.pallas_call(patch_kernel, out_shape=(jax.ShapeDtypeStruct((9, 96, 128)...]
  transfers between devices with their start and end apart: 5 -> 5, of which waited for: 4 -> 3; matrix products, arithmetic and copies ran while one was open for 4% -> 11% of each run, Pallas kernels for 0% -> 0%
where the time goes in v2:
time: 57.9 us; the launch traced here: 57.1 us
  Pallas kernels  29.1 us (50%)
  starting transfers between devices  14.1 us (24%)
  local copies, waits for them, and re-layouts  6.88 us (12%)
  waiting for transfers between devices  4.78 us (8%)
  other arithmetic  2.06 us (4%)
    pallas_call x1, Pallas kernels, first_block(): pl.pallas_call(first_kernel, out_shape=(jax.ShapeDtypeStruct((2, 12, 80,...  14.8 us
    pallas_call x1, Pallas kernels, second_block(): pl.pallas_call(second_kernel, out_shape=jax.ShapeDtypeStruct((2, 4, 32, 1...  11.7 us
    ppermute x3, starting transfers between devices, swap(): return lax.ppermute(block, 'lat', pairs)  8.12 us
    ppermute x2, starting transfers between devices, around(): lax.ppermute(block, 'lon', [(i, (i + distance) % count) for i in range(co...  5.95 us
    ppermute x3, waiting for transfers between devices, swap(): return lax.ppermute(block, 'lat', pairs)  2.51 us
    reshape x1, local copies, waits for them, and re-layouts, embedding_matrix(): return jnp.concatenate([w, land], axis=3).reshape(9 * 128, D)  2.46 us
    unnamed x22, local copies, waits for them, and re-layouts  2.43 us
    ppermute x2, waiting for transfers between devices, around(): lax.ppermute(block, 'lon', [(i, (i + distance) % count) for i in range(co...  2.27 us
  transfers between devices with their start and end apart: 5, of which 3 were waited for; matrix products, arithmetic and copies ran while one was open for 11% of the time, Pallas kernels for 0%

profile of v2, /device:TPU:25, one launch (start us, length us, event | category | flops | bytes accessed | tf_op | source)
XLA Modules:
  0.0 57.1 jit_solution(9613602654871258629)
XLA Ops:
  0.0 0.1 pad_add_fusion.par_ref
  0.1 0.0 copy-start.4
  0.1 0.9 %copy-done.4 = bf16[2,5,32,256]{3,2,1,0:T(8,128)(2,1)S(1)} copy-done((bf16[2,5,32,256]{3,2,1,0:T(8,128)(2,1)S(1)}, bf16[2,5,32,256]{3,2,1,0:T(8,128)(2,1)}, u32[]{:S(2)}) %copy-start.4) | copy-done | bytes 163864
  1.0 0.0 copy-start.5
  1.0 0.8 %copy-done.5 = s32[32,256]{1,0:T(8,128)S(1)} copy-done((s32[32,256]{1,0:T(8,128)S(1)}, s32[32,256]{1,0:T(8,128)}, u32[]{:S(2)}) %copy-start.5) | copy-done | bytes 32792
  1.8 0.0 copy-start.6
  1.8 0.7 %copy-done.6 = bf16[32,256]{1,0:T(8,128)(2,1)S(1)} copy-done((bf16[32,256]{1,0:T(8,128)(2,1)S(1)}, bf16[32,256]{1,0:T(8,128)(2,1)}, u32[]{:S(2)}) %copy-start.6) | copy-done | bytes 16408
  2.5 0.0 copy-start.10
  2.5 1.8 %shard_map.118 = (bf16[9,96,128]{2,1,0:T(8,128)(2,1)S(1)}, bf16[1,96,128]{2,1,0:T(8,128)(2,1)S(1)}) custom-call(s32[2]{0:T(128)S(1)} %pad_add_fusion.par_ref, bf16[2,5,32,256]{3,2,1,0:T(8,128)(2,1)S(1)} %copy-done.4, bf16[32,256]{1,0:T(8,128)(2,1)S(1)} %copy-done.6, s32[32,256]{1,0:T(8,128)S(1)} %copy-done.5), custom_call_target="tpu_custom_call" | custom-call | flops 1000000000 | bytes 1000000 | tf_op jit(solution)/shard_map/pallas_call | solution.py:70
  4.2 0.8 %collective-permute-start = (bf16[1,96,128]{2,1,0:T(8,128)(2,1)S(1)}, bf16[1,96,128]{2,1,0:T(8,128)(2,1)S(1)}, u32[]{:S(2)}, u32[]{:S(2)}) collective-permute-start(bf16[1,96,128]{2,1,0:T(8,128)(2,1)S(1)} %get-tuple-element.15), channel_id=1, source_target_pairs={{0,16},{16,0},{32,48},{48,32},{64,80},{80,64},{96,112},{112,96},{1... | collective-permute-start | bytes 73736 | tf_op jit(solution)/shard_map/ppermute | solution.py:381
  5.0 0.0 copy-done.10
  5.1 0.8 %collective-permute-done = bf16[1,96,128]{2,1,0:T(8,128)(2,1)S(1)} collective-permute-done((bf16[1,96,128]{2,1,0:T(8,128)(2,1)S(1)}, bf16[1,96,128]{2,1,0:T(8,128)(2,1)S(1)}, u32[]{:S(2)}, u32[]{:S(2)}) %collective-permute-start) | collective-permute-done | bytes 24608 | tf_op jit(solution)/shard_map/ppermute | solution.py:381
  5.9 4.9 %collective-permute-start.1 = (bf16[9,96,128]{2,1,0:T(8,128)(2,1)S(1)}, bf16[9,96,128]{2,1,0:T(8,128)(2,1)S(1)}, u32[]{:S(2)}, u32[]{:S(2)}) collective-permute-start(bf16[9,96,128]{2,1,0:T(8,128)(2,1)S(1)} %constant_dynamic-update-slice_fusion.band_ref), channel_id=1, source_target_pairs={{16,32},{32,16},{48,64},{64,48},{80,96},{96,80},{112,128},{128,112... | collective-permute-start | bytes 663560 | tf_op jit(solution)/shard_map/ppermute | solution.py:381
  10.7 0.1 broadcast_select_fusion
  10.9 2.0 %copy.15 = bf16[3,4,3,4,6,512]{5,1,4,3,2,0:T(4,128)(2,1)S(1)} copy(bf16[3,4,3,4,6,512]{5,4,3,2,1,0:T(8,128)(2,1)} %bitcast.9) | data formatting | bytes 1769472 | tf_op jit(solution)/shard_map/reshape | solution.py:366
  12.9 1.8 %pad_maximum_fusion = bf16[3,3,4,8,4,512]{5,4,3,2,1,0:T(4,128)(2,1)} fusion(bf16[3,3,4,2,4,512]{5,4,3,2,1,0:T(4,128)(2,1)S(1)} %broadcast_select_fusion, bf16[3,3,4,6,4,512]{5,4,3,2,1,0:T(4,128)(2,1)S(1)} %bitcast.8), kind=kLoop, calls=%fused_computation | loop fusion | flops 589824 | bytes 2359296 | tf_op jit(solution)/shard_map/concatenate | solution.py:373
  14.7 0.0 copy-start.3
  14.7 2.5 %reshape.38.wemb_ref = bf16[1152,512]{1,0:T(8,128)(2,1)S(1)} reshape(bf16[3,3,4,8,4,512]{5,4,3,2,1,0:T(4,128)(2,1)} %pad_maximum_fusion) | data formatting | bytes 2359296 | tf_op jit(solution)/shard_map/reshape | solution.py:373
  17.1 0.0 copy-start.1
  17.2 0.0 copy-start.2
  17.2 0.0 copy-start.8
  17.2 0.0 copy-start.9
  17.2 0.0 collective-permute-done.1.far_ref
  17.2 0.9 %shard_map.119 = (bf16[2,18,64,128]{3,2,1,0:T(8,128)(2,1)S(1)}, bf16[2,18,16,128]{3,2,1,0:T(8,128)(2,1)S(1)}, bf16[2,18,16,128]{3,2,1,0:T(8,128)(2,1)S(1)}) custom-call(s32[2]{0:T(128)S(1)} %pad_add_fusion.par_ref, bf16[9,96,128]{2,1,0:T(8,128)(2,1)S(1)} %constant_dynamic-update-slice_fusion.band_ref, bf16[9,96,128]{2,1,0:T(8,128)(2,1)S(1)} %collective-permute-done.1.far_ref), custom_call_target="tpu_custom_call" | custom-call | flops 1000000000 | bytes 1000000 | tf_op jit(solution)/shard_map/pallas_call | solution.py:107
  18.1 1.7 %collective-permute-start.2 = (bf16[2,18,16,128]{3,2,1,0:T(8,128)(2,1)S(1)}, bf16[2,18,16,128]{3,2,1,0:T(8,128)(2,1)S(1)}, u32[]{:S(2)}, u32[]{:S(2)}) collective-permute-start(bf16[2,18,16,128]{3,2,1,0:T(8,128)(2,1)S(1)} %get-tuple-element.18), channel_id=1, source_target_pairs={{0,1},{1,2},{2,3},{3,4},{4,5},{5,6},{6,7},{7,8},{8,9},{9,10},{10,1... | collective-permute-start | bytes 442376 | tf_op jit(solution)/shard_map/ppermute | solution.py:386
  19.8 4.2 %collective-permute-start.3 = (bf16[2,18,16,128]{3,2,1,0:T(8,128)(2,1)S(1)}, bf16[2,18,16,128]{3,2,1,0:T(8,128)(2,1)S(1)}, u32[]{:S(2)}, u32[]{:S(2)}) collective-permute-start(bf16[2,18,16,128]{3,2,1,0:T(8,128)(2,1)S(1)} %get-tuple-element.19), channel_id=1, source_target_pairs={{0,15},{1,0},{2,1},{3,2},{4,3},{5,4},{6,5},{7,6},{8,7},{9,8},{10,9... | collective-permute-start | bytes 442376 | tf_op jit(solution)/shard_map/ppermute | solution.py:386
  24.0 2.3 %collective-permute-done.2.low_ref = bf16[2,18,16,128]{3,2,1,0:T(8,128)(2,1)S(1)} collective-permute-done((bf16[2,18,16,128]{3,2,1,0:T(8,128)(2,1)S(1)}, bf16[2,18,16,128]{3,2,1,0:T(8,128)(2,1)S(1)}, u32[]{:S(2)}, u32[]{:S(2)}) %collective-permute-start.2) | collective-permute-done | bytes 147488 | tf_op jit(solution)/shard_map/ppermute | solution.py:386
  26.3 0.0 collective-permute-done.3.high_ref
  26.3 0.0 copy-done.3
  26.3 0.0 copy-done.1
  26.3 0.0 copy-done.2
  26.3 0.0 copy-done.8
  26.3 0.0 copy-done.9
  26.3 0.0 copy-start
  26.4 0.0 copy-start.7
  26.4 14.8 %shard_map.120 = (f32[2,12,80,512]{3,2,1,0:T(8,128)S(1)}, bf16[2,4,80,512]{3,2,1,0:T(8,128)(2,1)S(1)}) custom-call(s32[2]{0:T(128)S(1)} %pad_add_fusion.par_ref, bf16[2,18,64,128]{3,2,1,0:T(8,128)(2,1)S(1)} %get-tuple-element.17.full_ref, bf16[2,18,16,128]{3,2,1,0:T(8,128)(2,1)S(1)} %collective-permute-done.2.low_ref, ...), custom_call_target="tpu_custom_call" | custom-call | flops 20000000000 | bytes 10000000 | tf_op jit(solution)/shard_map/pallas_call | solution.py:237
  41.1 2.5 %collective-permute-start.4 = (bf16[2,4,80,512]{3,2,1,0:T(8,128)(2,1)S(1)}, bf16[2,4,80,512]{3,2,1,0:T(8,128)(2,1)S(1)}, u32[]{:S(2)}, u32[]{:S(2)}) collective-permute-start(bf16[2,4,80,512]{3,2,1,0:T(8,128)(2,1)S(1)} %get-tuple-element.22), channel_id=1, source_target_pairs={{0,16},{16,0},{32,48},{48,32},{64,80},{80,64},{96,112},{112,96},{1... | collective-permute-start | bytes 1966088 | tf_op jit(solution)/shard_map/ppermute | solution.py:381
  43.6 1.7 %collective-permute-done.4.near_ref = bf16[2,4,80,512]{3,2,1,0:T(8,128)(2,1)S(1)} collective-permute-done((bf16[2,4,80,512]{3,2,1,0:T(8,128)(2,1)S(1)}, bf16[2,4,80,512]{3,2,1,0:T(8,128)(2,1)S(1)}, u32[]{:S(2)}, u32[]{:S(2)}) %collective-permute-start.4) | collective-permute-done | bytes 655392 | tf_op jit(solution)/shard_map/ppermute | solution.py:381
  45.4 0.0 copy-done
  45.4 0.0 copy-done.7
  45.4 11.7 %shard_map.121 = bf16[2,4,32,1024]{3,2,1,0:T(8,128)(2,1)} custom-call(s32[2]{0:T(128)S(1)} %pad_add_fusion.par_ref, f32[2,12,80,512]{3,2,1,0:T(8,128)S(1)} %get-tuple-element.21.x1_ref, bf16[2,4,80,512]{3,2,1,0:T(8,128)(2,1)S(1)} %collective-permute-done.4.near_ref, f32[2,512]{1,0:T(2,128)S(1)} %copy-done.9, f32[1,2048]{1,0:T(1,128)S(1)} %bitcast.7, ...), custom_call_target="tpu_custom_call" | custom-call | flops 10000000000 | bytes 10000000 | tf_op jit(solution)/shard_map/pallas_call | solution.py:347
  (6 shorter events, 0.0 us)
Async XLA Ops:
  0.1 0.9 %copy-start.4 = (bf16[2,5,32,256]{3,2,1,0:T(8,128)(2,1)S(1)}, bf16[2,5,32,256]{3,2,1,0:T(8,128)(2,1)}, u32[]{:S(2)}) copy-start(bf16[2,5,32,256]{3,2,1,0:T(8,128)(2,1)} %atmos_ref.1) | copy-start | bytes 491524
  1.0 0.8 %copy-start.5 = (s32[32,256]{1,0:T(8,128)S(1)}, s32[32,256]{1,0:T(8,128)}, u32[]{:S(2)}) copy-start(s32[32,256]{1,0:T(8,128)} %land_ref.1) | copy-start | bytes 98308
  1.8 0.7 %copy-start.6 = (bf16[32,256]{1,0:T(8,128)(2,1)S(1)}, bf16[32,256]{1,0:T(8,128)(2,1)}, u32[]{:S(2)}) copy-start(bf16[32,256]{1,0:T(8,128)(2,1)} %oro_ref.1) | copy-start | bytes 49156
  2.5 2.5 %copy-start.10 = (f32[512]{0:T(512)S(1)}, f32[512]{0:T(512)}, u32[]{:S(2)}) copy-start(f32[512]{0:T(512)} %param.17) | copy-start | bytes 6148
  4.2 1.6 %collective-permute-start = (bf16[1,96,128]{2,1,0:T(8,128)(2,1)S(1)}, bf16[1,96,128]{2,1,0:T(8,128)(2,1)S(1)}, u32[]{:S(2)}, u32[]{:S(2)}) collective-permute-start(bf16[1,96,128]{2,1,0:T(8,128)(2,1)S(1)} %get-tuple-element.15), channel_id=1, source_target_pairs={{0,16},{16,0},{32,48},{48,32},{64,80},{80,64},{96,112},{112,96},{1... | collective-permute-start | bytes 73736 | tf_op jit(solution)/shard_map/ppermute | solution.py:381
  5.9 11.3 %collective-permute-start.1 = (bf16[9,96,128]{2,1,0:T(8,128)(2,1)S(1)}, bf16[9,96,128]{2,1,0:T(8,128)(2,1)S(1)}, u32[]{:S(2)}, u32[]{:S(2)}) collective-permute-start(bf16[9,96,128]{2,1,0:T(8,128)(2,1)S(1)} %constant_dynamic-update-slice_fusion.band_ref), channel_id=1, source_target_pairs={{16,32},{32,16},{48,64},{64,48},{80,96},{96,80},{112,128},{128,112... | collective-permute-start | bytes 663560 | tf_op jit(solution)/shard_map/ppermute | solution.py:381
  14.7 11.6 %copy-start.3 = (bf16[2,512,512]{2,1,0:T(8,128)(2,1)S(1)}, bf16[2,512,512]{2,1,0:T(8,128)(2,1)}, u32[]{:S(2)}) copy-start(bf16[2,512,512]{2,1,0:T(8,128)(2,1)} %wo_ref.3) | copy-start | bytes 3145732
  17.1 9.2 %copy-start.1 = (bf16[2,512,1024]{2,1,0:T(8,128)(2,1)S(1)}, bf16[2,512,1024]{2,1,0:T(8,128)(2,1)}, u32[]{:S(2)}) copy-start(bf16[2,512,1024]{2,1,0:T(8,128)(2,1)} %wkv_ref.3) | copy-start | bytes 6291460
  17.2 9.2 %copy-start.2 = (bf16[2,512,512]{2,1,0:T(8,128)(2,1)S(1)}, bf16[2,512,512]{2,1,0:T(8,128)(2,1)}, u32[]{:S(2)}) copy-start(bf16[2,512,512]{2,1,0:T(8,128)(2,1)} %wq_ref.3) | copy-start | bytes 3145732
  17.2 9.2 %copy-start.8 = (f32[2,512]{1,0:T(2,128)S(1)}, f32[2,512]{1,0:T(2,128)}, u32[]{:S(2)}) copy-start(f32[2,512]{1,0:T(2,128)} %lev_ref.1) | copy-start | bytes 12292
  17.2 9.2 %copy-start.9 = (f32[2,512]{1,0:T(2,128)S(1)}, f32[2,512]{1,0:T(2,128)}, u32[]{:S(2)}) copy-start(f32[2,512]{1,0:T(2,128)} %gain_ref.3) | copy-start | bytes 12292
  18.1 8.2 %collective-permute-start.2 = (bf16[2,18,16,128]{3,2,1,0:T(8,128)(2,1)S(1)}, bf16[2,18,16,128]{3,2,1,0:T(8,128)(2,1)S(1)}, u32[]{:S(2)}, u32[]{:S(2)}) collective-permute-start(bf16[2,18,16,128]{3,2,1,0:T(8,128)(2,1)S(1)} %get-tuple-element.18), channel_id=1, source_target_pairs={{0,1},{1,2},{2,3},{3,4},{4,5},{5,6},{6,7},{7,8},{8,9},{9,10},{10,1... | collective-permute-start | bytes 442376 | tf_op jit(solution)/shard_map/ppermute | solution.py:386
  19.8 6.5 %collective-permute-start.3 = (bf16[2,18,16,128]{3,2,1,0:T(8,128)(2,1)S(1)}, bf16[2,18,16,128]{3,2,1,0:T(8,128)(2,1)S(1)}, u32[]{:S(2)}, u32[]{:S(2)}) collective-permute-start(bf16[2,18,16,128]{3,2,1,0:T(8,128)(2,1)S(1)} %get-tuple-element.19), channel_id=1, source_target_pairs={{0,15},{1,0},{2,1},{3,2},{4,3},{5,4},{6,5},{7,6},{8,7},{9,8},{10,9... | collective-permute-start | bytes 442376 | tf_op jit(solution)/shard_map/ppermute | solution.py:386
  26.3 19.0 %copy-start = (bf16[2048,1024]{1,0:T(8,128)(2,1)S(1)}, bf16[2048,1024]{1,0:T(8,128)(2,1)}, u32[]{:S(2)}) copy-start(bf16[2048,1024]{1,0:T(8,128)(2,1)} %wm_ref.1) | copy-start | bytes 12582916
  26.4 19.0 %copy-start.7 = (f32[2048]{0:T(1024)S(1)}, f32[2048]{0:T(1024)}, u32[]{:S(2)}) copy-start(f32[2048]{0:T(1024)} %param.22) | copy-start | bytes 24580
  41.1 4.2 %collective-permute-start.4 = (bf16[2,4,80,512]{3,2,1,0:T(8,128)(2,1)S(1)}, bf16[2,4,80,512]{3,2,1,0:T(8,128)(2,1)S(1)}, u32[]{:S(2)}, u32[]{:S(2)}) collective-permute-start(bf16[2,4,80,512]{3,2,1,0:T(8,128)(2,1)S(1)} %get-tuple-element.22), channel_id=1, source_target_pairs={{0,16},{16,0},{32,48},{48,32},{64,80},{80,64},{96,112},{112,96},{1... | collective-permute-start | bytes 1966088 | tf_op jit(solution)/shard_map/ppermute | solution.py:381

commit v3 on v2

--- a/solution.py
+++ b/solution.py
@@ -1,3 +1,4 @@
+import functools
 import math
 
 import jax
@@ -36,8 +37,20 @@
     return pltpu.CompilerParams(vmem_limit_bytes=VMEM_LIMIT)
 
 
-def patch_kernel(par_ref, atmos_ref, oro_ref, land_ref, band_ref, edge_ref):
+def patch_kernel(
+    par_ref, atmos_any, oro_any, land_any, band_ref, edge_ref, atmos_ref, oro_ref, land_ref, sems
+):
     par = par_ref[0]
+    loads = [
+        pltpu.make_async_copy(src, dst, sems.at[n])
+        for n, (src, dst) in enumerate(
+            [(atmos_any, atmos_ref), (oro_any, oro_ref), (land_any, land_ref)]
+        )
+    ]
+    for load in loads:
+        load.start()
+    for load in loads:
+        load.wait()
     cells = jnp.concatenate(
         [
             atmos_ref[...].reshape(320, 256),
@@ -73,8 +86,14 @@
             jax.ShapeDtypeStruct((9, 96, 128), BF),
             jax.ShapeDtypeStruct((1, 96, 128), BF),
         ),
-        in_specs=[pl.BlockSpec(memory_space=pltpu.SMEM)] + [pl.BlockSpec(memory_space=pltpu.VMEM)] * 3,
+        in_specs=[pl.BlockSpec(memory_space=pltpu.SMEM)] + [pl.BlockSpec(memory_space=pltpu.HBM)] * 3,
         out_specs=(pl.BlockSpec(memory_space=pltpu.VMEM),) * 2,
+        scratch_shapes=[
+            pltpu.VMEM(atmos.shape, BF),
+            pltpu.VMEM(orography.shape, BF),
+            pltpu.VMEM(land_sea.shape, jnp.int32),
+            pltpu.SemaphoreType.DMA((3,)),
+        ],
         compiler_params=params(),
         cost_estimate=pl.CostEstimate(flops=10**9, bytes_accessed=10**6, transcendentals=0),
     )(par, atmos, orography, land_sea)
@@ -121,7 +140,7 @@
 
 def pipelined(stages, groups):
     for step in range(len(groups) + len(stages) - 1):
-        for k in reversed(range(len(stages))):
+        for k in range(len(stages)):
             if 0 <= step - k < len(groups):
                 stages[k](groups[step - k])
 
@@ -161,21 +180,29 @@
     return jnp.concatenate(out, axis=1)
 
 
-def first_kernel(
-    par_ref, full_ref, low_ref, high_ref, wemb_ref, lev_ref, gain_ref, wq_ref, wkv_ref, wo_ref,
-    x1_ref, send_ref,
-    wide, gathered, x0, normed, query, keyval, heads,
-):
+MIDDLE, EDGES = (1, 2, 3), (0, 4)
+
+
+def first_kernel(which, *refs):
+    par_ref, full_ref, refs = refs[0], refs[1], refs[2:]
+    if which == EDGES:
+        low_ref, high_ref, refs = refs[0], refs[1], refs[2:]
+    wemb_ref, lev_ref, gain_ref, wq_ref, wkv_ref, wo_ref, x1_ref, send_ref, *refs = refs
+    wide, gathered, x0, normed, query, keyval, heads = refs
     par = par_ref[0]
-    wide[:, :, 0:16, :] = low_ref[...].astype(F32)
-    wide[:, :, 16:80, :] = full_ref[...].astype(F32)
-    wide[:, :, 80:96, :] = high_ref[...].astype(F32)
+    if which == EDGES:
+        wide[:, :, 0:16, :] = low_ref[...].astype(F32)
+        wide[:, :, 16:32, :] = full_ref[:, :, 0:16, :].astype(F32)
+        wide[:, :, 64:80, :] = full_ref[:, :, 48:64, :].astype(F32)
+        wide[:, :, 80:96, :] = high_ref[...].astype(F32)
+    else:
+        wide[:, :, 16:80, :] = full_ref[...].astype(F32)
     gain = gain_ref[0:1, :]
     half = 1 - par
 
     def embed(group):
         part, g = group
-        slot = part * 5 + g
+        slot = part * len(which) + which.index(g)
         base = 8 * (par if part else half)
         for dj in range(3):
             cols = slice(g * 16 + 7 + dj, g * 16 + 23 + dj)
@@ -189,13 +216,13 @@
             x0[slot, level] = x.reshape(8, 16, D)
 
     def norm(group):
-        slot = group[0] * 5 + group[1]
+        slot = group[0] * len(which) + which.index(group[1])
         for u in range(2):
             x = x0[slot, :, :, u * 8 : u * 8 + 8, :].reshape(128, D)
             normed[slot, u] = normalize(x, gain).astype(BF).reshape(2, 4, 16, D)
 
     def project(group):
-        slot = group[0] * 5 + group[1]
+        slot = group[0] * len(which) + which.index(group[1])
         n = normed[slot].reshape(256, D)
         keyval[slot] = mm(n, wkv_ref[0]).astype(BF).reshape(2, 128, 1024)
         if group[0]:
@@ -204,7 +231,7 @@
         query[slot, :, : q.shape[0] // 2] = q.reshape(2, -1, D)
 
     def attention(group):
-        slot = group[0] * 5 + group[1]
+        slot = group[0] * len(which) + which.index(group[1])
         count = 64 if group[0] else 128
         for u in range(2):
             kv = keyval[slot, u]
@@ -212,11 +239,12 @@
 
     def project_out(group):
         part, g = group
-        slot = part * 5 + g
+        slot = part * len(which) + which.index(g)
         count = 64 if part else 128
         out = mm(heads[slot, :, :count].reshape(2 * count, D), wo_ref[0])
         for u in range(2):
-            cols = slice(g * 16 + u * 8, g * 16 + u * 8 + 8)
+            at = which.index(g) * 16 + u * 8
+            cols = slice(at, at + 8)
             mine = slice(u * 8, u * 8 + 8)
             add = out[u * count : u * count + count].reshape(2, count // 16, 8, D)
             if part:
@@ -227,63 +255,73 @@
                     rows = slice(4 * h, 4 * h + 4)
                     x1_ref[:, to, cols, :] = x0[slot, :, rows, mine, :] + add[:, rows]
 
-    groups = [(part, g) for part in range(2) for g in range(5)]
+    groups = [(part, g) for part in range(2) for g in which]
     pipelined([embed, norm, project, attention, project_out], groups)
     send_ref[...] = x1_ref[:, 8:12].astype(BF)
 
 
-def first_block(par, full, low, high, wemb, level_embed, norm_gain, w_query, w_keyval, w_out):
+def first_block(which, par, patch_arrays, wemb, level_embed, norm_gain, w_query, w_keyval, w_out):
     vmem = pl.BlockSpec(memory_space=pltpu.VMEM)
+    count = 2 * len(which)
     return pl.pallas_call(
-        first_kernel,
+        functools.partial(first_kernel, which),
         out_shape=(
-            jax.ShapeDtypeStruct((2, 12, 80, D), F32),
-            jax.ShapeDtypeStruct((2, 4, 80, D), BF),
+            jax.ShapeDtypeStruct((2, 12, 8 * count, D), F32),
+            jax.ShapeDtypeStruct((2, 4, 8 * count, D), BF),
         ),
-        in_specs=[pl.BlockSpec(memory_space=pltpu.SMEM)] + [vmem] * 9,
+        in_specs=[pl.BlockSpec(memory_space=pltpu.SMEM)] + [vmem] * (6 + len(patch_arrays)),
         out_specs=(vmem, vmem),
         scratch_shapes=[
             pltpu.VMEM((2, 18, 96, 128), F32),
-            pltpu.VMEM((10, 2, 10, 16, 384), BF),
-            pltpu.VMEM((10, 2, 8, 16, D), F32),
-            pltpu.VMEM((10, 2, 2, 4, 16, D), BF),
-            pltpu.VMEM((10, 2, 128, D), BF),
-            pltpu.VMEM((10, 2, 128, 1024), BF),
-            pltpu.VMEM((10, 2, 128, D), BF),
+            pltpu.VMEM((count, 2, 10, 16, 384), BF),
+            pltpu.VMEM((count, 2, 8, 16, D), F32),
+            pltpu.VMEM((count, 2, 2, 4, 16, D), BF),
+            pltpu.VMEM((count, 2, 128, D), BF),
+            pltpu.VMEM((count, 2, 128, 1024), BF),
+            pltpu.VMEM((count, 2, 128, D), BF),
         ],
         compiler_params=params(),
-        cost_estimate=pl.CostEstimate(flops=2 * 10**10, bytes_accessed=10**7, transcendentals=0),
-    )(par, full, low, high, wemb, level_embed, norm_gain, w_query, w_keyval, w_out)
+        cost_estimate=pl.CostEstimate(flops=10**10, bytes_accessed=10**7, transcendentals=0),
+    )(par, *patch_arrays, wemb, level_embed, norm_gain, w_query, w_keyval, w_out)
 
 
 SHIFTED = WINS - 1
 
 
 def second_kernel(
-    par_ref, x1_ref, near_ref, gain_ref, mgain_ref, wq_ref, wkv_ref, wo_ref, wm_ref,
+    par_ref, mid_ref, edge_ref, near_mid_ref, near_edge_ref, gain_ref, mgain_ref,
+    wq_ref, wkv_ref, wo_ref, wm_ref,
     out_ref,
     near, x2, normed, query, keyval, heads,
 ):
     par, pole = par_ref[0], par_ref[1]
-    near[...] = near_ref[...].astype(F32)
+    near[:, :, 0:16, :] = near_edge_ref[:, :, 0:16, :].astype(F32)
+    near[:, :, 16:64, :] = near_mid_ref[...].astype(F32)
+    near[:, :, 64:80, :] = near_edge_ref[:, :, 16:32, :].astype(F32)
     gain = gain_ref[1:2, :]
     upper = iota((8, D), 0) >= 4
     key_row = (iota((1, 256), 1) // 8) % 8
     bias = jnp.where(key_row < 4, F32(-1e30), F32(0)) * pole.astype(F32)
 
-    def window(ref, w, rows):
-        a = ref[:, rows, w * 8 : w * 8 + 8, :]
-        b = ref[:, rows, w * 8 + 8 : w * 8 + 16, :]
-        return jnp.where(upper, a, b)
+    def block(n, first, last):
+        if first >= 12:
+            return near[:, first - 12 : last - 12, n * 8 : n * 8 + 8, :]
+        if 2 <= n < 8:
+            return mid_ref[:, first:last, n * 8 - 16 : n * 8 - 8, :]
+        at = n * 8 - (48 if n >= 8 else 0)
+        return edge_ref[:, first:last, at : at + 8, :]
+
+    def window(w, first, last):
+        return jnp.where(upper, block(w, first, last), block(w + 1, first, last))
 
     def norm(group):
         s, g = group
         for w in range(g * 3, g * 3 + 3):
             if s == 0:
-                x = window(x1_ref, w, slice(0, 8))
+                x = window(w, 0, 8)
             else:
                 x = jnp.concatenate(
-                    [window(x1_ref, w, slice(8, 12)), window(near, w, slice(0, 4))], axis=1
+                    [window(w, 8, 12), window(w, 12, 16)], axis=1
                 )
             n = normalize(x.reshape(128, D), gain).astype(BF)
             normed[s * SHIFTED + w] = n.reshape(2, 4, 16, D)
@@ -309,7 +347,7 @@
         rows = slice(s * 4, s * 4 + 4)
         for u in range(3):
             w = g * 3 + u
-            new = window(x1_ref, w, slice(4 + s * 4, 8 + s * 4))
+            new = window(w, 4 + s * 4, 8 + s * 4)
             new = new + out[u * 64 : u * 64 + 64].reshape(2, 4, 8, D)
             for c in range(4):
                 piece = new[..., c * 128 : c * 128 + 128]
@@ -342,12 +380,12 @@
     pipelined([norm, project, attention, project_out, merge], groups)
 
 
-def second_block(par, x1, near, norm_gain, merge_gain, w_query, w_keyval, w_out, merge_weight):
+def second_block(par, mid, edge, near_mid, near_edge, norm_gain, merge_gain, w_query, w_keyval, w_out, merge_weight):
     vmem = pl.BlockSpec(memory_space=pltpu.VMEM)
     return pl.pallas_call(
         second_kernel,
         out_shape=jax.ShapeDtypeStruct((2, 4, 32, 1024), BF),
-        in_specs=[pl.BlockSpec(memory_space=pltpu.SMEM)] + [vmem] * 8,
+        in_specs=[pl.BlockSpec(memory_space=pltpu.SMEM)] + [vmem] * 10,
         out_specs=vmem,
         scratch_shapes=[
             pltpu.VMEM((2, 4, 80, D), F32),
@@ -359,7 +397,9 @@
         ],
         compiler_params=params(),
         cost_estimate=pl.CostEstimate(flops=10**10, bytes_accessed=10**7, transcendentals=0),
-    )(par, x1, near, norm_gain, merge_gain, w_query, w_keyval, w_out, merge_weight)
+    )(
+        par, mid, edge, near_mid, near_edge, norm_gain, merge_gain, w_query, w_keyval, w_out, merge_weight
+    )
 
 
 def embedding_matrix(embed_weight, land_embed):
@@ -405,12 +445,14 @@
     far, wemb = lax.optimization_barrier((far, wemb))
     full, low, high = unpack(place, band, far)
     from_low, from_high = around(high, 1), around(low, -1)
-    x1, send = first_block(
-        place, full, from_low, from_high, wemb, level_embed, norm_gain, w_query, w_keyval, w_out
-    )
-    near = swap(send, 0)
+    weights = wemb, level_embed, norm_gain, w_query, w_keyval, w_out
+    mid, send_mid = first_block(MIDDLE, place, (full,), *weights)
+    near_mid = swap(send_mid, 0)
+    edge, send_edge = first_block(EDGES, place, (full, from_low, from_high), *weights)
+    near_edge = swap(send_edge, 0)
     return second_block(
-        place, x1, near, norm_gain, merge_gain.reshape(1, -1), w_query, w_keyval, w_out, merge_weight
+        place, mid, edge, near_mid, near_edge, norm_gain, merge_gain.reshape(1, -1),
+        w_query, w_keyval, w_out, merge_weight,
     )
 
 

time: 57.9 us -> 55.6 us (0.960)
  waiting for transfers between devices: 4.78 us -> 2.31 us
  Pallas kernels: 29.1 us -> 29.8 us
    ppermute x2, waiting for transfers between devices: 2.27 us -> 0.01 us  [around(): lax.ppermute(block, 'lon', [(i, (i + distance) % count) for i in range(co...]
    pallas_call x1 -> x2, Pallas kernels: 14.8 us -> 15.1 us  [first_block(): pl.pallas_call(functools.partial(first_kernel, which), out_shape=(jax.Sha...]
    ppermute x3 -> x4, waiting for transfers between devices: 2.51 us -> 2.3 us  [swap(): return lax.ppermute(block, 'lat', pairs)]
    ppermute x3 -> x4, starting transfers between devices: 8.12 us -> 8.13 us  [swap(): return lax.ppermute(block, 'lat', pairs)]
  transfers between devices with their start and end apart: 5 -> 6, of which waited for: 3 -> 2; matrix products, arithmetic and copies ran while one was open for 11% -> 12% of each run, Pallas kernels for 0% -> 27%
where the time goes in v3:
time: 55.6 us; the launch traced here: 55.3 us
  Pallas kernels  29.8 us (54%)
  starting transfers between devices  14.1 us (25%)
  local copies, waits for them, and re-layouts  6.88 us (12%)
  waiting for transfers between devices  2.31 us (4%)
  other arithmetic  2.05 us (4%)
    pallas_call x2, Pallas kernels, first_block(): pl.pallas_call(functools.partial(first_kernel, which), out_shape=(jax.Sha...  15.1 us
    pallas_call x1, Pallas kernels, second_block(): pl.pallas_call(second_kernel, out_shape=jax.ShapeDtypeStruct((2, 4, 32, 1...  11.8 us
    ppermute x4, starting transfers between devices, swap(): return lax.ppermute(block, 'lat', pairs)  8.13 us
    ppermute x2, starting transfers between devices, around(): lax.ppermute(block, 'lon', [(i, (i + distance) % count) for i in range(co...  5.96 us
    reshape x1, local copies, waits for them, and re-layouts, embedding_matrix(): return jnp.concatenate([w, land], axis=3).reshape(9 * 128, D)  2.46 us
    unnamed x22, local copies, waits for them, and re-layouts  2.43 us
    ppermute x4, waiting for transfers between devices, swap(): return lax.ppermute(block, 'lat', pairs)  2.3 us
    pallas_call x1, Pallas kernels, patches(): pl.pallas_call(patch_kernel, out_shape=(jax.ShapeDtypeStruct((9, 96, 128)...  2.05 us
  transfers between devices with their start and end apart: 6, of which 2 were waited for; matrix products, arithmetic and copies ran while one was open for 12% of the time, Pallas kernels for 27%

profile of v3, /device:TPU:25, one launch (start us, length us, event | category | flops | bytes accessed | tf_op | source)
XLA Modules:
  0.0 55.3 jit_solution(12629984434666978917)
XLA Ops:
  0.0 0.1 pad_add_fusion.par_ref.refs_0_
  0.1 0.0 copy-start.4
  0.1 0.9 %copy-done.4 = bf16[2,5,32,256]{3,2,1,0:T(8,128)(2,1)S(1)} copy-done((bf16[2,5,32,256]{3,2,1,0:T(8,128)(2,1)S(1)}, bf16[2,5,32,256]{3,2,1,0:T(8,128)(2,1)}, u32[]{:S(2)}) %copy-start.4) | copy-done | bytes 163864
  1.0 0.0 copy-start.5
  1.0 0.8 %copy-done.5 = s32[32,256]{1,0:T(8,128)S(1)} copy-done((s32[32,256]{1,0:T(8,128)S(1)}, s32[32,256]{1,0:T(8,128)}, u32[]{:S(2)}) %copy-start.5) | copy-done | bytes 32792
  1.8 0.0 copy-start.6
  1.8 0.7 %copy-done.6 = bf16[32,256]{1,0:T(8,128)(2,1)S(1)} copy-done((bf16[32,256]{1,0:T(8,128)(2,1)S(1)}, bf16[32,256]{1,0:T(8,128)(2,1)}, u32[]{:S(2)}) %copy-start.6) | copy-done | bytes 16408
  2.5 0.0 copy-start.10
  2.5 2.1 %shard_map.118 = (bf16[9,96,128]{2,1,0:T(8,128)(2,1)S(1)}, bf16[1,96,128]{2,1,0:T(8,128)(2,1)S(1)}) custom-call(s32[2]{0:T(128)S(1)} %pad_add_fusion.par_ref.refs_0_, bf16[2,5,32,256]{3,2,1,0:T(8,128)(2,1)S(1)} %copy-done.4, bf16[32,256]{1,0:T(8,128)(2,1)S(1)} %copy-done.6, s32[32,256]{1,0:T(8,128)S(1)} %copy-done.5), custom_call_target="tpu_custom_call" | custom-call | flops 1000000000 | bytes 1000000 | tf_op jit(solution)/shard_map/pallas_call | solution.py:83
  4.5 0.8 %collective-permute-start = (bf16[1,96,128]{2,1,0:T(8,128)(2,1)S(1)}, bf16[1,96,128]{2,1,0:T(8,128)(2,1)S(1)}, u32[]{:S(2)}, u32[]{:S(2)}) collective-permute-start(bf16[1,96,128]{2,1,0:T(8,128)(2,1)S(1)} %get-tuple-element.17), channel_id=1, source_target_pairs={{0,16},{16,0},{32,48},{48,32},{64,80},{80,64},{96,112},{112,96},{1... | collective-permute-start | bytes 73736 | tf_op jit(solution)/shard_map/ppermute | solution.py:421
  5.3 0.0 copy-done.10
  5.4 0.8 %collective-permute-done = bf16[1,96,128]{2,1,0:T(8,128)(2,1)S(1)} collective-permute-done((bf16[1,96,128]{2,1,0:T(8,128)(2,1)S(1)}, bf16[1,96,128]{2,1,0:T(8,128)(2,1)S(1)}, u32[]{:S(2)}, u32[]{:S(2)}) %collective-permute-start) | collective-permute-done | bytes 24608 | tf_op jit(solution)/shard_map/ppermute | solution.py:421
  6.2 4.9 %collective-permute-start.1 = (bf16[9,96,128]{2,1,0:T(8,128)(2,1)S(1)}, bf16[9,96,128]{2,1,0:T(8,128)(2,1)S(1)}, u32[]{:S(2)}, u32[]{:S(2)}) collective-permute-start(bf16[9,96,128]{2,1,0:T(8,128)(2,1)S(1)} %constant_dynamic-update-slice_fusion.band_ref), channel_id=1, source_target_pairs={{16,32},{32,16},{48,64},{64,48},{80,96},{96,80},{112,128},{128,112... | collective-permute-start | bytes 663560 | tf_op jit(solution)/shard_map/ppermute | solution.py:421
  11.0 0.1 broadcast_select_fusion
  11.2 2.0 %copy.15 = bf16[3,4,3,4,6,512]{5,1,4,3,2,0:T(4,128)(2,1)S(1)} copy(bf16[3,4,3,4,6,512]{5,4,3,2,1,0:T(8,128)(2,1)} %bitcast.9) | data formatting | bytes 1769472 | tf_op jit(solution)/shard_map/reshape | solution.py:406
  13.2 1.8 %pad_maximum_fusion = bf16[3,3,4,8,4,512]{5,4,3,2,1,0:T(4,128)(2,1)} fusion(bf16[3,3,4,2,4,512]{5,4,3,2,1,0:T(4,128)(2,1)S(1)} %broadcast_select_fusion, bf16[3,3,4,6,4,512]{5,4,3,2,1,0:T(4,128)(2,1)S(1)} %bitcast.8), kind=kLoop, calls=%fused_computation | loop fusion | flops 589824 | bytes 2359296 | tf_op jit(solution)/shard_map/concatenate | solution.py:413
  15.0 0.0 copy-start.3
  15.0 2.5 %reshape.38.refs_2_.refs_4_ = bf16[1152,512]{1,0:T(8,128)(2,1)S(1)} reshape(bf16[3,3,4,8,4,512]{5,4,3,2,1,0:T(4,128)(2,1)} %pad_maximum_fusion) | data formatting | bytes 2359296 | tf_op jit(solution)/shard_map/reshape | solution.py:413
  17.4 0.0 copy-start.1
  17.4 0.0 copy-start.2
  17.5 0.0 copy-start.8
  17.5 0.0 copy-start.9
  17.5 0.0 collective-permute-done.1.far_ref
  17.5 0.9 %shard_map.119 = (bf16[2,18,64,128]{3,2,1,0:T(8,128)(2,1)S(1)}, bf16[2,18,16,128]{3,2,1,0:T(8,128)(2,1)S(1)}, bf16[2,18,16,128]{3,2,1,0:T(8,128)(2,1)S(1)}) custom-call(s32[2]{0:T(128)S(1)} %pad_add_fusion.par_ref.refs_0_, bf16[9,96,128]{2,1,0:T(8,128)(2,1)S(1)} %constant_dynamic-update-slice_fusion.band_ref, ...), custom_call_target="tpu_custom_call" | custom-call | flops 1000000000 | bytes 1000000 | tf_op jit(solution)/shard_map/pallas_call | solution.py:126
  18.4 1.7 %collective-permute-start.2 = (bf16[2,18,16,128]{3,2,1,0:T(8,128)(2,1)S(1)}, bf16[2,18,16,128]{3,2,1,0:T(8,128)(2,1)S(1)}, u32[]{:S(2)}, u32[]{:S(2)}) collective-permute-start(bf16[2,18,16,128]{3,2,1,0:T(8,128)(2,1)S(1)} %get-tuple-element.22), channel_id=1, source_target_pairs={{0,1},{1,2},{2,3},{3,4},{4,5},{5,6},{6,7},{7,8},{8,9},{9,10},{10,1... | collective-permute-start | bytes 442376 | tf_op jit(solution)/shard_map/ppermute | solution.py:426
  20.1 4.2 %collective-permute-start.3 = (bf16[2,18,16,128]{3,2,1,0:T(8,128)(2,1)S(1)}, bf16[2,18,16,128]{3,2,1,0:T(8,128)(2,1)S(1)}, u32[]{:S(2)}, u32[]{:S(2)}) collective-permute-start(bf16[2,18,16,128]{3,2,1,0:T(8,128)(2,1)S(1)} %get-tuple-element.23), channel_id=1, source_target_pairs={{0,15},{1,0},{2,1},{3,2},{4,3},{5,4},{6,5},{7,6},{8,7},{9,8},{10,9... | collective-permute-start | bytes 442376 | tf_op jit(solution)/shard_map/ppermute | solution.py:426
  24.3 0.0 copy-done.3
  24.3 0.0 copy-done.1
  24.3 0.0 copy-done.2
  24.3 0.0 copy-done.8
  24.3 0.0 copy-done.9
  24.4 9.0 %shard_map.120 = (f32[2,12,48,512]{3,2,1,0:T(8,128)S(1)}, bf16[2,4,48,512]{3,2,1,0:T(8,128)(2,1)S(1)}) custom-call(s32[2]{0:T(128)S(1)} %pad_add_fusion.par_ref.refs_0_, bf16[2,18,64,128]{3,2,1,0:T(8,128)(2,1)S(1)} %get-tuple-element.19.refs_1_, bf16[1152,512]{1,0:T(8,128)(2,1)S(1)} %reshape.38.refs_2_.refs_4_, f32[2,512]{1,0:T(2,128)S(1)} %copy-done.8, ...), custom_call_target="tpu_custom_call" | custom-call | flops 10000000000 | bytes 10000000 | tf_op jit(solution)/shard_map/pallas_call | solution.py:266
  33.3 0.0 copy-start
  33.3 0.0 copy-start.7
  33.3 2.1 %collective-permute-start.4 = (bf16[2,4,48,512]{3,2,1,0:T(8,128)(2,1)S(1)}, bf16[2,4,48,512]{3,2,1,0:T(8,128)(2,1)S(1)}, u32[]{:S(2)}, u32[]{:S(2)}) collective-permute-start(bf16[2,4,48,512]{3,2,1,0:T(8,128)(2,1)S(1)} %get-tuple-element.25), channel_id=1, source_target_pairs={{0,16},{16,0},{32,48},{48,32},{64,80},{80,64},{96,112},{112,96},{1... | collective-permute-start | bytes 1179656 | tf_op jit(solution)/shard_map/ppermute | solution.py:421
  35.5 0.0 collective-permute-done.2.refs_2_
  35.5 0.0 collective-permute-done.3.refs_3_
  35.5 6.2 %shard_map.121 = (f32[2,12,32,512]{3,2,1,0:T(8,128)S(1)}, bf16[2,4,32,512]{3,2,1,0:T(8,128)(2,1)S(1)}) custom-call(s32[2]{0:T(128)S(1)} %pad_add_fusion.par_ref.refs_0_, bf16[2,18,64,128]{3,2,1,0:T(8,128)(2,1)S(1)} %get-tuple-element.19.refs_1_, bf16[2,18,16,128]{3,2,1,0:T(8,128)(2,1)S(1)} %collective-permute-done.2.refs_2_, ...), custom_call_target="tpu_custom_call" | custom-call | flops 10000000000 | bytes 10000000 | tf_op jit(solution)/shard_map/pallas_call | solution.py:266
  41.6 0.4 collective-permute-start.5
  42.0 0.0 collective-permute-done.4.near_mid_ref
  42.0 1.5 %collective-permute-done.5.near_edge_ref = bf16[2,4,32,512]{3,2,1,0:T(8,128)(2,1)S(1)} collective-permute-done((bf16[2,4,32,512]{3,2,1,0:T(8,128)(2,1)S(1)}, bf16[2,4,32,512]{3,2,1,0:T(8,128)(2,1)S(1)}, u32[]{:S(2)}, u32[]{:S(2)}) %collective-permute-start.5) | collective-permute-done | bytes 262176 | tf_op jit(solution)/shard_map/ppermute | solution.py:421
  43.5 0.0 copy-done
  43.5 0.0 copy-done.7
  43.5 11.8 %shard_map.122 = bf16[2,4,32,1024]{3,2,1,0:T(8,128)(2,1)} custom-call(s32[2]{0:T(128)S(1)} %pad_add_fusion.par_ref.refs_0_, f32[2,12,48,512]{3,2,1,0:T(8,128)S(1)} %get-tuple-element.21.mid_ref, f32[2,12,32,512]{3,2,1,0:T(8,128)S(1)} %get-tuple-element.24.edge_ref, bf16[2,4,48,512]{3,2,1,0:T(8,128)(2,1)S(1)} %collective-permute-done.4.near_mid_ref, ...), custom_call_target="tpu_custom_call" | custom-call | flops 10000000000 | bytes 10000000 | tf_op jit(solution)/shard_map/pallas_call | solution.py:385
  (6 shorter events, 0.0 us)
Async XLA Ops:
  0.1 0.9 %copy-start.4 = (bf16[2,5,32,256]{3,2,1,0:T(8,128)(2,1)S(1)}, bf16[2,5,32,256]{3,2,1,0:T(8,128)(2,1)}, u32[]{:S(2)}) copy-start(bf16[2,5,32,256]{3,2,1,0:T(8,128)(2,1)} %atmos_any.1) | copy-start | bytes 491524
  1.0 0.8 %copy-start.5 = (s32[32,256]{1,0:T(8,128)S(1)}, s32[32,256]{1,0:T(8,128)}, u32[]{:S(2)}) copy-start(s32[32,256]{1,0:T(8,128)} %land_any.1) | copy-start | bytes 98308
  1.8 0.7 %copy-start.6 = (bf16[32,256]{1,0:T(8,128)(2,1)S(1)}, bf16[32,256]{1,0:T(8,128)(2,1)}, u32[]{:S(2)}) copy-start(bf16[32,256]{1,0:T(8,128)(2,1)} %oro_any.1) | copy-start | bytes 49156
  2.5 2.8 %copy-start.10 = (f32[512]{0:T(512)S(1)}, f32[512]{0:T(512)}, u32[]{:S(2)}) copy-start(f32[512]{0:T(512)} %param.17) | copy-start | bytes 6148
  4.5 1.6 %collective-permute-start = (bf16[1,96,128]{2,1,0:T(8,128)(2,1)S(1)}, bf16[1,96,128]{2,1,0:T(8,128)(2,1)S(1)}, u32[]{:S(2)}, u32[]{:S(2)}) collective-permute-start(bf16[1,96,128]{2,1,0:T(8,128)(2,1)S(1)} %get-tuple-element.17), channel_id=1, source_target_pairs={{0,16},{16,0},{32,48},{48,32},{64,80},{80,64},{96,112},{112,96},{1... | collective-permute-start | bytes 73736 | tf_op jit(solution)/shard_map/ppermute | solution.py:421
  6.2 11.3 %collective-permute-start.1 = (bf16[9,96,128]{2,1,0:T(8,128)(2,1)S(1)}, bf16[9,96,128]{2,1,0:T(8,128)(2,1)S(1)}, u32[]{:S(2)}, u32[]{:S(2)}) collective-permute-start(bf16[9,96,128]{2,1,0:T(8,128)(2,1)S(1)} %constant_dynamic-update-slice_fusion.band_ref), channel_id=1, source_target_pairs={{16,32},{32,16},{48,64},{64,48},{80,96},{96,80},{112,128},{128,112... | collective-permute-start | bytes 663560 | tf_op jit(solution)/shard_map/ppermute | solution.py:421
  15.0 9.4 %copy-start.3 = (bf16[2,512,512]{2,1,0:T(8,128)(2,1)S(1)}, bf16[2,512,512]{2,1,0:T(8,128)(2,1)}, u32[]{:S(2)}) copy-start(bf16[2,512,512]{2,1,0:T(8,128)(2,1)} %wo_ref.1) | copy-start | bytes 3145732
  17.4 6.9 %copy-start.1 = (bf16[2,512,1024]{2,1,0:T(8,128)(2,1)S(1)}, bf16[2,512,1024]{2,1,0:T(8,128)(2,1)}, u32[]{:S(2)}) copy-start(bf16[2,512,1024]{2,1,0:T(8,128)(2,1)} %wkv_ref.1) | copy-start | bytes 6291460
  17.4 6.9 %copy-start.2 = (bf16[2,512,512]{2,1,0:T(8,128)(2,1)S(1)}, bf16[2,512,512]{2,1,0:T(8,128)(2,1)}, u32[]{:S(2)}) copy-start(bf16[2,512,512]{2,1,0:T(8,128)(2,1)} %wq_ref.1) | copy-start | bytes 3145732
  17.5 6.9 %copy-start.8 = (f32[2,512]{1,0:T(2,128)S(1)}, f32[2,512]{1,0:T(2,128)}, u32[]{:S(2)}) copy-start(f32[2,512]{1,0:T(2,128)} %refs_5_.3) | copy-start | bytes 12292
  17.5 6.9 %copy-start.9 = (f32[2,512]{1,0:T(2,128)S(1)}, f32[2,512]{1,0:T(2,128)}, u32[]{:S(2)}) copy-start(f32[2,512]{1,0:T(2,128)} %gain_ref.1) | copy-start | bytes 12292
  18.4 17.1 %collective-permute-start.2 = (bf16[2,18,16,128]{3,2,1,0:T(8,128)(2,1)S(1)}, bf16[2,18,16,128]{3,2,1,0:T(8,128)(2,1)S(1)}, u32[]{:S(2)}, u32[]{:S(2)}) collective-permute-start(bf16[2,18,16,128]{3,2,1,0:T(8,128)(2,1)S(1)} %get-tuple-element.22), channel_id=1, source_target_pairs={{0,1},{1,2},{2,3},{3,4},{4,5},{5,6},{6,7},{7,8},{8,9},{9,10},{10,1... | collective-permute-start | bytes 442376 | tf_op jit(solution)/shard_map/ppermute | solution.py:426
  20.1 15.4 %collective-permute-start.3 = (bf16[2,18,16,128]{3,2,1,0:T(8,128)(2,1)S(1)}, bf16[2,18,16,128]{3,2,1,0:T(8,128)(2,1)S(1)}, u32[]{:S(2)}, u32[]{:S(2)}) collective-permute-start(bf16[2,18,16,128]{3,2,1,0:T(8,128)(2,1)S(1)} %get-tuple-element.23), channel_id=1, source_target_pairs={{0,15},{1,0},{2,1},{3,2},{4,3},{5,4},{6,5},{7,6},{8,7},{9,8},{10,9... | collective-permute-start | bytes 442376 | tf_op jit(solution)/shard_map/ppermute | solution.py:426
  33.3 10.2 %copy-start = (bf16[2048,1024]{1,0:T(8,128)(2,1)S(1)}, bf16[2048,1024]{1,0:T(8,128)(2,1)}, u32[]{:S(2)}) copy-start(bf16[2048,1024]{1,0:T(8,128)(2,1)} %wm_ref.1) | copy-start | bytes 12582916
  33.3 10.2 %copy-start.7 = (f32[2048]{0:T(1024)S(1)}, f32[2048]{0:T(1024)}, u32[]{:S(2)}) copy-start(f32[2048]{0:T(1024)} %param.22) | copy-start | bytes 24580
  33.3 8.7 %collective-permute-start.4 = (bf16[2,4,48,512]{3,2,1,0:T(8,128)(2,1)S(1)}, bf16[2,4,48,512]{3,2,1,0:T(8,128)(2,1)S(1)}, u32[]{:S(2)}, u32[]{:S(2)}) collective-permute-start(bf16[2,4,48,512]{3,2,1,0:T(8,128)(2,1)S(1)} %get-tuple-element.25), channel_id=1, source_target_pairs={{0,16},{16,0},{32,48},{48,32},{64,80},{80,64},{96,112},{112,96},{1... | collective-permute-start | bytes 1179656 | tf_op jit(solution)/shard_map/ppermute | solution.py:421
  41.6 1.9 %collective-permute-start.5 = (bf16[2,4,32,512]{3,2,1,0:T(8,128)(2,1)S(1)}, bf16[2,4,32,512]{3,2,1,0:T(8,128)(2,1)S(1)}, u32[]{:S(2)}, u32[]{:S(2)}) collective-permute-start(bf16[2,4,32,512]{3,2,1,0:T(8,128)(2,1)S(1)} %get-tuple-element.26), channel_id=1, source_target_pairs={{0,16},{16,0},{32,48},{48,32},{64,80},{80,64},{96,112},{112,96},{1... | collective-permute-start | bytes 786440 | tf_op jit(solution)/shard_map/ppermute | solution.py:421

commit v4 on v3

--- a/solution.py
+++ b/solution.py
@@ -38,7 +38,8 @@
 
 
 def patch_kernel(
-    par_ref, atmos_any, oro_any, land_any, band_ref, edge_ref, atmos_ref, oro_ref, land_ref, sems
+    par_ref, atmos_any, oro_any, land_any, own_ref, send_ref, edge_ref, near_ref,
+    atmos_ref, oro_ref, land_ref, sems,
 ):
     par = par_ref[0]
     loads = [
@@ -49,6 +50,11 @@
     ]
     for load in loads:
         load.start()
+    row, src = iota((1024, 384), 0), iota((1024, 384), 1)
+    i, r, ch = row // 128, (row % 128) // 32, row % 8
+    channel = jnp.where(ch < 5, ch, jnp.where(ch == 5, 10, jnp.where(ch == 6, 11, 9)))
+    pick_main = one_hot(src == channel * 32 + i * 4 + r)
+    pick_aux = one_hot(src == (5 + row % 4) * 32 + i * 4 + r)
     for load in loads:
         load.wait()
     cells = jnp.concatenate(
@@ -59,14 +65,9 @@
         ],
         axis=0,
     )
-    row, src = iota((1024, 384), 0), iota((1024, 384), 1)
-    i, ch, r = row // 128, (row % 32) // 4, row % 4
-    channel = jnp.where(ch < 5, ch, jnp.where(ch == 5, 10, jnp.where(ch == 6, 11, 9)))
-    main = mm(one_hot(src == channel * 32 + i * 4 + r), cells)
-    channel = 5 + (row % 16) // 4
-    aux = mm(one_hot(src == channel * 32 + i * 4 + r), cells)
+    main, aux = mm(pick_main, cells), mm(pick_aux, cells)
     row, col = iota((1024, 256), 0), iota((1024, 256), 1)
-    c, half = (row % 128) // 32, (row % 32) // 16
+    c, half = (row % 32) // 8, (row % 8) // 4
     main = jnp.where(col % 4 == c, main, 0.0).astype(BF)
     aux = jnp.where((col % 4 == c) & (col // 128 == half), aux, 0.0).astype(BF)
     j, col = iota((64, 256), 0), iota((64, 256), 1)
@@ -74,20 +75,20 @@
     j, col = iota((32, 256), 0), iota((32, 256), 1)
     aux = mm_t(one_hot((col % 128) // 4 == j), aux).astype(BF)
     for i in range(8):
-        band_ref[par + i, 0:64, :] = main[:, i * 128 : i * 128 + 128]
-        band_ref[par + i, 64:96, :] = aux[:, i * 128 : i * 128 + 128]
-    edge_ref[...] = band_ref[pl.ds(par + 7 * (1 - par), 1)]
+        own_ref[i, 0:64, :] = main[:, i * 128 : i * 128 + 128]
+        own_ref[i, 64:96, :] = aux[:, i * 128 : i * 128 + 128]
+    send_ref[pl.ds(par, 7)] = own_ref[pl.ds(1 - par, 7)]
+    edge_ref[...] = own_ref[pl.ds(7 * (1 - par), 1)]
+    near_ref[...] = own_ref[pl.ds(7 * par, 1)]
 
 
 def patches(par, atmos, orography, land_sea):
+    cells = [pltpu.with_memory_space_constraint(a, pltpu.HBM) for a in (atmos, orography, land_sea)]
     return pl.pallas_call(
         patch_kernel,
-        out_shape=(
-            jax.ShapeDtypeStruct((9, 96, 128), BF),
-            jax.ShapeDtypeStruct((1, 96, 128), BF),
-        ),
+        out_shape=tuple(jax.ShapeDtypeStruct((n, 96, 128), BF) for n in (8, 8, 1, 1)),
         in_specs=[pl.BlockSpec(memory_space=pltpu.SMEM)] + [pl.BlockSpec(memory_space=pltpu.HBM)] * 3,
-        out_specs=(pl.BlockSpec(memory_space=pltpu.VMEM),) * 2,
+        out_specs=(pl.BlockSpec(memory_space=pltpu.VMEM),) * 4,
         scratch_shapes=[
             pltpu.VMEM(atmos.shape, BF),
             pltpu.VMEM(orography.shape, BF),
@@ -96,46 +97,70 @@
         ],
         compiler_params=params(),
         cost_estimate=pl.CostEstimate(flops=10**9, bytes_accessed=10**6, transcendentals=0),
-    )(par, atmos, orography, land_sea)
-
-
-def unpack_kernel(par_ref, band_ref, far_ref, full_ref, low_ref, high_ref, packed):
-    par = par_ref[0]
-    packed[pl.ds(9 * (1 - par), 9)] = band_ref[...]
-    packed[pl.ds(9 * par, 9)] = far_ref[...]
+    )(par, *cells)
+
+
+def unpack_rows(packed, out_ref):
+    rows = packed.shape[0]
     k, n = iota((256, 256), 0), iota((256, 256), 1)
-    ch, lane = (n % 32) // 4, n % 128
-    from_main0 = jnp.where(ch == 7, lane - 4, lane)
-    from_main1 = jnp.where(ch == 7, lane - 4, jnp.where(ch == 4, lane + 12, lane))
+    ch, lane = n % 8, n % 128
+    from_main0 = jnp.where(ch == 7, lane - 1, lane)
+    from_main1 = jnp.where(ch == 7, lane - 1, jnp.where(ch == 4, lane + 3, lane))
     aux = packed[:, 64:96, :]
     for half in range(2):
-        from_one = jnp.where(ch < 4, 128 + lane + 16 * half, from_main1)
+        from_one = jnp.where(ch < 4, 128 + lane + 4 * half, from_main1)
         pick = one_hot(k == jnp.where(n < 128, from_main0, from_one))
         both = jnp.concatenate([packed[:, half * 32 : half * 32 + 32, :], aux], axis=2)
-        got = mm(both.reshape(18 * 32, 256), pick).astype(BF).reshape(18, 32, 256)
+        got = mm(both.reshape(rows * 32, 256), pick).astype(BF).reshape(rows, 32, 256)
         for level in range(2):
             tile = got[:, :, level * 128 : level * 128 + 128]
-            full_ref[level, :, half * 32 : half * 32 + 32, :] = tile
-            if half == 0:
-                low_ref[level] = tile[:, :16, :]
-            else:
-                high_ref[level] = tile[:, 16:, :]
-
-
-def unpack(par, band, far):
+            out_ref[level, :, half * 32 : half * 32 + 32, :] = tile
+
+
+def unpack_own_kernel(par_ref, own_ref, edge_ref, near_ref, full_ref, packed):
+    par = par_ref[0]
+    packed[1:9] = own_ref[...]
+    packed[pl.ds(9 * par, 1)] = near_ref[...]
+    packed[pl.ds(9 * (1 - par), 1)] = edge_ref[...]
+    unpack_rows(packed, full_ref)
+
+
+def unpack_own(par, own, edge, near):
+    vmem = pl.BlockSpec(memory_space=pltpu.VMEM)
     return pl.pallas_call(
-        unpack_kernel,
+        unpack_own_kernel,
+        out_shape=jax.ShapeDtypeStruct((2, 10, 64, 128), BF),
+        in_specs=[pl.BlockSpec(memory_space=pltpu.SMEM)] + [vmem] * 3,
+        out_specs=vmem,
+        scratch_shapes=[pltpu.VMEM((10, 96, 128), BF)],
+        compiler_params=params(),
+        cost_estimate=pl.CostEstimate(flops=10**9, bytes_accessed=10**6, transcendentals=0),
+    )(par, own, edge, near)
+
+
+def unpack_far_kernel(after_ref, packed_ref, own_ref, far_ref, low_ref, high_ref):
+    del after_ref
+    unpack_rows(packed_ref, far_ref)
+    low_ref[:, 0:10] = own_ref[:, :, 0:16, :]
+    low_ref[:, 10:18] = far_ref[:, :, 0:16, :]
+    high_ref[:, 0:10] = own_ref[:, :, 48:64, :]
+    high_ref[:, 10:18] = far_ref[:, :, 48:64, :]
+
+
+def unpack_far(after, packed, own):
+    vmem = pl.BlockSpec(memory_space=pltpu.VMEM)
+    return pl.pallas_call(
+        unpack_far_kernel,
         out_shape=(
-            jax.ShapeDtypeStruct((2, 18, 64, 128), BF),
+            jax.ShapeDtypeStruct((2, 8, 64, 128), BF),
             jax.ShapeDtypeStruct((2, 18, 16, 128), BF),
             jax.ShapeDtypeStruct((2, 18, 16, 128), BF),
         ),
-        in_specs=[pl.BlockSpec(memory_space=pltpu.SMEM)] + [pl.BlockSpec(memory_space=pltpu.VMEM)] * 2,
-        out_specs=(pl.BlockSpec(memory_space=pltpu.VMEM),) * 3,
-        scratch_shapes=[pltpu.VMEM((18, 96, 128), BF)],
+        in_specs=[pl.BlockSpec(memory_space=pl.ANY)] + [vmem] * 2,
+        out_specs=(vmem,) * 3,
         compiler_params=params(),
         cost_estimate=pl.CostEstimate(flops=10**9, bytes_accessed=10**6, transcendentals=0),
-    )(par, band, far)
+    )(after, packed, own)
 
 
 def pipelined(stages, groups):
@@ -183,30 +208,46 @@
 MIDDLE, EDGES = (1, 2, 3), (0, 4)
 
 
-def first_kernel(which, *refs):
-    par_ref, full_ref, refs = refs[0], refs[1], refs[2:]
+def first_kernel(parts, which, after_ref, *refs):
+    del after_ref
+    par_ref, own_ref, refs = refs[0], refs[1], refs[2:]
+    if 1 in parts:
+        far_ref, refs = refs[0], refs[1:]
     if which == EDGES:
         low_ref, high_ref, refs = refs[0], refs[1], refs[2:]
-    wemb_ref, lev_ref, gain_ref, wq_ref, wkv_ref, wo_ref, x1_ref, send_ref, *refs = refs
+    wemb_ref, lev_ref, gain_ref, wq_ref, wkv_ref, wo_ref, *refs = refs
+    x1_refs, refs = refs[: len(parts)], refs[len(parts) :]
+    if 0 in parts:
+        send_ref, refs = refs[0], refs[1:]
     wide, gathered, x0, normed, query, keyval, heads = refs
     par = par_ref[0]
-    if which == EDGES:
-        wide[:, :, 0:16, :] = low_ref[...].astype(F32)
-        wide[:, :, 16:32, :] = full_ref[:, :, 0:16, :].astype(F32)
-        wide[:, :, 64:80, :] = full_ref[:, :, 48:64, :].astype(F32)
-        wide[:, :, 80:96, :] = high_ref[...].astype(F32)
-    else:
-        wide[:, :, 16:80, :] = full_ref[...].astype(F32)
+
+    def spread(part, to, count, center, low, high):
+        rows = (slice(None), pl.ds(to, count))
+        if which == EDGES:
+            wide[part, *rows, 0:16, :] = low.astype(F32)
+            wide[part, *rows, 16:32, :] = center[:, :, 0:16, :].astype(F32)
+            wide[part, *rows, 64:80, :] = center[:, :, 48:64, :].astype(F32)
+            wide[part, *rows, 80:96, :] = high.astype(F32)
+        else:
+            wide[part, *rows, 16:80, :] = center.astype(F32)
+
+    sides = [r for r in ((low_ref, high_ref) if which == EDGES else ())]
+    if 0 in parts:
+        spread(0, 0, 10, own_ref[...], *([r[:, 0:10] for r in sides] or (None, None)))
+    if 1 in parts:
+        spread(1, 2 * par, 8, far_ref[...], *([r[:, 10:18] for r in sides] or (None, None)))
+        beside = pl.ds(8 * par, 2)
+        spread(1, 8 * (1 - par), 2, own_ref[:, beside], *([r[:, beside] for r in sides] or (None, None)))
     gain = gain_ref[0:1, :]
     half = 1 - par
 
     def embed(group):
         part, g = group
-        slot = part * len(which) + which.index(g)
-        base = 8 * (par if part else half)
+        slot = groups.index(group)
         for dj in range(3):
             cols = slice(g * 16 + 7 + dj, g * 16 + 23 + dj)
-            got = wide[:, pl.ds(base, 10), cols, :].astype(BF)
+            got = wide[part, :, :, cols, :].astype(BF)
             gathered[slot, :, :, :, dj * 128 : dj * 128 + 128] = got
         for level in range(2):
             lhs = jnp.concatenate(
@@ -216,13 +257,13 @@
             x0[slot, level] = x.reshape(8, 16, D)
 
     def norm(group):
-        slot = group[0] * len(which) + which.index(group[1])
+        slot = groups.index(group)
         for u in range(2):
             x = x0[slot, :, :, u * 8 : u * 8 + 8, :].reshape(128, D)
             normed[slot, u] = normalize(x, gain).astype(BF).reshape(2, 4, 16, D)
 
     def project(group):
-        slot = group[0] * len(which) + which.index(group[1])
+        slot = groups.index(group)
         n = normed[slot].reshape(256, D)
         keyval[slot] = mm(n, wkv_ref[0]).astype(BF).reshape(2, 128, 1024)
         if group[0]:
@@ -231,7 +272,7 @@
         query[slot, :, : q.shape[0] // 2] = q.reshape(2, -1, D)
 
     def attention(group):
-        slot = group[0] * len(which) + which.index(group[1])
+        slot = groups.index(group)
         count = 64 if group[0] else 128
         for u in range(2):
             kv = keyval[slot, u]
@@ -239,7 +280,7 @@
 
     def project_out(group):
         part, g = group
-        slot = part * len(which) + which.index(g)
+        slot = groups.index(group)
         count = 64 if part else 128
         out = mm(heads[slot, :, :count].reshape(2 * count, D), wo_ref[0])
         for u in range(2):
@@ -248,31 +289,33 @@
             mine = slice(u * 8, u * 8 + 8)
             add = out[u * count : u * count + count].reshape(2, count // 16, 8, D)
             if part:
-                x1_ref[:, 0:4, cols, :] = x0[slot, :, pl.ds(4 * half, 4), mine, :] + add
+                x1_refs[-1][:, :, cols, :] = x0[slot, :, pl.ds(4 * half, 4), mine, :] + add
             else:
                 for h in range(2):
-                    to = pl.ds(4 + 4 * (par if h == 0 else half), 4)
+                    to = pl.ds(4 * (par if h == 0 else half), 4)
                     rows = slice(4 * h, 4 * h + 4)
-                    x1_ref[:, to, cols, :] = x0[slot, :, rows, mine, :] + add[:, rows]
-
-    groups = [(part, g) for part in range(2) for g in which]
+                    x1_refs[0][:, to, cols, :] = x0[slot, :, rows, mine, :] + add[:, rows]
+
+    groups = [(part, g) for part in parts for g in which]
     pipelined([embed, norm, project, attention, project_out], groups)
-    send_ref[...] = x1_ref[:, 8:12].astype(BF)
-
-
-def first_block(which, par, patch_arrays, wemb, level_embed, norm_gain, w_query, w_keyval, w_out):
+    if 0 in parts:
+        send_ref[...] = x1_refs[0][:, 4:8].astype(BF)
+
+
+def first_block(parts, which, after, par, patch_arrays, wemb, level_embed, norm_gain, w_query, w_keyval, w_out):
     vmem = pl.BlockSpec(memory_space=pltpu.VMEM)
-    count = 2 * len(which)
+    width, count = 16 * len(which), len(parts) * len(which)
+    outs = [jax.ShapeDtypeStruct((2, 4 if part else 8, width, D), F32) for part in parts]
+    if 0 in parts:
+        outs.append(jax.ShapeDtypeStruct((2, 4, width, D), BF))
     return pl.pallas_call(
-        functools.partial(first_kernel, which),
-        out_shape=(
-            jax.ShapeDtypeStruct((2, 12, 8 * count, D), F32),
-            jax.ShapeDtypeStruct((2, 4, 8 * count, D), BF),
-        ),
-        in_specs=[pl.BlockSpec(memory_space=pltpu.SMEM)] + [vmem] * (6 + len(patch_arrays)),
-        out_specs=(vmem, vmem),
+        functools.partial(first_kernel, parts, which),
+        out_shape=tuple(outs),
+        in_specs=[pl.BlockSpec(memory_space=pl.ANY), pl.BlockSpec(memory_space=pltpu.SMEM)]
+        + [vmem] * (6 + len(patch_arrays)),
+        out_specs=(vmem,) * len(outs),
         scratch_shapes=[
-            pltpu.VMEM((2, 18, 96, 128), F32),
+            pltpu.VMEM((2, 2, 10, 96, 128), F32),
             pltpu.VMEM((count, 2, 10, 16, 384), BF),
             pltpu.VMEM((count, 2, 8, 16, D), F32),
             pltpu.VMEM((count, 2, 2, 4, 16, D), BF),
@@ -282,14 +325,14 @@
         ],
         compiler_params=params(),
         cost_estimate=pl.CostEstimate(flops=10**10, bytes_accessed=10**7, transcendentals=0),
-    )(par, *patch_arrays, wemb, level_embed, norm_gain, w_query, w_keyval, w_out)
+    )(after, par, *patch_arrays, wemb, level_embed, norm_gain, w_query, w_keyval, w_out)
 
 
 SHIFTED = WINS - 1
 
 
 def second_kernel(
-    par_ref, mid_ref, edge_ref, near_mid_ref, near_edge_ref, gain_ref, mgain_ref,
+    par_ref, own_mid, outer_mid, own_edge, outer_edge, near_mid_ref, near_edge_ref, gain_ref, mgain_ref,
     wq_ref, wkv_ref, wo_ref, wm_ref,
     out_ref,
     near, x2, normed, query, keyval, heads,
@@ -304,12 +347,15 @@
     bias = jnp.where(key_row < 4, F32(-1e30), F32(0)) * pole.astype(F32)
 
     def block(n, first, last):
+        if first < 4 < last:
+            return jnp.concatenate([block(n, first, 4), block(n, 4, last)], axis=1)
         if first >= 12:
             return near[:, first - 12 : last - 12, n * 8 : n * 8 + 8, :]
-        if 2 <= n < 8:
-            return mid_ref[:, first:last, n * 8 - 16 : n * 8 - 8, :]
-        at = n * 8 - (48 if n >= 8 else 0)
-        return edge_ref[:, first:last, at : at + 8, :]
+        middle = 2 <= n < 8
+        at = n * 8 - (16 if middle else 48 if n >= 8 else 0)
+        if first < 4:
+            return (outer_mid if middle else outer_edge)[:, first:last, at : at + 8, :]
+        return (own_mid if middle else own_edge)[:, first - 4 : last - 4, at : at + 8, :]
 
     def window(w, first, last):
         return jnp.where(upper, block(w, first, last), block(w + 1, first, last))
@@ -380,12 +426,12 @@
     pipelined([norm, project, attention, project_out, merge], groups)
 
 
-def second_block(par, mid, edge, near_mid, near_edge, norm_gain, merge_gain, w_query, w_keyval, w_out, merge_weight):
+def second_block(par, x1_parts, near_mid, near_edge, norm_gain, merge_gain, w_query, w_keyval, w_out, merge_weight):
     vmem = pl.BlockSpec(memory_space=pltpu.VMEM)
     return pl.pallas_call(
         second_kernel,
         out_shape=jax.ShapeDtypeStruct((2, 4, 32, 1024), BF),
-        in_specs=[pl.BlockSpec(memory_space=pltpu.SMEM)] + [vmem] * 10,
+        in_specs=[pl.BlockSpec(memory_space=pltpu.SMEM)] + [vmem] * 12,
         out_specs=vmem,
         scratch_shapes=[
             pltpu.VMEM((2, 4, 80, D), F32),
@@ -398,19 +444,20 @@
         compiler_params=params(),
         cost_estimate=pl.CostEstimate(flops=10**10, bytes_accessed=10**7, transcendentals=0),
     )(
-        par, mid, edge, near_mid, near_edge, norm_gain, merge_gain, w_query, w_keyval, w_out, merge_weight
+        par, *x1_parts, near_mid, near_edge, norm_gain, merge_gain, w_query, w_keyval, w_out, merge_weight
     )
 
 
 def embedding_matrix(embed_weight, land_embed):
-    w = embed_weight.reshape(3, 4, 3, 4, 6, D).transpose(0, 2, 3, 4, 1, 5)
+    w = jnp.pad(embed_weight, ((0, 0), (0, 0), (0, 2), (0, 0))).reshape(3, 4, 3, 4, 8, D)
+    w = w.transpose(0, 2, 1, 3, 4, 5)
     share = land_embed / 16
     high = lax.reduce_precision(share, 8, 7)
-    terms = jnp.stack([high, share - high]).astype(BF)
-    terms = jnp.broadcast_to(terms[None, :, None, :], (4, 2, 4, D))
-    middle = (jnp.arange(9) == 4).reshape(3, 3, 1, 1, 1, 1)
-    land = jnp.where(middle, terms, jnp.zeros((), BF))
-    return jnp.concatenate([w, land], axis=3).reshape(9 * 128, D)
+    at = [lax.broadcasted_iota(jnp.int32, w.shape, d) for d in (0, 1, 4)]
+    middle = (at[0] == 1) & (at[1] == 1)
+    w = jnp.where(middle & (at[2] == 6), high.astype(BF), w)
+    w = jnp.where(middle & (at[2] == 7), (share - high).astype(BF), w)
+    return w.reshape(9 * 128, D)
 
 
 def swap(block, first):
@@ -437,22 +484,26 @@
     par = lat % 2
     pole = (lat == 0) | (lat == lax.axis_size("lat") - 1)
     place = jnp.stack([par, pole]).astype(jnp.int32)
-    band, edge = patches(place, atmos, orography, land_sea)
+    own, send, edge, near = patches(place, atmos, orography, land_sea)
     edge = swap(edge, 0)
-    band = lax.dynamic_update_slice(band, edge, (8 * (1 - par), 0, 0))
-    far = swap(band, 1)
+    near = swap(near, 1)
+    send = lax.dynamic_update_slice(send, edge, (7 * (1 - par), 0, 0))
+    far = swap(send, 1)
     wemb = embedding_matrix(embed_weight, land_embed)
-    far, wemb = lax.optimization_barrier((far, wemb))
-    full, low, high = unpack(place, band, far)
+    weights = wemb, level_embed, norm_gain, w_query, w_keyval, w_out
+    own = unpack_own(place, own, edge, near)
+    own_mid, send_mid = first_block((0,), MIDDLE, edge, place, (own,), *weights)
+    near_mid = swap(send_mid, 0)
+    far, low, high = unpack_far(own_mid, far, own)
     from_low, from_high = around(high, 1), around(low, -1)
-    weights = wemb, level_embed, norm_gain, w_query, w_keyval, w_out
-    mid, send_mid = first_block(MIDDLE, place, (full,), *weights)
-    near_mid = swap(send_mid, 0)
-    edge, send_edge = first_block(EDGES, place, (full, from_low, from_high), *weights)
+    (outer_mid,) = first_block((1,), MIDDLE, own_mid, place, (own, far), *weights)
+    own_edge, outer_edge, send_edge = first_block(
+        (0, 1), EDGES, outer_mid, place, (own, far, from_low, from_high), *weights
+    )
     near_edge = swap(send_edge, 0)
     return second_block(
-        place, mid, edge, near_mid, near_edge, norm_gain, merge_gain.reshape(1, -1),
-        w_query, w_keyval, w_out, merge_weight,
+        place, (own_mid, outer_mid, own_edge, outer_edge), near_mid, near_edge, norm_gain,
+        merge_gain.reshape(1, -1), w_query, w_keyval, w_out, merge_weight,
     )
 
 

time: 55.6 us -> 50.4 us (0.906)
  local copies, waits for them, and re-layouts: 6.88 us -> 1.29 us
  starting transfers between devices: 14.1 us -> 16.7 us
  other arithmetic: 2.05 us -> 0.53 us
  waiting for transfers between devices: 2.31 us -> 1.17 us
  Pallas kernels: 29.8 us -> 30.4 us
    reshape x2 -> x0, local copies, waits for them, and re-layouts: 4.43 us -> none  [the longest x1 2.46 us: embedding_matrix(): return jnp.concatenate([w, land], axis=3).reshape(9 * 128, D)]
    concatenate x1 -> x0, other arithmetic: 1.8 us -> none  [embedding_matrix(): return jnp.concatenate([w, land], axis=3).reshape(9 * 128, D)]
    ppermute x4 -> x5, starting transfers between devices: 8.13 us -> 9.82 us  [swap(): return lax.ppermute(block, 'lat', pairs)]
    unnamed x22 -> x18, local copies, waits for them, and re-layouts: 2.43 us -> 1.04 us
    ppermute x4 -> x5, waiting for transfers between devices: 2.3 us -> 1.17 us  [swap(): return lax.ppermute(block, 'lat', pairs)]
    ppermute x2, starting transfers between devices: 5.96 us -> 6.85 us  [around(): lax.ppermute(block, 'lon', [(i, (i + distance) % count) for i in range(co...]
    pallas_call x4 -> x6, Pallas kernels: 18 us -> 18.7 us  [the longest x3 15.1 us: first_block(): pl.pallas_call(functools.partial(first_kernel, parts, which), out_shape=t...]
  transfers between devices with their start and end apart: 6 -> 7, of which waited for: 2 -> 1; matrix products, arithmetic and copies ran while one was open for 12% -> 1% of each run, Pallas kernels for 27% -> 32%
where the time goes in v4:
time: 50.4 us; the launch traced here: 50.2 us
  Pallas kernels  30.4 us (60%)
  starting transfers between devices  16.7 us (33%)
  local copies, waits for them, and re-layouts  1.29 us (3%)
  waiting for transfers between devices  1.17 us (2%)
  other arithmetic  0.53 us (1%)
    pallas_call x3, Pallas kernels, first_block(): pl.pallas_call(functools.partial(first_kernel, parts, which), out_shape=t...  15.1 us
    pallas_call x1, Pallas kernels, second_block(): pl.pallas_call(second_kernel, out_shape=jax.ShapeDtypeStruct((2, 4, 32, 1...  11.6 us
    ppermute x5, starting transfers between devices, swap(): return lax.ppermute(block, 'lat', pairs)  9.82 us
    ppermute x2, starting transfers between devices, around(): lax.ppermute(block, 'lon', [(i, (i + distance) % count) for i in range(co...  6.85 us
    pallas_call x1, Pallas kernels, patches(): pl.pallas_call(patch_kernel, out_shape=tuple((jax.ShapeDtypeStruct((n, 96...  2.59 us
    ppermute x5, waiting for transfers between devices, swap(): return lax.ppermute(block, 'lat', pairs)  1.17 us
    unnamed x18, local copies, waits for them, and re-layouts  1.04 us
  transfers between devices with their start and end apart: 7, of which 1 were waited for; matrix products, arithmetic and copies ran while one was open for 1% of the time, Pallas kernels for 32%

profile of v4, /device:TPU:25, one launch (start us, length us, event | category | flops | bytes accessed | tf_op | source)
XLA Modules:
  0.0 50.2 jit_solution(14738715021744755791)
XLA Ops:
  0.0 0.1 pad_add_fusion.par_ref.refs_0_
  0.1 0.0 copy-start.8
  0.1 0.0 copy-start.7
  0.1 2.6 %shard_map.118 = (bf16[8,96,128]{2,1,0:T(8,128)(2,1)S(1)}, bf16[8,96,128]{2,1,0:T(8,128)(2,1)S(1)}, bf16[1,96,128]{2,1,0:T(8,128)(2,1)S(1)}, bf16[1,96,128]{2,1,0:T(8,128)(2,1)S(1)}) custom-call(s32[2]{0:T(128)S(1)} %pad_add_fusion.par_ref.refs_0_, bf16[2,5,32,256]{3,2,1,0:T(8,128)(2,1)} %atmos_any.1, bf16[32,256]{1,0:T(8,128)(2,1)} %oro_any.1, ...), custom_call_target="tpu_custom_call" | custom-call | flops 1000000000 | bytes 1000000 | tf_op jit(solution)/shard_map/pallas_call | solution.py:87
  2.7 0.8 %collective-permute-start = (bf16[1,96,128]{2,1,0:T(8,128)(2,1)S(1)}, bf16[1,96,128]{2,1,0:T(8,128)(2,1)S(1)}, u32[]{:S(2)}, u32[]{:S(2)}) collective-permute-start(bf16[1,96,128]{2,1,0:T(8,128)(2,1)S(1)} %get-tuple-element.17), channel_id=1, source_target_pairs={{0,16},{16,0},{32,48},{48,32},{64,80},{80,64},{96,112},{112,96},{1... | collective-permute-start | bytes 73736 | tf_op jit(solution)/shard_map/ppermute | solution.py:468
  3.4 4.5 %collective-permute-start.1 = (bf16[1,96,128]{2,1,0:T(8,128)(2,1)S(1)}, bf16[1,96,128]{2,1,0:T(8,128)(2,1)S(1)}, u32[]{:S(2)}, u32[]{:S(2)}) collective-permute-start(bf16[1,96,128]{2,1,0:T(8,128)(2,1)S(1)} %get-tuple-element.19), channel_id=1, source_target_pairs={{16,32},{32,16},{48,64},{64,48},{80,96},{96,80},{112,128},{128,112... | collective-permute-start | bytes 73736 | tf_op jit(solution)/shard_map/ppermute | solution.py:468
  8.0 0.0 copy-done.8
  8.0 0.0 copy-done.7
  8.1 0.2 pad.4
  8.3 0.0 copy-start.3
  8.3 0.4 fusion
  8.8 0.0 collective-permute-done.edge_ref.after_ref
  8.8 2.5 %collective-permute-start.2 = (bf16[8,96,128]{2,1,0:T(8,128)(2,1)S(1)}, bf16[8,96,128]{2,1,0:T(8,128)(2,1)S(1)}, u32[]{:S(2)}, u32[]{:S(2)}) collective-permute-start(bf16[8,96,128]{2,1,0:T(8,128)(2,1)S(1)} %constant_dynamic-update-slice_fusion), channel_id=1, source_target_pairs={{16,32},{32,16},{48,64},{64,48},{80,96},{96,80},{112,128},{128,112... | collective-permute-start | bytes 589832 | tf_op jit(solution)/shard_map/ppermute | solution.py:468
  11.3 0.0 collective-permute-done.1.near_ref
  11.3 0.0 copy-start.1
  11.3 0.0 copy-start.2
  11.3 0.0 copy-start.5
  11.3 0.0 copy-start.6
  11.4 0.8 %shard_map.119.refs_1_.own_ref = bf16[2,10,64,128]{3,2,1,0:T(8,128)(2,1)S(1)} custom-call(s32[2]{0:T(128)S(1)} %pad_add_fusion.par_ref.refs_0_, bf16[8,96,128]{2,1,0:T(8,128)(2,1)S(1)} %get-tuple-element.18.own_ref, bf16[1,96,128]{2,1,0:T(8,128)(2,1)S(1)} %collective-permute-done.edge_ref.after_ref, bf16[1,96,128]{2,1,0:T(8,128)(2,1)S(1)} %collective-permute-done.1.near_ref), custom_call_target="tpu_custom_call" | custom-call | flops 1000000000 | bytes 1000000 | tf_op jit(solution)/shard_map/pallas_call | solution.py:130
  12.2 0.0 copy-done.3
  12.2 0.7 %copy-done.1 = bf16[2,512,1024]{2,1,0:T(8,128)(2,1)S(1)} copy-done((bf16[2,512,1024]{2,1,0:T(8,128)(2,1)S(1)}, bf16[2,512,1024]{2,1,0:T(8,128)(2,1)}, u32[]{:S(2)}) %copy-start.1) | copy-done | bytes 2097176
  12.9 0.3 copy-done.2
  13.2 0.0 copy-done.5
  13.2 0.0 copy-done.6
  13.2 4.8 %shard_map.120 = (f32[2,8,48,512]{3,2,1,0:T(8,128)S(1)}, bf16[2,4,48,512]{3,2,1,0:T(8,128)(2,1)S(1)}) custom-call(bf16[1,96,128]{2,1,0:T(8,128)(2,1)S(1)} %collective-permute-done.edge_ref.after_ref, s32[2]{0:T(128)S(1)} %pad_add_fusion.par_ref.refs_0_, bf16[2,10,64,128]{3,2,1,0:T(8,128)(2,1)S(1)} %shard_map.119.refs_1_.own_ref, ...), custom_call_target="tpu_custom_call" | custom-call | flops 10000000000 | bytes 10000000 | tf_op jit(solution)/shard_map/pallas_call | solution.py:311
  17.9 1.0 %collective-permute-start.5 = (bf16[2,4,48,512]{3,2,1,0:T(8,128)(2,1)S(1)}, bf16[2,4,48,512]{3,2,1,0:T(8,128)(2,1)S(1)}, u32[]{:S(2)}, u32[]{:S(2)}) collective-permute-start(bf16[2,4,48,512]{3,2,1,0:T(8,128)(2,1)S(1)} %get-tuple-element.27), channel_id=1, source_target_pairs={{0,16},{16,0},{32,48},{48,32},{64,80},{80,64},{96,112},{112,96},{1... | collective-permute-start | bytes 1179656 | tf_op jit(solution)/shard_map/ppermute | solution.py:468
  19.0 0.0 collective-permute-done.2.packed_ref
  19.0 0.3 shard_map.121
  19.2 1.7 %collective-permute-start.3 = (bf16[2,18,16,128]{3,2,1,0:T(8,128)(2,1)S(1)}, bf16[2,18,16,128]{3,2,1,0:T(8,128)(2,1)S(1)}, u32[]{:S(2)}, u32[]{:S(2)}) collective-permute-start(bf16[2,18,16,128]{3,2,1,0:T(8,128)(2,1)S(1)} %get-tuple-element.23), channel_id=1, source_target_pairs={{0,1},{1,2},{2,3},{3,4},{4,5},{5,6},{6,7},{7,8},{8,9},{9,10},{10,1... | collective-permute-start | bytes 442376 | tf_op jit(solution)/shard_map/ppermute | solution.py:473
  20.9 5.1 %collective-permute-start.4 = (bf16[2,18,16,128]{3,2,1,0:T(8,128)(2,1)S(1)}, bf16[2,18,16,128]{3,2,1,0:T(8,128)(2,1)S(1)}, u32[]{:S(2)}, u32[]{:S(2)}) collective-permute-start(bf16[2,18,16,128]{3,2,1,0:T(8,128)(2,1)S(1)} %get-tuple-element.24), channel_id=1, source_target_pairs={{0,15},{1,0},{2,1},{3,2},{4,3},{5,4},{6,5},{7,6},{8,7},{9,8},{10,9... | collective-permute-start | bytes 442376 | tf_op jit(solution)/shard_map/ppermute | solution.py:473
  26.1 4.4 %shard_map.122.after_ref.outer_mid = f32[2,4,48,512]{3,2,1,0:T(8,128)S(1)} custom-call(f32[2,8,48,512]{3,2,1,0:T(8,128)S(1)} %get-tuple-element.20.after_ref.own_mid, s32[2]{0:T(128)S(1)} %pad_add_fusion.par_ref.refs_0_, bf16[2,10,64,128]{3,2,1,0:T(8,128)(2,1)S(1)} %shard_map.119.refs_1_.own_ref, bf16[2,8,64,128]{3,2,1,0:T(8,128)(2,1)S(1)} %get-tuple-element.22.refs_2_, ...), custom_call_target="tpu_custom_call" | custom-call | flops 10000000000 | bytes 10000000 | tf_op jit(solution)/shard_map/pallas_call | solution.py:311
  30.5 0.0 copy-start
  30.5 0.0 copy-start.4
  30.5 0.0 collective-permute-done.3.refs_3_
  30.5 0.0 collective-permute-done.4.refs_4_
  30.5 5.9 %shard_map.123 = (f32[2,8,32,512]{3,2,1,0:T(8,128)S(1)}, f32[2,4,32,512]{3,2,1,0:T(8,128)S(1)}, bf16[2,4,32,512]{3,2,1,0:T(8,128)(2,1)S(1)}) custom-call(f32[2,4,48,512]{3,2,1,0:T(8,128)S(1)} %shard_map.122.after_ref.outer_mid, s32[2]{0:T(128)S(1)} %pad_add_fusion.par_ref.refs_0_, bf16[2,10,64,128]{3,2,1,0:T(8,128)(2,1)S(1)} %shard_map.119.refs_1_.own_ref, ...), custom_call_target="tpu_custom_call" | custom-call | flops 10000000000 | bytes 10000000 | tf_op jit(solution)/shard_map/pallas_call | solution.py:311
  36.5 1.0 %collective-permute-start.6 = (bf16[2,4,32,512]{3,2,1,0:T(8,128)(2,1)S(1)}, bf16[2,4,32,512]{3,2,1,0:T(8,128)(2,1)S(1)}, u32[]{:S(2)}, u32[]{:S(2)}) collective-permute-start(bf16[2,4,32,512]{3,2,1,0:T(8,128)(2,1)S(1)} %get-tuple-element.28), channel_id=1, source_target_pairs={{0,16},{16,0},{32,48},{48,32},{64,80},{80,64},{96,112},{112,96},{1... | collective-permute-start | bytes 786440 | tf_op jit(solution)/shard_map/ppermute | solution.py:468
  37.4 0.0 collective-permute-done.5.near_mid_ref
  37.4 1.2 %collective-permute-done.6.near_edge_ref = bf16[2,4,32,512]{3,2,1,0:T(8,128)(2,1)S(1)} collective-permute-done((bf16[2,4,32,512]{3,2,1,0:T(8,128)(2,1)S(1)}, bf16[2,4,32,512]{3,2,1,0:T(8,128)(2,1)S(1)}, u32[]{:S(2)}, u32[]{:S(2)}) %collective-permute-start.6) | collective-permute-done | bytes 262176 | tf_op jit(solution)/shard_map/ppermute | solution.py:468
  38.6 0.0 copy-done
  38.6 0.0 copy-done.4
  38.6 11.6 %shard_map.124 = bf16[2,4,32,1024]{3,2,1,0:T(8,128)(2,1)} custom-call(s32[2]{0:T(128)S(1)} %pad_add_fusion.par_ref.refs_0_, f32[2,8,48,512]{3,2,1,0:T(8,128)S(1)} %get-tuple-element.20.after_ref.own_mid, f32[2,4,48,512]{3,2,1,0:T(8,128)S(1)} %shard_map.122.after_ref.outer_mid, f32[2,8,32,512]{3,2,1,0:T(8,128)S(1)} %get-tuple-element.25.own_edge, ...), custom_call_target="tpu_custom_call" | custom-call | flops 10000000000 | bytes 10000000 | tf_op jit(solution)/shard_map/pallas_call | solution.py:431
  (4 shorter events, 0.0 us)
Async XLA Ops:
  0.1 7.9 %copy-start.8 = (f32[512]{0:T(512)S(1)}, f32[512]{0:T(512)}, u32[]{:S(2)}) copy-start(f32[512]{0:T(512)} %param.17) | copy-start | bytes 6148
  0.1 8.0 %copy-start.7 = (bf16[12,12,6,512]{3,2,1,0:T(8,128)(2,1)S(1)}, bf16[12,12,6,512]{3,2,1,0:T(8,128)(2,1)}, u32[]{:S(2)}) copy-start(bf16[12,12,6,512]{3,2,1,0:T(8,128)(2,1)} %param.15) | copy-start | bytes 2654212
  2.7 6.1 %collective-permute-start = (bf16[1,96,128]{2,1,0:T(8,128)(2,1)S(1)}, bf16[1,96,128]{2,1,0:T(8,128)(2,1)S(1)}, u32[]{:S(2)}, u32[]{:S(2)}) collective-permute-start(bf16[1,96,128]{2,1,0:T(8,128)(2,1)S(1)} %get-tuple-element.17), channel_id=1, source_target_pairs={{0,16},{16,0},{32,48},{48,32},{64,80},{80,64},{96,112},{112,96},{1... | collective-permute-start | bytes 73736 | tf_op jit(solution)/shard_map/ppermute | solution.py:468
  3.4 7.9 %collective-permute-start.1 = (bf16[1,96,128]{2,1,0:T(8,128)(2,1)S(1)}, bf16[1,96,128]{2,1,0:T(8,128)(2,1)S(1)}, u32[]{:S(2)}, u32[]{:S(2)}) collective-permute-start(bf16[1,96,128]{2,1,0:T(8,128)(2,1)S(1)} %get-tuple-element.19), channel_id=1, source_target_pairs={{16,32},{32,16},{48,64},{64,48},{80,96},{96,80},{112,128},{128,112... | collective-permute-start | bytes 73736 | tf_op jit(solution)/shard_map/ppermute | solution.py:468
  8.3 3.9 %copy-start.3 = (bf16[2,512,512]{2,1,0:T(8,128)(2,1)S(1)}, bf16[2,512,512]{2,1,0:T(8,128)(2,1)}, u32[]{:S(2)}) copy-start(bf16[2,512,512]{2,1,0:T(8,128)(2,1)} %wo_ref.1) | copy-start | bytes 3145732
  8.8 10.2 %collective-permute-start.2 = (bf16[8,96,128]{2,1,0:T(8,128)(2,1)S(1)}, bf16[8,96,128]{2,1,0:T(8,128)(2,1)S(1)}, u32[]{:S(2)}, u32[]{:S(2)}) collective-permute-start(bf16[8,96,128]{2,1,0:T(8,128)(2,1)S(1)} %constant_dynamic-update-slice_fusion), channel_id=1, source_target_pairs={{16,32},{32,16},{48,64},{64,48},{80,96},{96,80},{112,128},{128,112... | collective-permute-start | bytes 589832 | tf_op jit(solution)/shard_map/ppermute | solution.py:468
  11.3 1.6 %copy-start.1 = (bf16[2,512,1024]{2,1,0:T(8,128)(2,1)S(1)}, bf16[2,512,1024]{2,1,0:T(8,128)(2,1)}, u32[]{:S(2)}) copy-start(bf16[2,512,1024]{2,1,0:T(8,128)(2,1)} %wkv_ref.1) | copy-start | bytes 6291460
  11.3 1.8 %copy-start.2 = (bf16[2,512,512]{2,1,0:T(8,128)(2,1)S(1)}, bf16[2,512,512]{2,1,0:T(8,128)(2,1)}, u32[]{:S(2)}) copy-start(bf16[2,512,512]{2,1,0:T(8,128)(2,1)} %wq_ref.1) | copy-start | bytes 3145732
  11.3 1.8 %copy-start.5 = (f32[2,512]{1,0:T(2,128)S(1)}, f32[2,512]{1,0:T(2,128)}, u32[]{:S(2)}) copy-start(f32[2,512]{1,0:T(2,128)} %refs_6_.5) | copy-start | bytes 12292
  11.3 1.8 %copy-start.6 = (f32[2,512]{1,0:T(2,128)S(1)}, f32[2,512]{1,0:T(2,128)}, u32[]{:S(2)}) copy-start(f32[2,512]{1,0:T(2,128)} %gain_ref.1) | copy-start | bytes 12292
  17.9 19.5 %collective-permute-start.5 = (bf16[2,4,48,512]{3,2,1,0:T(8,128)(2,1)S(1)}, bf16[2,4,48,512]{3,2,1,0:T(8,128)(2,1)S(1)}, u32[]{:S(2)}, u32[]{:S(2)}) collective-permute-start(bf16[2,4,48,512]{3,2,1,0:T(8,128)(2,1)S(1)} %get-tuple-element.27), channel_id=1, source_target_pairs={{0,16},{16,0},{32,48},{48,32},{64,80},{80,64},{96,112},{112,96},{1... | collective-permute-start | bytes 1179656 | tf_op jit(solution)/shard_map/ppermute | solution.py:468
  19.2 11.3 %collective-permute-start.3 = (bf16[2,18,16,128]{3,2,1,0:T(8,128)(2,1)S(1)}, bf16[2,18,16,128]{3,2,1,0:T(8,128)(2,1)S(1)}, u32[]{:S(2)}, u32[]{:S(2)}) collective-permute-start(bf16[2,18,16,128]{3,2,1,0:T(8,128)(2,1)S(1)} %get-tuple-element.23), channel_id=1, source_target_pairs={{0,1},{1,2},{2,3},{3,4},{4,5},{5,6},{6,7},{7,8},{8,9},{9,10},{10,1... | collective-permute-start | bytes 442376 | tf_op jit(solution)/shard_map/ppermute | solution.py:473
  20.9 9.6 %collective-permute-start.4 = (bf16[2,18,16,128]{3,2,1,0:T(8,128)(2,1)S(1)}, bf16[2,18,16,128]{3,2,1,0:T(8,128)(2,1)S(1)}, u32[]{:S(2)}, u32[]{:S(2)}) collective-permute-start(bf16[2,18,16,128]{3,2,1,0:T(8,128)(2,1)S(1)} %get-tuple-element.24), channel_id=1, source_target_pairs={{0,15},{1,0},{2,1},{3,2},{4,3},{5,4},{6,5},{7,6},{8,7},{9,8},{10,9... | collective-permute-start | bytes 442376 | tf_op jit(solution)/shard_map/ppermute | solution.py:473
  30.5 8.1 %copy-start = (bf16[2048,1024]{1,0:T(8,128)(2,1)S(1)}, bf16[2048,1024]{1,0:T(8,128)(2,1)}, u32[]{:S(2)}) copy-start(bf16[2048,1024]{1,0:T(8,128)(2,1)} %wm_ref.1) | copy-start | bytes 12582916
  30.5 8.1 %copy-start.4 = (f32[2048]{0:T(1024)S(1)}, f32[2048]{0:T(1024)}, u32[]{:S(2)}) copy-start(f32[2048]{0:T(1024)} %param.22) | copy-start | bytes 24580
  36.5 2.2 %collective-permute-start.6 = (bf16[2,4,32,512]{3,2,1,0:T(8,128)(2,1)S(1)}, bf16[2,4,32,512]{3,2,1,0:T(8,128)(2,1)S(1)}, u32[]{:S(2)}, u32[]{:S(2)}) collective-permute-start(bf16[2,4,32,512]{3,2,1,0:T(8,128)(2,1)S(1)} %get-tuple-element.28), channel_id=1, source_target_pairs={{0,16},{16,0},{32,48},{48,32},{64,80},{80,64},{96,112},{112,96},{1... | collective-permute-start | bytes 786440 | tf_op jit(solution)/shard_map/ppermute | solution.py:468

commit v5 on v4

--- a/solution.py
+++ b/solution.py
@@ -117,27 +117,6 @@
             out_ref[level, :, half * 32 : half * 32 + 32, :] = tile
 
 
-def unpack_own_kernel(par_ref, own_ref, edge_ref, near_ref, full_ref, packed):
-    par = par_ref[0]
-    packed[1:9] = own_ref[...]
-    packed[pl.ds(9 * par, 1)] = near_ref[...]
-    packed[pl.ds(9 * (1 - par), 1)] = edge_ref[...]
-    unpack_rows(packed, full_ref)
-
-
-def unpack_own(par, own, edge, near):
-    vmem = pl.BlockSpec(memory_space=pltpu.VMEM)
-    return pl.pallas_call(
-        unpack_own_kernel,
-        out_shape=jax.ShapeDtypeStruct((2, 10, 64, 128), BF),
-        in_specs=[pl.BlockSpec(memory_space=pltpu.SMEM)] + [vmem] * 3,
-        out_specs=vmem,
-        scratch_shapes=[pltpu.VMEM((10, 96, 128), BF)],
-        compiler_params=params(),
-        cost_estimate=pl.CostEstimate(flops=10**9, bytes_accessed=10**6, transcendentals=0),
-    )(par, own, edge, near)
-
-
 def unpack_far_kernel(after_ref, packed_ref, own_ref, far_ref, low_ref, high_ref):
     del after_ref
     unpack_rows(packed_ref, far_ref)
@@ -210,7 +189,12 @@
 
 def first_kernel(parts, which, after_ref, *refs):
     del after_ref
-    par_ref, own_ref, refs = refs[0], refs[1], refs[2:]
+    par_ref, refs = refs[0], refs[1:]
+    leading = parts == (0,) and which == MIDDLE
+    if leading:
+        own_packed, edge_ref, near_ref, refs = refs[0], refs[1], refs[2], refs[3:]
+    else:
+        own_ref, refs = refs[0], refs[1:]
     if 1 in parts:
         far_ref, refs = refs[0], refs[1:]
     if which == EDGES:
@@ -219,8 +203,24 @@
     x1_refs, refs = refs[: len(parts)], refs[len(parts) :]
     if 0 in parts:
         send_ref, refs = refs[0], refs[1:]
-    wide, gathered, x0, normed, query, keyval, heads = refs
+    if leading:
+        own_ref, refs = refs[0], refs[1:]
+    wide, gathered, x0, normed, query, keyval, heads, *refs = refs
     par = par_ref[0]
+    if leading:
+        packed, wq, wkv, wo, sems = refs
+        loads = [
+            pltpu.make_async_copy(src.at[0], dst, sems.at[n])
+            for n, (src, dst) in enumerate([(wkv_ref, wkv), (wq_ref, wq), (wo_ref, wo)])
+        ]
+        for load in loads:
+            load.start()
+        packed[1:9] = own_packed[...]
+        packed[pl.ds(9 * par, 1)] = near_ref[...]
+        packed[pl.ds(9 * (1 - par), 1)] = edge_ref[...]
+        unpack_rows(packed, own_ref)
+    else:
+        wq, wkv, wo = wq_ref.at[0], wkv_ref.at[0], wo_ref.at[0]
 
     def spread(part, to, count, center, low, high):
         rows = (slice(None), pl.ds(to, count))
@@ -242,52 +242,64 @@
     gain = gain_ref[0:1, :]
     half = 1 - par
 
-    def embed(group):
-        part, g = group
-        slot = groups.index(group)
-        for dj in range(3):
-            cols = slice(g * 16 + 7 + dj, g * 16 + 23 + dj)
-            got = wide[part, :, :, cols, :].astype(BF)
-            gathered[slot, :, :, :, dj * 128 : dj * 128 + 128] = got
-        for level in range(2):
+    cols_of = len(which)
+
+    def slots(part):
+        at = parts.index(part) * cols_of
+        return at, slice(at, at + cols_of)
+
+    def embed(part):
+        first, here = slots(part)
+        for n, g in enumerate(which):
+            for dj in range(3):
+                cols = slice(g * 16 + 7 + dj, g * 16 + 23 + dj)
+                got = wide[part, :, :, cols, :].astype(BF)
+                gathered[first + n, :, :, :, dj * 128 : dj * 128 + 128] = got
+        for n in range(cols_of):
             lhs = jnp.concatenate(
-                [gathered[slot, level, di : di + 8].reshape(128, 384) for di in range(3)], axis=1
+                [gathered[first + n, :, di : di + 8].reshape(256, 384) for di in range(3)], axis=1
             )
-            x = mm(lhs, wemb_ref[...]) + lev_ref[level : level + 1, :]
-            x0[slot, level] = x.reshape(8, 16, D)
-
-    def norm(group):
-        slot = groups.index(group)
-        for u in range(2):
-            x = x0[slot, :, :, u * 8 : u * 8 + 8, :].reshape(128, D)
-            normed[slot, u] = normalize(x, gain).astype(BF).reshape(2, 4, 16, D)
-
-    def project(group):
-        slot = groups.index(group)
-        n = normed[slot].reshape(256, D)
-        keyval[slot] = mm(n, wkv_ref[0]).astype(BF).reshape(2, 128, 1024)
-        if group[0]:
-            n = normed[slot, :, :, pl.ds(half * 2, 2)].reshape(128, D)
-        q = (mm(n, wq_ref[0]) * SCALE).astype(BF)
-        query[slot, :, : q.shape[0] // 2] = q.reshape(2, -1, D)
-
-    def attention(group):
-        slot = groups.index(group)
-        count = 64 if group[0] else 128
-        for u in range(2):
-            kv = keyval[slot, u]
-            heads[slot, u, :count] = attend(query[slot, u, :count], kv[:, :D], kv[:, D:], None)
-
-    def project_out(group):
-        part, g = group
-        slot = groups.index(group)
+            x = mm(lhs, wemb_ref[...]).reshape(2, 8, 16, D)
+            for level in range(2):
+                x0[first + n, level] = x[level] + lev_ref[level : level + 1, :]
+
+    def norm(part):
+        first, here = slots(part)
+        for slot in range(first, first + cols_of):
+            for u in range(2):
+                x = x0[slot, :, :, u * 8 : u * 8 + 8, :].reshape(128, D)
+                normed[slot, u] = normalize(x, gain).astype(BF).reshape(2, 4, 16, D)
+
+    def project(part):
+        first, here = slots(part)
+        n = normed[here].reshape(256 * cols_of, D)
+        if leading:
+            loads[0].wait()
+            loads[1].wait()
+        keyval[here] = mm(n, wkv[...]).astype(BF).reshape(cols_of, 2, 128, 1024)
+        if part:
+            n = normed[here, :, :, pl.ds(half * 2, 2)].reshape(128 * cols_of, D)
+        q = (mm(n, wq[...]) * SCALE).astype(BF)
+        query[here, :, : 64 if part else 128] = q.reshape(cols_of, 2, -1, D)
+
+    def attention(part):
+        first, here = slots(part)
         count = 64 if part else 128
-        out = mm(heads[slot, :, :count].reshape(2 * count, D), wo_ref[0])
-        for u in range(2):
-            at = which.index(g) * 16 + u * 8
-            cols = slice(at, at + 8)
-            mine = slice(u * 8, u * 8 + 8)
-            add = out[u * count : u * count + count].reshape(2, count // 16, 8, D)
+        for slot in range(first, first + cols_of):
+            for u in range(2):
+                kv = keyval[slot, u]
+                heads[slot, u, :count] = attend(query[slot, u, :count], kv[:, :D], kv[:, D:], None)
+
+    def project_out(part):
+        first, here = slots(part)
+        count = 64 if part else 128
+        if leading:
+            loads[2].wait()
+        out = mm(heads[here, :, :count].reshape(2 * cols_of * count, D), wo[...])
+        for n in range(2 * cols_of):
+            slot, u = first + n // 2, n % 2
+            cols, mine = slice(n * 8, n * 8 + 8), slice(u * 8, u * 8 + 8)
+            add = out[n * count : n * count + count].reshape(2, count // 16, 8, D)
             if part:
                 x1_refs[-1][:, :, cols, :] = x0[slot, :, pl.ds(4 * half, 4), mine, :] + add
             else:
@@ -296,8 +308,7 @@
                     rows = slice(4 * h, 4 * h + 4)
                     x1_refs[0][:, to, cols, :] = x0[slot, :, rows, mine, :] + add[:, rows]
 
-    groups = [(part, g) for part in parts for g in which]
-    pipelined([embed, norm, project, attention, project_out], groups)
+    pipelined([embed, norm, project, attention, project_out], list(parts))
     if 0 in parts:
         send_ref[...] = x1_refs[0][:, 4:8].astype(BF)
 
@@ -305,27 +316,43 @@
 def first_block(parts, which, after, par, patch_arrays, wemb, level_embed, norm_gain, w_query, w_keyval, w_out):
     vmem = pl.BlockSpec(memory_space=pltpu.VMEM)
     width, count = 16 * len(which), len(parts) * len(which)
+    leading = parts == (0,) and which == MIDDLE
     outs = [jax.ShapeDtypeStruct((2, 4 if part else 8, width, D), F32) for part in parts]
     if 0 in parts:
         outs.append(jax.ShapeDtypeStruct((2, 4, width, D), BF))
+    scratch = [
+        pltpu.VMEM((2, 2, 10, 96, 128), F32),
+        pltpu.VMEM((count, 2, 10, 16, 384), BF),
+        pltpu.VMEM((count, 2, 8, 16, D), F32),
+        pltpu.VMEM((count, 2, 2, 4, 16, D), BF),
+        pltpu.VMEM((count, 2, 128, D), BF),
+        pltpu.VMEM((count, 2, 128, 1024), BF),
+        pltpu.VMEM((count, 2, 128, D), BF),
+    ]
+    projections = [w_query, w_keyval, w_out]
+    if leading:
+        outs.append(jax.ShapeDtypeStruct((2, 10, 64, 128), BF))
+        scratch += [
+            pltpu.VMEM((10, 96, 128), BF),
+            pltpu.VMEM((D, D), BF),
+            pltpu.VMEM((D, 1024), BF),
+            pltpu.VMEM((D, D), BF),
+            pltpu.SemaphoreType.DMA((3,)),
+        ]
+        projections = [pltpu.with_memory_space_constraint(w, pltpu.HBM) for w in projections]
+    else:
+        projections = [pltpu.with_memory_space_constraint(w, pltpu.VMEM) for w in projections]
+    place_of = pl.BlockSpec(memory_space=pltpu.HBM if leading else pltpu.VMEM)
     return pl.pallas_call(
         functools.partial(first_kernel, parts, which),
         out_shape=tuple(outs),
         in_specs=[pl.BlockSpec(memory_space=pl.ANY), pl.BlockSpec(memory_space=pltpu.SMEM)]
-        + [vmem] * (6 + len(patch_arrays)),
+        + [vmem] * (3 + len(patch_arrays)) + [place_of] * 3,
         out_specs=(vmem,) * len(outs),
-        scratch_shapes=[
-            pltpu.VMEM((2, 2, 10, 96, 128), F32),
-            pltpu.VMEM((count, 2, 10, 16, 384), BF),
-            pltpu.VMEM((count, 2, 8, 16, D), F32),
-            pltpu.VMEM((count, 2, 2, 4, 16, D), BF),
-            pltpu.VMEM((count, 2, 128, D), BF),
-            pltpu.VMEM((count, 2, 128, 1024), BF),
-            pltpu.VMEM((count, 2, 128, D), BF),
-        ],
+        scratch_shapes=scratch,
         compiler_params=params(),
         cost_estimate=pl.CostEstimate(flops=10**10, bytes_accessed=10**7, transcendentals=0),
-    )(after, par, *patch_arrays, wemb, level_embed, norm_gain, w_query, w_keyval, w_out)
+    )(after, par, *patch_arrays, wemb, level_embed, norm_gain, *projections)
 
 
 SHIFTED = WINS - 1
@@ -360,9 +387,8 @@
     def window(w, first, last):
         return jnp.where(upper, block(w, first, last), block(w + 1, first, last))
 
-    def norm(group):
-        s, g = group
-        for w in range(g * 3, g * 3 + 3):
+    def norm(s):
+        for w in range(SHIFTED):
             if s == 0:
                 x = window(w, 0, 8)
             else:
@@ -372,38 +398,31 @@
             n = normalize(x.reshape(128, D), gain).astype(BF)
             normed[s * SHIFTED + w] = n.reshape(2, 4, 16, D)
 
-    def project(group):
-        s, g = group
-        at = slice(s * SHIFTED + g * 3, s * SHIFTED + g * 3 + 3)
-        n = normed[at].reshape(384, D)
-        keyval[at] = mm(n, wkv_ref[1]).astype(BF).reshape(3, 128, 1024)
-        n = normed[at, :, 2 - 2 * s : 4 - 2 * s].reshape(192, D)
-        query[at] = (mm(n, wq_ref[1]) * SCALE).astype(BF).reshape(3, 64, D)
-
-    def attention(group):
-        s, g = group
-        for t in range(s * SHIFTED + g * 3, s * SHIFTED + g * 3 + 3):
+    def project(s):
+        at = slice(s * SHIFTED, s * SHIFTED + SHIFTED)
+        n = normed[at].reshape(SHIFTED * 128, D)
+        keyval[at] = mm(n, wkv_ref[1]).astype(BF).reshape(SHIFTED, 128, 1024)
+        n = normed[at, :, 2 - 2 * s : 4 - 2 * s].reshape(SHIFTED * 64, D)
+        query[at] = (mm(n, wq_ref[1]) * SCALE).astype(BF).reshape(SHIFTED, 64, D)
+
+    def attention(s):
+        for t in range(s * SHIFTED, s * SHIFTED + SHIFTED):
             kv = keyval[t]
             heads[t] = attend(query[t], kv[:, :D], kv[:, D:], None if s else bias)
 
-    def project_out(group):
-        s, g = group
-        at = slice(s * SHIFTED + g * 3, s * SHIFTED + g * 3 + 3)
-        out = mm(heads[at].reshape(192, D), wo_ref[1])
+    def project_out(s):
+        at = slice(s * SHIFTED, s * SHIFTED + SHIFTED)
+        out = mm(heads[at].reshape(SHIFTED * 64, D), wo_ref[1])
         rows = slice(s * 4, s * 4 + 4)
-        for u in range(3):
-            w = g * 3 + u
+        for w in range(SHIFTED):
             new = window(w, 4 + s * 4, 8 + s * 4)
-            new = new + out[u * 64 : u * 64 + 64].reshape(2, 4, 8, D)
+            new = new + out[w * 64 : w * 64 + 64].reshape(2, 4, 8, D)
             for c in range(4):
                 piece = new[..., c * 128 : c * 128 + 128]
                 x2[c, :, rows, w * 8 + 4 : w * 8 + 8, :] = piece[:, :, 4:8, :]
                 x2[c, :, rows, w * 8 + 8 : w * 8 + 12, :] = piece[:, :, 0:4, :]
 
-    def merge(group):
-        s, g = group
-        if g < 2:
-            return
+    def merge(s):
         parts = []
         for p in range(4):
             got = [
@@ -422,12 +441,14 @@
         out = mm(n, wm_ref[...]).astype(BF)
         out_ref[:, pl.ds(2 * ((par + s) % 2), 2)] = out.reshape(2, 2, 32, 1024)
 
-    groups = [(s, g) for s in range(2) for g in range(3)]
-    pipelined([norm, project, attention, project_out, merge], groups)
+    pipelined([norm, project, attention, project_out, merge], [0, 1])
 
 
 def second_block(par, x1_parts, near_mid, near_edge, norm_gain, merge_gain, w_query, w_keyval, w_out, merge_weight):
     vmem = pl.BlockSpec(memory_space=pltpu.VMEM)
+    weights = [
+        pltpu.with_memory_space_constraint(w, pltpu.VMEM) for w in (w_query, w_keyval, w_out, merge_weight)
+    ]
     return pl.pallas_call(
         second_kernel,
         out_shape=jax.ShapeDtypeStruct((2, 4, 32, 1024), BF),
@@ -444,7 +465,7 @@
         compiler_params=params(),
         cost_estimate=pl.CostEstimate(flops=10**10, bytes_accessed=10**7, transcendentals=0),
     )(
-        par, *x1_parts, near_mid, near_edge, norm_gain, merge_gain, w_query, w_keyval, w_out, merge_weight
+        par, *x1_parts, near_mid, near_edge, norm_gain, merge_gain, *weights
     )
 
 
@@ -477,9 +498,6 @@
     atmos, orography, land_sea, embed_weight, level_embed, land_embed, norm_gain,
     w_query, w_keyval, w_out, merge_gain, merge_weight,
 ):
-    w_query, w_keyval, w_out, merge_weight = [
-        pltpu.with_memory_space_constraint(w, pltpu.VMEM) for w in (w_query, w_keyval, w_out, merge_weight)
-    ]
     lat = lax.axis_index("lat")
     par = lat % 2
     pole = (lat == 0) | (lat == lax.axis_size("lat") - 1)
@@ -491,16 +509,18 @@
     far = swap(send, 1)
     wemb = embedding_matrix(embed_weight, land_embed)
     weights = wemb, level_embed, norm_gain, w_query, w_keyval, w_out
-    own = unpack_own(place, own, edge, near)
-    own_mid, send_mid = first_block((0,), MIDDLE, edge, place, (own,), *weights)
+    own_mid, send_mid, own = first_block((0,), MIDDLE, edge, place, (own, edge, near), *weights)
     near_mid = swap(send_mid, 0)
     far, low, high = unpack_far(own_mid, far, own)
     from_low, from_high = around(high, 1), around(low, -1)
     (outer_mid,) = first_block((1,), MIDDLE, own_mid, place, (own, far), *weights)
-    own_edge, outer_edge, send_edge = first_block(
-        (0, 1), EDGES, outer_mid, place, (own, far, from_low, from_high), *weights
+    own_edge, send_edge = first_block(
+        (0,), EDGES, outer_mid, place, (own, from_low, from_high), *weights
     )
     near_edge = swap(send_edge, 0)
+    (outer_edge,) = first_block(
+        (1,), EDGES, own_edge, place, (own, far, from_low, from_high), *weights
+    )
     return second_block(
         place, (own_mid, outer_mid, own_edge, outer_edge), near_mid, near_edge, norm_gain,
         merge_gain.reshape(1, -1), w_query, w_keyval, w_out, merge_weight,

time: 50.4 us -> 49.7 us (0.986)
  starting transfers between devices: 16.7 us -> 18 us
  waiting for transfers between devices: 1.17 us -> 0.02 us
  local copies, waits for them, and re-layouts: 1.29 us -> 0.29 us
    pallas_call x3 -> x4, Pallas kernels: 15.1 us -> 16.8 us  [first_block(): pl.pallas_call(functools.partial(first_kernel, parts, which), out_shape=t...]
    ppermute x5, starting transfers between devices: 9.82 us -> 11.1 us  [swap(): return lax.ppermute(block, 'lat', pairs)]
    ppermute x5, waiting for transfers between devices: 1.17 us -> 0.01 us  [swap(): return lax.ppermute(block, 'lat', pairs)]
    unnamed x18, local copies, waits for them, and re-layouts: 1.04 us -> 0.04 us
    pallas_call x1 -> x0, Pallas kernels: 0.8 us -> none  [unpack_own(): pl.pallas_call(unpack_own_kernel, out_shape=jax.ShapeDtypeStruct((2, 10,...]
    pallas_call x1, Pallas kernels: 11.6 us -> 10.9 us  [second_block(): pl.pallas_call(second_kernel, out_shape=jax.ShapeDtypeStruct((2, 4, 32, 1...]
  transfers between devices with their start and end apart: 7 -> 7, of which waited for: 1 -> 0; matrix products, arithmetic and copies ran while one was open for 1% -> 1% of each run, Pallas kernels for 32% -> 34%
where the time goes in v5:
time: 49.7 us; the launch traced here: 49.5 us
  Pallas kernels  30.5 us (61%)
  starting transfers between devices  18 us (36%)
  other arithmetic  0.53 us (1%)
    pallas_call x4, Pallas kernels, first_block(): pl.pallas_call(functools.partial(first_kernel, parts, which), out_shape=t...  16.8 us
    ppermute x5, starting transfers between devices, swap(): return lax.ppermute(block, 'lat', pairs)  11.1 us
    pallas_call x1, Pallas kernels, second_block(): pl.pallas_call(second_kernel, out_shape=jax.ShapeDtypeStruct((2, 4, 32, 1...  10.9 us
    ppermute x2, starting transfers between devices, around(): lax.ppermute(block, 'lon', [(i, (i + distance) % count) for i in range(co...  6.85 us
    pallas_call x1, Pallas kernels, patches(): pl.pallas_call(patch_kernel, out_shape=tuple((jax.ShapeDtypeStruct((n, 96...  2.59 us
  transfers between devices with their start and end apart: 7, of which 0 were waited for; matrix products, arithmetic and copies ran while one was open for 1% of the time, Pallas kernels for 34%

profile of v5, /device:TPU:25, one launch (start us, length us, event | category | flops | bytes accessed | tf_op | source)
XLA Modules:
  0.0 49.5 jit_solution(9050543773715052275)
XLA Ops:
  0.0 0.1 pad_add_fusion.par_ref.refs_0_
  0.1 0.0 copy-start.8
  0.1 0.0 copy-start.7
  0.1 2.6 %shard_map.118 = (bf16[8,96,128]{2,1,0:T(8,128)(2,1)S(1)}, bf16[8,96,128]{2,1,0:T(8,128)(2,1)S(1)}, bf16[1,96,128]{2,1,0:T(8,128)(2,1)S(1)}, bf16[1,96,128]{2,1,0:T(8,128)(2,1)S(1)}) custom-call(s32[2]{0:T(128)S(1)} %pad_add_fusion.par_ref.refs_0_, bf16[2,5,32,256]{3,2,1,0:T(8,128)(2,1)} %atmos_any.1, bf16[32,256]{1,0:T(8,128)(2,1)} %oro_any.1, ...), custom_call_target="tpu_custom_call" | custom-call | flops 1000000000 | bytes 1000000 | tf_op jit(solution)/shard_map/pallas_call | solution.py:87
  2.7 0.8 %collective-permute-start = (bf16[1,96,128]{2,1,0:T(8,128)(2,1)S(1)}, bf16[1,96,128]{2,1,0:T(8,128)(2,1)S(1)}, u32[]{:S(2)}, u32[]{:S(2)}) collective-permute-start(bf16[1,96,128]{2,1,0:T(8,128)(2,1)S(1)} %get-tuple-element.17), channel_id=1, source_target_pairs={{0,16},{16,0},{32,48},{48,32},{64,80},{80,64},{96,112},{112,96},{1... | collective-permute-start | bytes 73736 | tf_op jit(solution)/shard_map/ppermute | solution.py:489
  3.4 4.5 %collective-permute-start.1 = (bf16[1,96,128]{2,1,0:T(8,128)(2,1)S(1)}, bf16[1,96,128]{2,1,0:T(8,128)(2,1)S(1)}, u32[]{:S(2)}, u32[]{:S(2)}) collective-permute-start(bf16[1,96,128]{2,1,0:T(8,128)(2,1)S(1)} %get-tuple-element.19), channel_id=1, source_target_pairs={{16,32},{32,16},{48,64},{64,48},{80,96},{96,80},{112,128},{128,112... | collective-permute-start | bytes 73736 | tf_op jit(solution)/shard_map/ppermute | solution.py:489
  8.0 0.0 copy-done.8
  8.0 0.0 copy-done.7
  8.1 0.2 pad.4
  8.3 0.0 copy-start.5
  8.3 0.0 copy-start.6
  8.3 0.4 fusion
  8.8 0.0 collective-permute-done.after_ref.refs_2_
  8.8 2.5 %collective-permute-start.2 = (bf16[8,96,128]{2,1,0:T(8,128)(2,1)S(1)}, bf16[8,96,128]{2,1,0:T(8,128)(2,1)S(1)}, u32[]{:S(2)}, u32[]{:S(2)}) collective-permute-start(bf16[8,96,128]{2,1,0:T(8,128)(2,1)S(1)} %constant_dynamic-update-slice_fusion), channel_id=1, source_target_pairs={{16,32},{32,16},{48,64},{64,48},{80,96},{96,80},{112,128},{128,112... | collective-permute-start | bytes 589832 | tf_op jit(solution)/shard_map/ppermute | solution.py:489
  11.3 0.0 collective-permute-done.1.refs_3_
  11.3 0.0 copy-done.5
  11.3 0.0 copy-done.6
  11.3 0.0 copy-start.3
  11.4 5.3 %shard_map.119 = (f32[2,8,48,512]{3,2,1,0:T(8,128)S(1)}, bf16[2,4,48,512]{3,2,1,0:T(8,128)(2,1)S(1)}, bf16[2,10,64,128]{3,2,1,0:T(8,128)(2,1)S(1)}) custom-call(bf16[1,96,128]{2,1,0:T(8,128)(2,1)S(1)} %collective-permute-done.after_ref.refs_2_, s32[2]{0:T(128)S(1)} %pad_add_fusion.par_ref.refs_0_, bf16[8,96,128]{2,1,0:T(8,128)(2,1)S(1)} %get-tuple-element.18.refs_1_, ...), custom_call_target="tpu_custom_call" | custom-call | flops 10000000000 | bytes 10000000 | tf_op jit(solution)/shard_map/pallas_call | solution.py:346
  16.6 1.0 %collective-permute-start.5 = (bf16[2,4,48,512]{3,2,1,0:T(8,128)(2,1)S(1)}, bf16[2,4,48,512]{3,2,1,0:T(8,128)(2,1)S(1)}, u32[]{:S(2)}, u32[]{:S(2)}) collective-permute-start(bf16[2,4,48,512]{3,2,1,0:T(8,128)(2,1)S(1)} %get-tuple-element.27), channel_id=1, source_target_pairs={{0,16},{16,0},{32,48},{48,32},{64,80},{80,64},{96,112},{112,96},{1... | collective-permute-start | bytes 1179656 | tf_op jit(solution)/shard_map/ppermute | solution.py:489
  17.6 0.0 collective-permute-done.2.packed_ref
  17.6 0.0 copy-start.1
  17.7 0.0 copy-start.2
  17.7 0.3 shard_map.120
  17.9 1.7 %collective-permute-start.3 = (bf16[2,18,16,128]{3,2,1,0:T(8,128)(2,1)S(1)}, bf16[2,18,16,128]{3,2,1,0:T(8,128)(2,1)S(1)}, u32[]{:S(2)}, u32[]{:S(2)}) collective-permute-start(bf16[2,18,16,128]{3,2,1,0:T(8,128)(2,1)S(1)} %get-tuple-element.24), channel_id=1, source_target_pairs={{0,1},{1,2},{2,3},{3,4},{4,5},{5,6},{6,7},{7,8},{8,9},{9,10},{10,1... | collective-permute-start | bytes 442376 | tf_op jit(solution)/shard_map/ppermute | solution.py:494
  19.6 5.1 %collective-permute-start.4 = (bf16[2,18,16,128]{3,2,1,0:T(8,128)(2,1)S(1)}, bf16[2,18,16,128]{3,2,1,0:T(8,128)(2,1)S(1)}, u32[]{:S(2)}, u32[]{:S(2)}) collective-permute-start(bf16[2,18,16,128]{3,2,1,0:T(8,128)(2,1)S(1)} %get-tuple-element.25), channel_id=1, source_target_pairs={{0,15},{1,0},{2,1},{3,2},{4,3},{5,4},{6,5},{7,6},{8,7},{9,8},{10,9... | collective-permute-start | bytes 442376 | tf_op jit(solution)/shard_map/ppermute | solution.py:494
  24.8 0.0 copy-done.3
  24.8 0.0 copy-done.1
  24.8 0.0 copy-done.2
  24.8 4.4 %shard_map.121.after_ref.outer_mid = f32[2,4,48,512]{3,2,1,0:T(8,128)S(1)} custom-call(f32[2,8,48,512]{3,2,1,0:T(8,128)S(1)} %get-tuple-element.20.after_ref.own_mid, s32[2]{0:T(128)S(1)} %pad_add_fusion.par_ref.refs_0_, bf16[2,10,64,128]{3,2,1,0:T(8,128)(2,1)S(1)} %get-tuple-element.21.own_ref.refs_1_, ...), custom_call_target="tpu_custom_call" | custom-call | flops 10000000000 | bytes 10000000 | tf_op jit(solution)/shard_map/pallas_call | solution.py:346
  29.2 0.0 collective-permute-done.3.refs_2_.refs_3_
  29.2 0.0 collective-permute-done.4.refs_3_.refs_4_
  29.2 3.6 %shard_map.122 = (f32[2,8,32,512]{3,2,1,0:T(8,128)S(1)}, bf16[2,4,32,512]{3,2,1,0:T(8,128)(2,1)S(1)}) custom-call(f32[2,4,48,512]{3,2,1,0:T(8,128)S(1)} %shard_map.121.after_ref.outer_mid, s32[2]{0:T(128)S(1)} %pad_add_fusion.par_ref.refs_0_, bf16[2,10,64,128]{3,2,1,0:T(8,128)(2,1)S(1)} %get-tuple-element.21.own_ref.refs_1_, ...), custom_call_target="tpu_custom_call" | custom-call | flops 10000000000 | bytes 10000000 | tf_op jit(solution)/shard_map/pallas_call | solution.py:346
  32.9 2.3 %collective-permute-start.6 = (bf16[2,4,32,512]{3,2,1,0:T(8,128)(2,1)S(1)}, bf16[2,4,32,512]{3,2,1,0:T(8,128)(2,1)S(1)}, u32[]{:S(2)}, u32[]{:S(2)}) collective-permute-start(bf16[2,4,32,512]{3,2,1,0:T(8,128)(2,1)S(1)} %get-tuple-element.28), channel_id=1, source_target_pairs={{0,16},{16,0},{32,48},{48,32},{64,80},{80,64},{96,112},{112,96},{1... | collective-permute-start | bytes 786440 | tf_op jit(solution)/shard_map/ppermute | solution.py:489
  35.2 0.0 copy-start
  35.2 0.0 copy-start.4
  35.2 3.4 %shard_map.123.outer_edge = f32[2,4,32,512]{3,2,1,0:T(8,128)S(1)} custom-call(f32[2,8,32,512]{3,2,1,0:T(8,128)S(1)} %get-tuple-element.26.after_ref.own_edge, s32[2]{0:T(128)S(1)} %pad_add_fusion.par_ref.refs_0_, bf16[2,10,64,128]{3,2,1,0:T(8,128)(2,1)S(1)} %get-tuple-element.21.own_ref.refs_1_, bf16[2,8,64,128]{3,2,1,0:T(8,128)(2,1)S(1)} %get-tuple-element.23.refs_2_, ...), custom_call_target="tpu_custom_call" | custom-call | flops 10000000000 | bytes 10000000 | tf_op jit(solution)/shard_map/pallas_call | solution.py:346
  38.6 0.0 collective-permute-done.5.near_mid_ref
  38.6 0.0 collective-permute-done.6.near_edge_ref
  38.6 0.0 copy-done
  38.6 0.0 copy-done.4
  38.6 10.9 %shard_map.124 = bf16[2,4,32,1024]{3,2,1,0:T(8,128)(2,1)} custom-call(s32[2]{0:T(128)S(1)} %pad_add_fusion.par_ref.refs_0_, f32[2,8,48,512]{3,2,1,0:T(8,128)S(1)} %get-tuple-element.20.after_ref.own_mid, f32[2,4,48,512]{3,2,1,0:T(8,128)S(1)} %shard_map.121.after_ref.outer_mid, f32[2,8,32,512]{3,2,1,0:T(8,128)S(1)} %get-tuple-element.26.after_ref.own_edge, ...), custom_call_target="tpu_custom_call" | custom-call | flops 10000000000 | bytes 10000000 | tf_op jit(solution)/shard_map/pallas_call | solution.py:452
  (4 shorter events, 0.0 us)
Async XLA Ops:
  0.1 7.9 %copy-start.8 = (f32[512]{0:T(512)S(1)}, f32[512]{0:T(512)}, u32[]{:S(2)}) copy-start(f32[512]{0:T(512)} %param.17) | copy-start | bytes 6148
  0.1 8.0 %copy-start.7 = (bf16[12,12,6,512]{3,2,1,0:T(8,128)(2,1)S(1)}, bf16[12,12,6,512]{3,2,1,0:T(8,128)(2,1)}, u32[]{:S(2)}) copy-start(bf16[12,12,6,512]{3,2,1,0:T(8,128)(2,1)} %param.15) | copy-start | bytes 2654212
  2.7 6.1 %collective-permute-start = (bf16[1,96,128]{2,1,0:T(8,128)(2,1)S(1)}, bf16[1,96,128]{2,1,0:T(8,128)(2,1)S(1)}, u32[]{:S(2)}, u32[]{:S(2)}) collective-permute-start(bf16[1,96,128]{2,1,0:T(8,128)(2,1)S(1)} %get-tuple-element.17), channel_id=1, source_target_pairs={{0,16},{16,0},{32,48},{48,32},{64,80},{80,64},{96,112},{112,96},{1... | collective-permute-start | bytes 73736 | tf_op jit(solution)/shard_map/ppermute | solution.py:489
  3.4 7.9 %collective-permute-start.1 = (bf16[1,96,128]{2,1,0:T(8,128)(2,1)S(1)}, bf16[1,96,128]{2,1,0:T(8,128)(2,1)S(1)}, u32[]{:S(2)}, u32[]{:S(2)}) collective-permute-start(bf16[1,96,128]{2,1,0:T(8,128)(2,1)S(1)} %get-tuple-element.19), channel_id=1, source_target_pairs={{16,32},{32,16},{48,64},{64,48},{80,96},{96,80},{112,128},{128,112... | collective-permute-start | bytes 73736 | tf_op jit(solution)/shard_map/ppermute | solution.py:489
  8.3 3.0 %copy-start.5 = (f32[2,512]{1,0:T(2,128)S(1)}, f32[2,512]{1,0:T(2,128)}, u32[]{:S(2)}) copy-start(f32[2,512]{1,0:T(2,128)} %refs_6_.7) | copy-start | bytes 12292
  8.3 3.0 %copy-start.6 = (f32[2,512]{1,0:T(2,128)S(1)}, f32[2,512]{1,0:T(2,128)}, u32[]{:S(2)}) copy-start(f32[2,512]{1,0:T(2,128)} %gain_ref.1) | copy-start | bytes 12292
  8.8 8.9 %collective-permute-start.2 = (bf16[8,96,128]{2,1,0:T(8,128)(2,1)S(1)}, bf16[8,96,128]{2,1,0:T(8,128)(2,1)S(1)}, u32[]{:S(2)}, u32[]{:S(2)}) collective-permute-start(bf16[8,96,128]{2,1,0:T(8,128)(2,1)S(1)} %constant_dynamic-update-slice_fusion), channel_id=1, source_target_pairs={{16,32},{32,16},{48,64},{64,48},{80,96},{96,80},{112,128},{128,112... | collective-permute-start | bytes 589832 | tf_op jit(solution)/shard_map/ppermute | solution.py:489
  11.3 13.4 %copy-start.3 = (bf16[2,512,512]{2,1,0:T(8,128)(2,1)S(1)}, bf16[2,512,512]{2,1,0:T(8,128)(2,1)}, u32[]{:S(2)}) copy-start(bf16[2,512,512]{2,1,0:T(8,128)(2,1)} %wo_ref.1) | copy-start | bytes 3145732
  16.6 22.0 %collective-permute-start.5 = (bf16[2,4,48,512]{3,2,1,0:T(8,128)(2,1)S(1)}, bf16[2,4,48,512]{3,2,1,0:T(8,128)(2,1)S(1)}, u32[]{:S(2)}, u32[]{:S(2)}) collective-permute-start(bf16[2,4,48,512]{3,2,1,0:T(8,128)(2,1)S(1)} %get-tuple-element.27), channel_id=1, source_target_pairs={{0,16},{16,0},{32,48},{48,32},{64,80},{80,64},{96,112},{112,96},{1... | collective-permute-start | bytes 1179656 | tf_op jit(solution)/shard_map/ppermute | solution.py:489
  17.6 7.1 %copy-start.1 = (bf16[2,512,1024]{2,1,0:T(8,128)(2,1)S(1)}, bf16[2,512,1024]{2,1,0:T(8,128)(2,1)}, u32[]{:S(2)}) copy-start(bf16[2,512,1024]{2,1,0:T(8,128)(2,1)} %wkv_ref.1) | copy-start | bytes 6291460
  17.7 7.1 %copy-start.2 = (bf16[2,512,512]{2,1,0:T(8,128)(2,1)S(1)}, bf16[2,512,512]{2,1,0:T(8,128)(2,1)}, u32[]{:S(2)}) copy-start(bf16[2,512,512]{2,1,0:T(8,128)(2,1)} %wq_ref.1) | copy-start | bytes 3145732
  17.9 11.3 %collective-permute-start.3 = (bf16[2,18,16,128]{3,2,1,0:T(8,128)(2,1)S(1)}, bf16[2,18,16,128]{3,2,1,0:T(8,128)(2,1)S(1)}, u32[]{:S(2)}, u32[]{:S(2)}) collective-permute-start(bf16[2,18,16,128]{3,2,1,0:T(8,128)(2,1)S(1)} %get-tuple-element.24), channel_id=1, source_target_pairs={{0,1},{1,2},{2,3},{3,4},{4,5},{5,6},{6,7},{7,8},{8,9},{9,10},{10,1... | collective-permute-start | bytes 442376 | tf_op jit(solution)/shard_map/ppermute | solution.py:494
  19.6 9.6 %collective-permute-start.4 = (bf16[2,18,16,128]{3,2,1,0:T(8,128)(2,1)S(1)}, bf16[2,18,16,128]{3,2,1,0:T(8,128)(2,1)S(1)}, u32[]{:S(2)}, u32[]{:S(2)}) collective-permute-start(bf16[2,18,16,128]{3,2,1,0:T(8,128)(2,1)S(1)} %get-tuple-element.25), channel_id=1, source_target_pairs={{0,15},{1,0},{2,1},{3,2},{4,3},{5,4},{6,5},{7,6},{8,7},{9,8},{10,9... | collective-permute-start | bytes 442376 | tf_op jit(solution)/shard_map/ppermute | solution.py:494
  32.9 5.8 %collective-permute-start.6 = (bf16[2,4,32,512]{3,2,1,0:T(8,128)(2,1)S(1)}, bf16[2,4,32,512]{3,2,1,0:T(8,128)(2,1)S(1)}, u32[]{:S(2)}, u32[]{:S(2)}) collective-permute-start(bf16[2,4,32,512]{3,2,1,0:T(8,128)(2,1)S(1)} %get-tuple-element.28), channel_id=1, source_target_pairs={{0,16},{16,0},{32,48},{48,32},{64,80},{80,64},{96,112},{112,96},{1... | collective-permute-start | bytes 786440 | tf_op jit(solution)/shard_map/ppermute | solution.py:489
  35.2 3.5 %copy-start = (bf16[2048,1024]{1,0:T(8,128)(2,1)S(1)}, bf16[2048,1024]{1,0:T(8,128)(2,1)}, u32[]{:S(2)}) copy-start(bf16[2048,1024]{1,0:T(8,128)(2,1)} %wm_ref.1) | copy-start | bytes 12582916
  35.2 3.5 %copy-start.4 = (f32[2048]{0:T(1024)S(1)}, f32[2048]{0:T(1024)}, u32[]{:S(2)}) copy-start(f32[2048]{0:T(1024)} %param.22) | copy-start | bytes 24580

commit v6 on v5

--- a/solution.py
+++ b/solution.py
@@ -117,11 +117,9 @@
             out_ref[level, :, half * 32 : half * 32 + 32, :] = tile
 
 
-def unpack_far_kernel(after_ref, packed_ref, own_ref, far_ref, low_ref, high_ref):
+def unpack_far_kernel(after_ref, packed_ref, own_ref, far_ref, high_ref):
     del after_ref
     unpack_rows(packed_ref, far_ref)
-    low_ref[:, 0:10] = own_ref[:, :, 0:16, :]
-    low_ref[:, 10:18] = far_ref[:, :, 0:16, :]
     high_ref[:, 0:10] = own_ref[:, :, 48:64, :]
     high_ref[:, 10:18] = far_ref[:, :, 48:64, :]
 
@@ -133,10 +131,9 @@
         out_shape=(
             jax.ShapeDtypeStruct((2, 8, 64, 128), BF),
             jax.ShapeDtypeStruct((2, 18, 16, 128), BF),
-            jax.ShapeDtypeStruct((2, 18, 16, 128), BF),
         ),
         in_specs=[pl.BlockSpec(memory_space=pl.ANY)] + [vmem] * 2,
-        out_specs=(vmem,) * 3,
+        out_specs=(vmem,) * 2,
         compiler_params=params(),
         cost_estimate=pl.CostEstimate(flops=10**9, bytes_accessed=10**6, transcendentals=0),
     )(after, packed, own)
@@ -184,27 +181,29 @@
     return jnp.concatenate(out, axis=1)
 
 
-MIDDLE, EDGES = (1, 2, 3), (0, 4)
+LOW, MIDDLE, HIGH = (0,), (1, 2, 3), (4,)
 
 
 def first_kernel(parts, which, after_ref, *refs):
     del after_ref
     par_ref, refs = refs[0], refs[1:]
-    leading = parts == (0,) and which == MIDDLE
+    leading, following = parts == (0,) and which == MIDDLE, parts == (1,) and which == MIDDLE
     if leading:
         own_packed, edge_ref, near_ref, refs = refs[0], refs[1], refs[2], refs[3:]
     else:
         own_ref, refs = refs[0], refs[1:]
     if 1 in parts:
         far_ref, refs = refs[0], refs[1:]
-    if which == EDGES:
-        low_ref, high_ref, refs = refs[0], refs[1], refs[2:]
+    if which != MIDDLE:
+        side_ref, refs = refs[0], refs[1:]
     wemb_ref, lev_ref, gain_ref, wq_ref, wkv_ref, wo_ref, *refs = refs
     x1_refs, refs = refs[: len(parts)], refs[len(parts) :]
     if 0 in parts:
         send_ref, refs = refs[0], refs[1:]
     if leading:
         own_ref, refs = refs[0], refs[1:]
+    if following:
+        low_ref, refs = refs[0], refs[1:]
     wide, gathered, x0, normed, query, keyval, heads, *refs = refs
     par = par_ref[0]
     if leading:
@@ -222,23 +221,26 @@
     else:
         wq, wkv, wo = wq_ref.at[0], wkv_ref.at[0], wo_ref.at[0]
 
-    def spread(part, to, count, center, low, high):
+    def spread(part, to, count, center, side):
         rows = (slice(None), pl.ds(to, count))
-        if which == EDGES:
-            wide[part, *rows, 0:16, :] = low.astype(F32)
+        if which == LOW:
+            wide[part, *rows, 0:16, :] = side().astype(F32)
             wide[part, *rows, 16:32, :] = center[:, :, 0:16, :].astype(F32)
+        elif which == HIGH:
             wide[part, *rows, 64:80, :] = center[:, :, 48:64, :].astype(F32)
-            wide[part, *rows, 80:96, :] = high.astype(F32)
+            wide[part, *rows, 80:96, :] = side().astype(F32)
         else:
             wide[part, *rows, 16:80, :] = center.astype(F32)
 
-    sides = [r for r in ((low_ref, high_ref) if which == EDGES else ())]
     if 0 in parts:
-        spread(0, 0, 10, own_ref[...], *([r[:, 0:10] for r in sides] or (None, None)))
+        spread(0, 0, 10, own_ref[...], lambda: side_ref[:, 0:10])
     if 1 in parts:
-        spread(1, 2 * par, 8, far_ref[...], *([r[:, 10:18] for r in sides] or (None, None)))
+        spread(1, 2 * par, 8, far_ref[...], lambda: side_ref[:, 10:18])
         beside = pl.ds(8 * par, 2)
-        spread(1, 8 * (1 - par), 2, own_ref[:, beside], *([r[:, beside] for r in sides] or (None, None)))
+        spread(1, 8 * (1 - par), 2, own_ref[:, beside], lambda: side_ref[:, beside])
+    if following:
+        low_ref[:, 0:10] = own_ref[:, :, 0:16, :]
+        low_ref[:, 10:18] = far_ref[:, :, 0:16, :]
     gain = gain_ref[0:1, :]
     half = 1 - par
 
@@ -329,6 +331,8 @@
         pltpu.VMEM((count, 2, 128, 1024), BF),
         pltpu.VMEM((count, 2, 128, D), BF),
     ]
+    if parts == (1,) and which == MIDDLE:
+        outs.append(jax.ShapeDtypeStruct((2, 18, 16, 128), BF))
     projections = [w_query, w_keyval, w_out]
     if leading:
         outs.append(jax.ShapeDtypeStruct((2, 10, 64, 128), BF))
@@ -359,15 +363,16 @@
 
 
 def second_kernel(
-    par_ref, own_mid, outer_mid, own_edge, outer_edge, near_mid_ref, near_edge_ref, gain_ref, mgain_ref,
+    par_ref, own_low, outer_low, own_mid, outer_mid, own_high, outer_high,
+    near_low_ref, near_mid_ref, near_high_ref, gain_ref, mgain_ref,
     wq_ref, wkv_ref, wo_ref, wm_ref,
     out_ref,
     near, x2, normed, query, keyval, heads,
 ):
     par, pole = par_ref[0], par_ref[1]
-    near[:, :, 0:16, :] = near_edge_ref[:, :, 0:16, :].astype(F32)
+    near[:, :, 0:16, :] = near_low_ref[...].astype(F32)
     near[:, :, 16:64, :] = near_mid_ref[...].astype(F32)
-    near[:, :, 64:80, :] = near_edge_ref[:, :, 16:32, :].astype(F32)
+    near[:, :, 64:80, :] = near_high_ref[...].astype(F32)
     gain = gain_ref[1:2, :]
     upper = iota((8, D), 0) >= 4
     key_row = (iota((1, 256), 1) // 8) % 8
@@ -378,11 +383,11 @@
             return jnp.concatenate([block(n, first, 4), block(n, 4, last)], axis=1)
         if first >= 12:
             return near[:, first - 12 : last - 12, n * 8 : n * 8 + 8, :]
-        middle = 2 <= n < 8
-        at = n * 8 - (16 if middle else 48 if n >= 8 else 0)
+        part = 0 if n < 2 else 1 if n < 8 else 2
+        at = n * 8 - (0, 16, 64)[part]
         if first < 4:
-            return (outer_mid if middle else outer_edge)[:, first:last, at : at + 8, :]
-        return (own_mid if middle else own_edge)[:, first - 4 : last - 4, at : at + 8, :]
+            return (outer_low, outer_mid, outer_high)[part][:, first:last, at : at + 8, :]
+        return (own_low, own_mid, own_high)[part][:, first - 4 : last - 4, at : at + 8, :]
 
     def window(w, first, last):
         return jnp.where(upper, block(w, first, last), block(w + 1, first, last))
@@ -444,7 +449,7 @@
     pipelined([norm, project, attention, project_out, merge], [0, 1])
 
 
-def second_block(par, x1_parts, near_mid, near_edge, norm_gain, merge_gain, w_query, w_keyval, w_out, merge_weight):
+def second_block(par, x1_parts, near_parts, norm_gain, merge_gain, w_query, w_keyval, w_out, merge_weight):
     vmem = pl.BlockSpec(memory_space=pltpu.VMEM)
     weights = [
         pltpu.with_memory_space_constraint(w, pltpu.VMEM) for w in (w_query, w_keyval, w_out, merge_weight)
@@ -452,7 +457,7 @@
     return pl.pallas_call(
         second_kernel,
         out_shape=jax.ShapeDtypeStruct((2, 4, 32, 1024), BF),
-        in_specs=[pl.BlockSpec(memory_space=pltpu.SMEM)] + [vmem] * 12,
+        in_specs=[pl.BlockSpec(memory_space=pltpu.SMEM)] + [vmem] * 15,
         out_specs=vmem,
         scratch_shapes=[
             pltpu.VMEM((2, 4, 80, D), F32),
@@ -465,7 +470,7 @@
         compiler_params=params(),
         cost_estimate=pl.CostEstimate(flops=10**10, bytes_accessed=10**7, transcendentals=0),
     )(
-        par, *x1_parts, near_mid, near_edge, norm_gain, merge_gain, *weights
+        par, *x1_parts, *near_parts, norm_gain, merge_gain, *weights
     )
 
 
@@ -511,18 +516,20 @@
     weights = wemb, level_embed, norm_gain, w_query, w_keyval, w_out
     own_mid, send_mid, own = first_block((0,), MIDDLE, edge, place, (own, edge, near), *weights)
     near_mid = swap(send_mid, 0)
-    far, low, high = unpack_far(own_mid, far, own)
-    from_low, from_high = around(high, 1), around(low, -1)
-    (outer_mid,) = first_block((1,), MIDDLE, own_mid, place, (own, far), *weights)
-    own_edge, send_edge = first_block(
-        (0,), EDGES, outer_mid, place, (own, from_low, from_high), *weights
+    far, high = unpack_far(own_mid, far, own)
+    from_low = around(high, 1)
+    outer_mid, low = first_block((1,), MIDDLE, own_mid, place, (own, far), *weights)
+    from_high = around(low, -1)
+    own_low, outer_low, send_low = first_block(
+        (0, 1), LOW, outer_mid, place, (own, far, from_low), *weights
     )
-    near_edge = swap(send_edge, 0)
-    (outer_edge,) = first_block(
-        (1,), EDGES, own_edge, place, (own, far, from_low, from_high), *weights
-    )
+    near_low = swap(send_low, 0)
+    own_high, send_high = first_block((0,), HIGH, own_low, place, (own, from_high), *weights)
+    near_high = swap(send_high, 0)
+    (outer_high,) = first_block((1,), HIGH, own_high, place, (own, far, from_high), *weights)
     return second_block(
-        place, (own_mid, outer_mid, own_edge, outer_edge), near_mid, near_edge, norm_gain,
+        place, (own_low, outer_low, own_mid, outer_mid, own_high, outer_high),
+        (near_low, near_mid, near_high), norm_gain,
         merge_gain.reshape(1, -1), w_query, w_keyval, w_out, merge_weight,
     )
 

time: 49.7 us -> 52.5 us (1.056)
  starting transfers between devices: 18 us -> 19.6 us
  Pallas kernels: 30.5 us -> 31.6 us
    ppermute x2, starting transfers between devices: 6.85 us -> 8.35 us  [around(): lax.ppermute(block, 'lon', [(i, (i + distance) % count) for i in range(co...]
    pallas_call x4 -> x5, Pallas kernels: 16.8 us -> 17.9 us  [first_block(): pl.pallas_call(functools.partial(first_kernel, parts, which), out_shape=t...]
    ppermute x5 -> x6, starting transfers between devices: 11.1 us -> 11.3 us  [swap(): return lax.ppermute(block, 'lat', pairs)]
  transfers between devices with their start and end apart: 7 -> 8, of which waited for: 0 -> 0; matrix products, arithmetic and copies ran while one was open for 1% -> 1% of each run, Pallas kernels for 34% -> 35%
where the time goes in v6:
time: 52.5 us; the launch traced here: 52.3 us
  Pallas kernels  31.6 us (60%)
  starting transfers between devices  19.6 us (37%)
  other arithmetic  0.53 us (1%)
    pallas_call x5, Pallas kernels, first_block(): pl.pallas_call(functools.partial(first_kernel, parts, which), out_shape=t...  17.9 us
    ppermute x6, starting transfers between devices, swap(): return lax.ppermute(block, 'lat', pairs)  11.3 us
    pallas_call x1, Pallas kernels, second_block(): pl.pallas_call(second_kernel, out_shape=jax.ShapeDtypeStruct((2, 4, 32, 1...  10.9 us
    ppermute x2, starting transfers between devices, around(): lax.ppermute(block, 'lon', [(i, (i + distance) % count) for i in range(co...  8.35 us
    pallas_call x1, Pallas kernels, patches(): pl.pallas_call(patch_kernel, out_shape=tuple((jax.ShapeDtypeStruct((n, 96...  2.59 us
  transfers between devices with their start and end apart: 8, of which 0 were waited for; matrix products, arithmetic and copies ran while one was open for 1% of the time, Pallas kernels for 35%

profile of v6, /device:TPU:25, one launch (start us, length us, event | category | flops | bytes accessed | tf_op | source)
XLA Modules:
  0.0 52.3 jit_solution(12467740818916542410)
XLA Ops:
  0.0 0.1 pad_add_fusion.par_ref.refs_0_
  0.1 0.0 copy-start.8
  0.1 0.0 copy-start.7
  0.1 2.6 %shard_map.118 = (bf16[8,96,128]{2,1,0:T(8,128)(2,1)S(1)}, bf16[8,96,128]{2,1,0:T(8,128)(2,1)S(1)}, bf16[1,96,128]{2,1,0:T(8,128)(2,1)S(1)}, bf16[1,96,128]{2,1,0:T(8,128)(2,1)S(1)}) custom-call(s32[2]{0:T(128)S(1)} %pad_add_fusion.par_ref.refs_0_, bf16[2,5,32,256]{3,2,1,0:T(8,128)(2,1)} %atmos_any.1, bf16[32,256]{1,0:T(8,128)(2,1)} %oro_any.1, ...), custom_call_target="tpu_custom_call" | custom-call | flops 1000000000 | bytes 1000000 | tf_op jit(solution)/shard_map/pallas_call | solution.py:87
  2.7 0.8 %collective-permute-start = (bf16[1,96,128]{2,1,0:T(8,128)(2,1)S(1)}, bf16[1,96,128]{2,1,0:T(8,128)(2,1)S(1)}, u32[]{:S(2)}, u32[]{:S(2)}) collective-permute-start(bf16[1,96,128]{2,1,0:T(8,128)(2,1)S(1)} %get-tuple-element.21), channel_id=1, source_target_pairs={{0,16},{16,0},{32,48},{48,32},{64,80},{80,64},{96,112},{112,96},{1... | collective-permute-start | bytes 73736 | tf_op jit(solution)/shard_map/ppermute | solution.py:494
  3.4 4.5 %collective-permute-start.1 = (bf16[1,96,128]{2,1,0:T(8,128)(2,1)S(1)}, bf16[1,96,128]{2,1,0:T(8,128)(2,1)S(1)}, u32[]{:S(2)}, u32[]{:S(2)}) collective-permute-start(bf16[1,96,128]{2,1,0:T(8,128)(2,1)S(1)} %get-tuple-element.23), channel_id=1, source_target_pairs={{16,32},{32,16},{48,64},{64,48},{80,96},{96,80},{112,128},{128,112... | collective-permute-start | bytes 73736 | tf_op jit(solution)/shard_map/ppermute | solution.py:494
  8.0 0.0 copy-done.8
  8.0 0.0 copy-done.7
  8.1 0.2 pad.4
  8.3 0.0 copy-start.5
  8.3 0.0 copy-start.6
  8.3 0.4 fusion
  8.8 0.0 collective-permute-done.after_ref.refs_2_
  8.8 2.5 %collective-permute-start.2 = (bf16[8,96,128]{2,1,0:T(8,128)(2,1)S(1)}, bf16[8,96,128]{2,1,0:T(8,128)(2,1)S(1)}, u32[]{:S(2)}, u32[]{:S(2)}) collective-permute-start(bf16[8,96,128]{2,1,0:T(8,128)(2,1)S(1)} %constant_dynamic-update-slice_fusion), channel_id=1, source_target_pairs={{16,32},{32,16},{48,64},{64,48},{80,96},{96,80},{112,128},{128,112... | collective-permute-start | bytes 589832 | tf_op jit(solution)/shard_map/ppermute | solution.py:494
  11.3 0.0 collective-permute-done.1.refs_3_
  11.3 0.0 copy-done.5
  11.3 0.0 copy-done.6
  11.3 0.0 copy-start.3
  11.4 5.3 %shard_map.119 = (f32[2,8,48,512]{3,2,1,0:T(8,128)S(1)}, bf16[2,4,48,512]{3,2,1,0:T(8,128)(2,1)S(1)}, bf16[2,10,64,128]{3,2,1,0:T(8,128)(2,1)S(1)}) custom-call(bf16[1,96,128]{2,1,0:T(8,128)(2,1)S(1)} %collective-permute-done.after_ref.refs_2_, s32[2]{0:T(128)S(1)} %pad_add_fusion.par_ref.refs_0_, bf16[8,96,128]{2,1,0:T(8,128)(2,1)S(1)} %get-tuple-element.22.refs_1_, ...), custom_call_target="tpu_custom_call" | custom-call | flops 10000000000 | bytes 10000000 | tf_op jit(solution)/shard_map/pallas_call | solution.py:350
  16.6 1.0 %collective-permute-start.6 = (bf16[2,4,48,512]{3,2,1,0:T(8,128)(2,1)S(1)}, bf16[2,4,48,512]{3,2,1,0:T(8,128)(2,1)S(1)}, u32[]{:S(2)}, u32[]{:S(2)}) collective-permute-start(bf16[2,4,48,512]{3,2,1,0:T(8,128)(2,1)S(1)} %get-tuple-element.35), channel_id=1, source_target_pairs={{0,16},{16,0},{32,48},{48,32},{64,80},{80,64},{96,112},{112,96},{1... | collective-permute-start | bytes 1179656 | tf_op jit(solution)/shard_map/ppermute | solution.py:494
  17.7 0.0 collective-permute-done.2.packed_ref
  17.7 0.0 copy-start.1
  17.7 0.0 copy-start.2
  17.7 0.2 shard_map.120
  17.9 1.7 %collective-permute-start.3 = (bf16[2,18,16,128]{3,2,1,0:T(8,128)(2,1)S(1)}, bf16[2,18,16,128]{3,2,1,0:T(8,128)(2,1)S(1)}, u32[]{:S(2)}, u32[]{:S(2)}) collective-permute-start(bf16[2,18,16,128]{3,2,1,0:T(8,128)(2,1)S(1)} %get-tuple-element.29), channel_id=1, source_target_pairs={{0,1},{1,2},{2,3},{3,4},{4,5},{5,6},{6,7},{7,8},{8,9},{9,10},{10,1... | collective-permute-start | bytes 442376 | tf_op jit(solution)/shard_map/ppermute | solution.py:499
  19.6 0.0 copy-done.3
  19.6 0.0 copy-done.1
  19.6 0.0 copy-done.2
  19.6 4.5 %shard_map.121 = (f32[2,4,48,512]{3,2,1,0:T(8,128)S(1)}, bf16[2,18,16,128]{3,2,1,0:T(8,128)(2,1)S(1)}) custom-call(f32[2,8,48,512]{3,2,1,0:T(8,128)S(1)} %get-tuple-element.24.after_ref.own_mid, s32[2]{0:T(128)S(1)} %pad_add_fusion.par_ref.refs_0_, bf16[2,10,64,128]{3,2,1,0:T(8,128)(2,1)S(1)} %get-tuple-element.25.own_ref.refs_1_, ...), custom_call_target="tpu_custom_call" | custom-call | flops 10000000000 | bytes 10000000 | tf_op jit(solution)/shard_map/pallas_call | solution.py:350
  24.1 6.6 %collective-permute-start.4 = (bf16[2,18,16,128]{3,2,1,0:T(8,128)(2,1)S(1)}, bf16[2,18,16,128]{3,2,1,0:T(8,128)(2,1)S(1)}, u32[]{:S(2)}, u32[]{:S(2)}) collective-permute-start(bf16[2,18,16,128]{3,2,1,0:T(8,128)(2,1)S(1)} %get-tuple-element.32), channel_id=1, source_target_pairs={{0,15},{1,0},{2,1},{3,2},{4,3},{5,4},{6,5},{7,6},{8,7},{9,8},{10,9... | collective-permute-start | bytes 442376 | tf_op jit(solution)/shard_map/ppermute | solution.py:499
  30.7 0.0 collective-permute-done.3.refs_3_
  30.7 3.2 %shard_map.122 = (f32[2,8,16,512]{3,2,1,0:T(8,128)S(1)}, f32[2,4,16,512]{3,2,1,0:T(8,128)S(1)}, bf16[2,4,16,512]{3,2,1,0:T(8,128)(2,1)S(1)}) custom-call(f32[2,4,48,512]{3,2,1,0:T(8,128)S(1)} %get-tuple-element.28.after_ref.outer_mid, s32[2]{0:T(128)S(1)} %pad_add_fusion.par_ref.refs_0_, bf16[2,10,64,128]{3,2,1,0:T(8,128)(2,1)S(1)} %get-tuple-element.25.own_ref.refs_1_, ...), custom_call_target="tpu_custom_call" | custom-call | flops 10000000000 | bytes 10000000 | tf_op jit(solution)/shard_map/pallas_call | solution.py:350
  34.0 2.1 %collective-permute-start.5 = (bf16[2,4,16,512]{3,2,1,0:T(8,128)(2,1)S(1)}, bf16[2,4,16,512]{3,2,1,0:T(8,128)(2,1)S(1)}, u32[]{:S(2)}, u32[]{:S(2)}) collective-permute-start(bf16[2,4,16,512]{3,2,1,0:T(8,128)(2,1)S(1)} %get-tuple-element.34), channel_id=1, source_target_pairs={{0,16},{16,0},{32,48},{48,32},{64,80},{80,64},{96,112},{112,96},{1... | collective-permute-start | bytes 393224 | tf_op jit(solution)/shard_map/ppermute | solution.py:494
  36.1 0.0 collective-permute-done.4.refs_2_.refs_3_
  36.1 2.5 %shard_map.123 = (f32[2,8,16,512]{3,2,1,0:T(8,128)S(1)}, bf16[2,4,16,512]{3,2,1,0:T(8,128)(2,1)S(1)}) custom-call(f32[2,8,16,512]{3,2,1,0:T(8,128)S(1)} %get-tuple-element.30.after_ref.own_low, s32[2]{0:T(128)S(1)} %pad_add_fusion.par_ref.refs_0_, bf16[2,10,64,128]{3,2,1,0:T(8,128)(2,1)S(1)} %get-tuple-element.25.own_ref.refs_1_, ...), custom_call_target="tpu_custom_call" | custom-call | flops 10000000000 | bytes 10000000 | tf_op jit(solution)/shard_map/pallas_call | solution.py:350
  38.6 0.3 collective-permute-start.7
  38.9 0.0 copy-start
  38.9 0.0 copy-start.4
  38.9 2.4 %shard_map.124.outer_high = f32[2,4,16,512]{3,2,1,0:T(8,128)S(1)} custom-call(f32[2,8,16,512]{3,2,1,0:T(8,128)S(1)} %get-tuple-element.33.after_ref.own_high, s32[2]{0:T(128)S(1)} %pad_add_fusion.par_ref.refs_0_, bf16[2,10,64,128]{3,2,1,0:T(8,128)(2,1)S(1)} %get-tuple-element.25.own_ref.refs_1_, bf16[2,8,64,128]{3,2,1,0:T(8,128)(2,1)S(1)} %get-tuple-element.27.refs_2_, ...), custom_call_target="tpu_custom_call" | custom-call | flops 10000000000 | bytes 10000000 | tf_op jit(solution)/shard_map/pallas_call | solution.py:350
  41.3 0.0 collective-permute-done.6.near_mid_ref
  41.3 0.0 collective-permute-done.5.near_low_ref
  41.4 0.0 collective-permute-done.7.near_high_ref
  41.4 0.0 copy-done
  41.4 0.0 copy-done.4
  41.4 10.9 %shard_map.125 = bf16[2,4,32,1024]{3,2,1,0:T(8,128)(2,1)} custom-call(s32[2]{0:T(128)S(1)} %pad_add_fusion.par_ref.refs_0_, f32[2,8,16,512]{3,2,1,0:T(8,128)S(1)} %get-tuple-element.30.after_ref.own_low, f32[2,4,16,512]{3,2,1,0:T(8,128)S(1)} %get-tuple-element.31.outer_low, f32[2,8,48,512]{3,2,1,0:T(8,128)S(1)} %get-tuple-element.24.after_ref.own_mid, ...), custom_call_target="tpu_custom_call" | custom-call | flops 10000000000 | bytes 10000000 | tf_op jit(solution)/shard_map/pallas_call | solution.py:457
  (4 shorter events, 0.0 us)
Async XLA Ops:
  0.1 7.9 %copy-start.8 = (f32[512]{0:T(512)S(1)}, f32[512]{0:T(512)}, u32[]{:S(2)}) copy-start(f32[512]{0:T(512)} %param.17) | copy-start | bytes 6148
  0.1 8.0 %copy-start.7 = (bf16[12,12,6,512]{3,2,1,0:T(8,128)(2,1)S(1)}, bf16[12,12,6,512]{3,2,1,0:T(8,128)(2,1)}, u32[]{:S(2)}) copy-start(bf16[12,12,6,512]{3,2,1,0:T(8,128)(2,1)} %param.15) | copy-start | bytes 2654212
  2.7 6.1 %collective-permute-start = (bf16[1,96,128]{2,1,0:T(8,128)(2,1)S(1)}, bf16[1,96,128]{2,1,0:T(8,128)(2,1)S(1)}, u32[]{:S(2)}, u32[]{:S(2)}) collective-permute-start(bf16[1,96,128]{2,1,0:T(8,128)(2,1)S(1)} %get-tuple-element.21), channel_id=1, source_target_pairs={{0,16},{16,0},{32,48},{48,32},{64,80},{80,64},{96,112},{112,96},{1... | collective-permute-start | bytes 73736 | tf_op jit(solution)/shard_map/ppermute | solution.py:494
  3.4 7.9 %collective-permute-start.1 = (bf16[1,96,128]{2,1,0:T(8,128)(2,1)S(1)}, bf16[1,96,128]{2,1,0:T(8,128)(2,1)S(1)}, u32[]{:S(2)}, u32[]{:S(2)}) collective-permute-start(bf16[1,96,128]{2,1,0:T(8,128)(2,1)S(1)} %get-tuple-element.23), channel_id=1, source_target_pairs={{16,32},{32,16},{48,64},{64,48},{80,96},{96,80},{112,128},{128,112... | collective-permute-start | bytes 73736 | tf_op jit(solution)/shard_map/ppermute | solution.py:494
  8.3 3.0 %copy-start.5 = (f32[2,512]{1,0:T(2,128)S(1)}, f32[2,512]{1,0:T(2,128)}, u32[]{:S(2)}) copy-start(f32[2,512]{1,0:T(2,128)} %refs_5_.9) | copy-start | bytes 12292
  8.3 3.0 %copy-start.6 = (f32[2,512]{1,0:T(2,128)S(1)}, f32[2,512]{1,0:T(2,128)}, u32[]{:S(2)}) copy-start(f32[2,512]{1,0:T(2,128)} %gain_ref.1) | copy-start | bytes 12292
  8.8 8.9 %collective-permute-start.2 = (bf16[8,96,128]{2,1,0:T(8,128)(2,1)S(1)}, bf16[8,96,128]{2,1,0:T(8,128)(2,1)S(1)}, u32[]{:S(2)}, u32[]{:S(2)}) collective-permute-start(bf16[8,96,128]{2,1,0:T(8,128)(2,1)S(1)} %constant_dynamic-update-slice_fusion), channel_id=1, source_target_pairs={{16,32},{32,16},{48,64},{64,48},{80,96},{96,80},{112,128},{128,112... | collective-permute-start | bytes 589832 | tf_op jit(solution)/shard_map/ppermute | solution.py:494
  11.3 8.3 %copy-start.3 = (bf16[2,512,512]{2,1,0:T(8,128)(2,1)S(1)}, bf16[2,512,512]{2,1,0:T(8,128)(2,1)}, u32[]{:S(2)}) copy-start(bf16[2,512,512]{2,1,0:T(8,128)(2,1)} %wo_ref.1) | copy-start | bytes 3145732
  16.6 24.7 %collective-permute-start.6 = (bf16[2,4,48,512]{3,2,1,0:T(8,128)(2,1)S(1)}, bf16[2,4,48,512]{3,2,1,0:T(8,128)(2,1)S(1)}, u32[]{:S(2)}, u32[]{:S(2)}) collective-permute-start(bf16[2,4,48,512]{3,2,1,0:T(8,128)(2,1)S(1)} %get-tuple-element.35), channel_id=1, source_target_pairs={{0,16},{16,0},{32,48},{48,32},{64,80},{80,64},{96,112},{112,96},{1... | collective-permute-start | bytes 1179656 | tf_op jit(solution)/shard_map/ppermute | solution.py:494
  17.7 2.0 %copy-start.1 = (bf16[2,512,1024]{2,1,0:T(8,128)(2,1)S(1)}, bf16[2,512,1024]{2,1,0:T(8,128)(2,1)}, u32[]{:S(2)}) copy-start(bf16[2,512,1024]{2,1,0:T(8,128)(2,1)} %wkv_ref.1) | copy-start | bytes 6291460
  17.7 2.0 %copy-start.2 = (bf16[2,512,512]{2,1,0:T(8,128)(2,1)S(1)}, bf16[2,512,512]{2,1,0:T(8,128)(2,1)}, u32[]{:S(2)}) copy-start(bf16[2,512,512]{2,1,0:T(8,128)(2,1)} %wq_ref.1) | copy-start | bytes 3145732
  17.9 12.8 %collective-permute-start.3 = (bf16[2,18,16,128]{3,2,1,0:T(8,128)(2,1)S(1)}, bf16[2,18,16,128]{3,2,1,0:T(8,128)(2,1)S(1)}, u32[]{:S(2)}, u32[]{:S(2)}) collective-permute-start(bf16[2,18,16,128]{3,2,1,0:T(8,128)(2,1)S(1)} %get-tuple-element.29), channel_id=1, source_target_pairs={{0,1},{1,2},{2,3},{3,4},{4,5},{5,6},{6,7},{7,8},{8,9},{9,10},{10,1... | collective-permute-start | bytes 442376 | tf_op jit(solution)/shard_map/ppermute | solution.py:499
  24.1 12.0 %collective-permute-start.4 = (bf16[2,18,16,128]{3,2,1,0:T(8,128)(2,1)S(1)}, bf16[2,18,16,128]{3,2,1,0:T(8,128)(2,1)S(1)}, u32[]{:S(2)}, u32[]{:S(2)}) collective-permute-start(bf16[2,18,16,128]{3,2,1,0:T(8,128)(2,1)S(1)} %get-tuple-element.32), channel_id=1, source_target_pairs={{0,15},{1,0},{2,1},{3,2},{4,3},{5,4},{6,5},{7,6},{8,7},{9,8},{10,9... | collective-permute-start | bytes 442376 | tf_op jit(solution)/shard_map/ppermute | solution.py:499
  34.0 7.4 %collective-permute-start.5 = (bf16[2,4,16,512]{3,2,1,0:T(8,128)(2,1)S(1)}, bf16[2,4,16,512]{3,2,1,0:T(8,128)(2,1)S(1)}, u32[]{:S(2)}, u32[]{:S(2)}) collective-permute-start(bf16[2,4,16,512]{3,2,1,0:T(8,128)(2,1)S(1)} %get-tuple-element.34), channel_id=1, source_target_pairs={{0,16},{16,0},{32,48},{48,32},{64,80},{80,64},{96,112},{112,96},{1... | collective-permute-start | bytes 393224 | tf_op jit(solution)/shard_map/ppermute | solution.py:494
  38.6 2.8 %collective-permute-start.7 = (bf16[2,4,16,512]{3,2,1,0:T(8,128)(2,1)S(1)}, bf16[2,4,16,512]{3,2,1,0:T(8,128)(2,1)S(1)}, u32[]{:S(2)}, u32[]{:S(2)}) collective-permute-start(bf16[2,4,16,512]{3,2,1,0:T(8,128)(2,1)S(1)} %get-tuple-element.36), channel_id=1, source_target_pairs={{0,16},{16,0},{32,48},{48,32},{64,80},{80,64},{96,112},{112,96},{1... | collective-permute-start | bytes 393224 | tf_op jit(solution)/shard_map/ppermute | solution.py:494
  38.9 2.5 %copy-start = (bf16[2048,1024]{1,0:T(8,128)(2,1)S(1)}, bf16[2048,1024]{1,0:T(8,128)(2,1)}, u32[]{:S(2)}) copy-start(bf16[2048,1024]{1,0:T(8,128)(2,1)} %wm_ref.1) | copy-start | bytes 12582916
  38.9 2.5 %copy-start.4 = (f32[2048]{0:T(1024)S(1)}, f32[2048]{0:T(1024)}, u32[]{:S(2)}) copy-start(f32[2048]{0:T(1024)} %param.22) | copy-start | bytes 24580

commit v7 on v5

--- a/solution.py
+++ b/solution.py
@@ -50,11 +50,11 @@
     ]
     for load in loads:
         load.start()
-    row, src = iota((1024, 384), 0), iota((1024, 384), 1)
-    i, r, ch = row // 128, (row % 128) // 32, row % 8
+    row, src = iota((1024, 1), 0), iota((1024, 384), 1)
+    i, r, ch = row >> 7, (row >> 5) & 3, row & 7
     channel = jnp.where(ch < 5, ch, jnp.where(ch == 5, 10, jnp.where(ch == 6, 11, 9)))
     pick_main = one_hot(src == channel * 32 + i * 4 + r)
-    pick_aux = one_hot(src == (5 + row % 4) * 32 + i * 4 + r)
+    pick_aux = one_hot(src == (5 + (row & 3)) * 32 + i * 4 + r)
     for load in loads:
         load.wait()
     cells = jnp.concatenate(
@@ -66,14 +66,14 @@
         axis=0,
     )
     main, aux = mm(pick_main, cells), mm(pick_aux, cells)
-    row, col = iota((1024, 256), 0), iota((1024, 256), 1)
-    c, half = (row % 32) // 8, (row % 8) // 4
-    main = jnp.where(col % 4 == c, main, 0.0).astype(BF)
-    aux = jnp.where((col % 4 == c) & (col // 128 == half), aux, 0.0).astype(BF)
+    col = iota((1, 256), 1)
+    c, half = (row >> 3) & 3, (row >> 2) & 1
+    main = jnp.where((col & 3) == c, main, 0.0).astype(BF)
+    aux = jnp.where((col & 3) + 4 * (col >> 7) == c + 4 * half, aux, 0.0).astype(BF)
     j, col = iota((64, 256), 0), iota((64, 256), 1)
-    main = mm_t(one_hot(col // 4 == j), main).astype(BF)
+    main = mm_t(one_hot((col >> 2) == j), main).astype(BF)
     j, col = iota((32, 256), 0), iota((32, 256), 1)
-    aux = mm_t(one_hot((col % 128) // 4 == j), aux).astype(BF)
+    aux = mm_t(one_hot(((col & 127) >> 2) == j), aux).astype(BF)
     for i in range(8):
         own_ref[i, 0:64, :] = main[:, i * 128 : i * 128 + 128]
         own_ref[i, 64:96, :] = aux[:, i * 128 : i * 128 + 128]
@@ -117,13 +117,20 @@
             out_ref[level, :, half * 32 : half * 32 + 32, :] = tile
 
 
-def unpack_far_kernel(after_ref, packed_ref, own_ref, far_ref, low_ref, high_ref):
+def unpack_far_kernel(after_ref, packed_ref, own_ref, far_ref, low_ref, high_ref, ninth):
     del after_ref
     unpack_rows(packed_ref, far_ref)
-    low_ref[:, 0:10] = own_ref[:, :, 0:16, :]
-    low_ref[:, 10:18] = far_ref[:, :, 0:16, :]
-    high_ref[:, 0:10] = own_ref[:, :, 48:64, :]
-    high_ref[:, 10:18] = far_ref[:, :, 48:64, :]
+    for n, (first, inner, out_ref) in enumerate([(0, 8, low_ref), (48, 7, high_ref)]):
+        cols = slice(first, first + 16)
+        edge = jnp.concatenate([own_ref[:, :, cols, :], far_ref[:, :, cols, :]], axis=1).astype(F32)
+        near = edge[:, :, 8 * n : 8 * n + 8, :]
+        out_ref[0:18] = near.reshape(18, 16, 128).astype(BF)
+        for level in range(2):
+            for row in range(18):
+                at = level * 18 + row
+                ninth[n, at : at + 1, :] = edge[level, row, inner : inner + 1, :]
+        ninth[n, 36:48, :] = jnp.zeros((12, 128), F32)
+        out_ref[18:21] = ninth[n].reshape(3, 16, 128).astype(BF)
 
 
 def unpack_far(after, packed, own):
@@ -132,11 +139,12 @@
         unpack_far_kernel,
         out_shape=(
             jax.ShapeDtypeStruct((2, 8, 64, 128), BF),
-            jax.ShapeDtypeStruct((2, 18, 16, 128), BF),
-            jax.ShapeDtypeStruct((2, 18, 16, 128), BF),
+            jax.ShapeDtypeStruct((21, 16, 128), BF),
+            jax.ShapeDtypeStruct((21, 16, 128), BF),
         ),
         in_specs=[pl.BlockSpec(memory_space=pl.ANY)] + [vmem] * 2,
         out_specs=(vmem,) * 3,
+        scratch_shapes=[pltpu.VMEM((2, 48, 128), F32)],
         compiler_params=params(),
         cost_estimate=pl.CostEstimate(flops=10**9, bytes_accessed=10**6, transcendentals=0),
     )(after, packed, own)
@@ -205,7 +213,7 @@
         send_ref, refs = refs[0], refs[1:]
     if leading:
         own_ref, refs = refs[0], refs[1:]
-    wide, gathered, x0, normed, query, keyval, heads, *refs = refs
+    wide, ninth, gathered, x0, normed, query, keyval, heads, *refs = refs
     par = par_ref[0]
     if leading:
         packed, wq, wkv, wo, sems = refs
@@ -222,23 +230,30 @@
     else:
         wq, wkv, wo = wq_ref.at[0], wkv_ref.at[0], wo_ref.at[0]
 
-    def spread(part, to, count, center, low, high):
+    if which == EDGES:
+        for n, side in enumerate((low_ref, high_ref)):
+            ninth[n] = side[18:21].astype(F32).reshape(48, 128)
+
+    def spread(part, to, count, center, first):
         rows = (slice(None), pl.ds(to, count))
-        if which == EDGES:
-            wide[part, *rows, 0:16, :] = low.astype(F32)
-            wide[part, *rows, 16:32, :] = center[:, :, 0:16, :].astype(F32)
-            wide[part, *rows, 64:80, :] = center[:, :, 48:64, :].astype(F32)
-            wide[part, *rows, 80:96, :] = high.astype(F32)
-        else:
+        if which != EDGES:
             wide[part, *rows, 16:80, :] = center.astype(F32)
-
-    sides = [r for r in ((low_ref, high_ref) if which == EDGES else ())]
+            return
+        wide[part, *rows, 16:32, :] = center[:, :, 0:16, :].astype(F32)
+        wide[part, *rows, 64:80, :] = center[:, :, 48:64, :].astype(F32)
+        for n, (side, cols, nine) in enumerate([(low_ref, slice(8, 16), 7), (high_ref, slice(80, 88), 88)]):
+            for level in range(2):
+                pairs = side[pl.ds(level * 9 + first // 2, count // 2)].astype(F32)
+                wide[part, level, pl.ds(to, count), cols, :] = pairs.reshape(count, 8, 128)
+                for row in range(count):
+                    got = ninth[n, pl.ds(level * 18 + first + row, 1), :]
+                    wide[part, level, pl.ds(to + row, 1), nine : nine + 1, :] = got.reshape(1, 1, 128)
+
     if 0 in parts:
-        spread(0, 0, 10, own_ref[...], *([r[:, 0:10] for r in sides] or (None, None)))
+        spread(0, 0, 10, own_ref[...], 0)
     if 1 in parts:
-        spread(1, 2 * par, 8, far_ref[...], *([r[:, 10:18] for r in sides] or (None, None)))
-        beside = pl.ds(8 * par, 2)
-        spread(1, 8 * (1 - par), 2, own_ref[:, beside], *([r[:, beside] for r in sides] or (None, None)))
+        spread(1, 2 * par, 8, far_ref[...], 10)
+        spread(1, 8 * (1 - par), 2, own_ref[:, pl.ds(8 * par, 2)], 8 * par)
     gain = gain_ref[0:1, :]
     half = 1 - par
 
@@ -322,6 +337,7 @@
         outs.append(jax.ShapeDtypeStruct((2, 4, width, D), BF))
     scratch = [
         pltpu.VMEM((2, 2, 10, 96, 128), F32),
+        pltpu.VMEM((2, 48, 128), F32),
         pltpu.VMEM((count, 2, 10, 16, 384), BF),
         pltpu.VMEM((count, 2, 8, 16, D), F32),
         pltpu.VMEM((count, 2, 2, 4, 16, D), BF),

time: 49.7 us -> 49.7 us (level)
  no operation moved by 1% of the time
where the time goes in v7:
time: 49.7 us; the launch traced here: 49.5 us
  Pallas kernels  30.5 us (61%)
  starting transfers between devices  18 us (36%)
  other arithmetic  0.53 us (1%)
    pallas_call x4, Pallas kernels, first_block(): pl.pallas_call(functools.partial(first_kernel, parts, which), out_shape=t...  16.8 us
    ppermute x5, starting transfers between devices, swap(): return lax.ppermute(block, 'lat', pairs)  11.1 us
    pallas_call x1, Pallas kernels, second_block(): pl.pallas_call(second_kernel, out_shape=jax.ShapeDtypeStruct((2, 4, 32, 1...  11 us
    ppermute x2, starting transfers between devices, around(): lax.ppermute(block, 'lon', [(i, (i + distance) % count) for i in range(co...  6.85 us
    pallas_call x1, Pallas kernels, patches(): pl.pallas_call(patch_kernel, out_shape=tuple((jax.ShapeDtypeStruct((n, 96...  2.48 us
  transfers between devices with their start and end apart: 7, of which 0 were waited for; matrix products, arithmetic and copies ran while one was open for 1% of the time, Pallas kernels for 34%

profile of v7, /device:TPU:25, one launch (start us, length us, event | category | flops | bytes accessed | tf_op | source)
XLA Modules:
  0.0 49.5 jit_solution(10911750775368246162)
XLA Ops:
  0.0 0.1 pad_add_fusion.par_ref.refs_0_
  0.1 0.0 copy-start.8
  0.1 0.0 copy-start.7
  0.1 2.5 %shard_map.118 = (bf16[8,96,128]{2,1,0:T(8,128)(2,1)S(1)}, bf16[8,96,128]{2,1,0:T(8,128)(2,1)S(1)}, bf16[1,96,128]{2,1,0:T(8,128)(2,1)S(1)}, bf16[1,96,128]{2,1,0:T(8,128)(2,1)S(1)}) custom-call(s32[2]{0:T(128)S(1)} %pad_add_fusion.par_ref.refs_0_, bf16[2,5,32,256]{3,2,1,0:T(8,128)(2,1)} %atmos_any.1, bf16[32,256]{1,0:T(8,128)(2,1)} %oro_any.1, ...), custom_call_target="tpu_custom_call" | custom-call | flops 1000000000 | bytes 1000000 | tf_op jit(solution)/shard_map/pallas_call | solution.py:87
  2.6 0.8 %collective-permute-start = (bf16[1,96,128]{2,1,0:T(8,128)(2,1)S(1)}, bf16[1,96,128]{2,1,0:T(8,128)(2,1)S(1)}, u32[]{:S(2)}, u32[]{:S(2)}) collective-permute-start(bf16[1,96,128]{2,1,0:T(8,128)(2,1)S(1)} %get-tuple-element.17), channel_id=1, source_target_pairs={{0,16},{16,0},{32,48},{48,32},{64,80},{80,64},{96,112},{112,96},{1... | collective-permute-start | bytes 73736 | tf_op jit(solution)/shard_map/ppermute | solution.py:505
  3.3 4.5 %collective-permute-start.1 = (bf16[1,96,128]{2,1,0:T(8,128)(2,1)S(1)}, bf16[1,96,128]{2,1,0:T(8,128)(2,1)S(1)}, u32[]{:S(2)}, u32[]{:S(2)}) collective-permute-start(bf16[1,96,128]{2,1,0:T(8,128)(2,1)S(1)} %get-tuple-element.19), channel_id=1, source_target_pairs={{16,32},{32,16},{48,64},{64,48},{80,96},{96,80},{112,128},{128,112... | collective-permute-start | bytes 73736 | tf_op jit(solution)/shard_map/ppermute | solution.py:505
  7.9 0.0 copy-done.8
  7.9 0.0 copy-done.7
  7.9 0.2 pad.4
  8.2 0.0 copy-start.5
  8.2 0.0 copy-start.6
  8.2 0.4 fusion
  8.7 0.0 collective-permute-done.after_ref.refs_2_
  8.7 2.5 %collective-permute-start.2 = (bf16[8,96,128]{2,1,0:T(8,128)(2,1)S(1)}, bf16[8,96,128]{2,1,0:T(8,128)(2,1)S(1)}, u32[]{:S(2)}, u32[]{:S(2)}) collective-permute-start(bf16[8,96,128]{2,1,0:T(8,128)(2,1)S(1)} %constant_dynamic-update-slice_fusion), channel_id=1, source_target_pairs={{16,32},{32,16},{48,64},{64,48},{80,96},{96,80},{112,128},{128,112... | collective-permute-start | bytes 589832 | tf_op jit(solution)/shard_map/ppermute | solution.py:505
  11.2 0.0 collective-permute-done.1.refs_3_
  11.2 0.0 copy-done.5
  11.2 0.0 copy-done.6
  11.2 0.0 copy-start.3
  11.2 5.3 %shard_map.119 = (f32[2,8,48,512]{3,2,1,0:T(8,128)S(1)}, bf16[2,4,48,512]{3,2,1,0:T(8,128)(2,1)S(1)}, bf16[2,10,64,128]{3,2,1,0:T(8,128)(2,1)S(1)}) custom-call(bf16[1,96,128]{2,1,0:T(8,128)(2,1)S(1)} %collective-permute-done.after_ref.refs_2_, s32[2]{0:T(128)S(1)} %pad_add_fusion.par_ref.refs_0_, bf16[8,96,128]{2,1,0:T(8,128)(2,1)S(1)} %get-tuple-element.18.refs_1_, ...), custom_call_target="tpu_custom_call" | custom-call | flops 10000000000 | bytes 10000000 | tf_op jit(solution)/shard_map/pallas_call | solution.py:362
  16.5 1.0 %collective-permute-start.5 = (bf16[2,4,48,512]{3,2,1,0:T(8,128)(2,1)S(1)}, bf16[2,4,48,512]{3,2,1,0:T(8,128)(2,1)S(1)}, u32[]{:S(2)}, u32[]{:S(2)}) collective-permute-start(bf16[2,4,48,512]{3,2,1,0:T(8,128)(2,1)S(1)} %get-tuple-element.27), channel_id=1, source_target_pairs={{0,16},{16,0},{32,48},{48,32},{64,80},{80,64},{96,112},{112,96},{1... | collective-permute-start | bytes 1179656 | tf_op jit(solution)/shard_map/ppermute | solution.py:505
  17.5 0.0 collective-permute-done.2.packed_ref
  17.5 0.0 copy-start.1
  17.5 0.0 copy-start.2
  17.5 0.3 shard_map.120
  17.8 1.7 %collective-permute-start.3 = (bf16[21,16,128]{2,1,0:T(8,128)(2,1)S(1)}, bf16[21,16,128]{2,1,0:T(8,128)(2,1)S(1)}, u32[]{:S(2)}, u32[]{:S(2)}) collective-permute-start(bf16[21,16,128]{2,1,0:T(8,128)(2,1)S(1)} %get-tuple-element.24), channel_id=1, source_target_pairs={{0,1},{1,2},{2,3},{3,4},{4,5},{5,6},{6,7},{7,8},{8,9},{9,10},{10,1... | collective-permute-start | bytes 258056 | tf_op jit(solution)/shard_map/ppermute | solution.py:510
  19.5 5.1 %collective-permute-start.4 = (bf16[21,16,128]{2,1,0:T(8,128)(2,1)S(1)}, bf16[21,16,128]{2,1,0:T(8,128)(2,1)S(1)}, u32[]{:S(2)}, u32[]{:S(2)}) collective-permute-start(bf16[21,16,128]{2,1,0:T(8,128)(2,1)S(1)} %get-tuple-element.25), channel_id=1, source_target_pairs={{0,15},{1,0},{2,1},{3,2},{4,3},{5,4},{6,5},{7,6},{8,7},{9,8},{10,9... | collective-permute-start | bytes 258056 | tf_op jit(solution)/shard_map/ppermute | solution.py:510
  24.7 0.0 copy-done.3
  24.7 0.0 copy-done.1
  24.7 0.0 copy-done.2
  24.7 4.4 %shard_map.121.after_ref.outer_mid = f32[2,4,48,512]{3,2,1,0:T(8,128)S(1)} custom-call(f32[2,8,48,512]{3,2,1,0:T(8,128)S(1)} %get-tuple-element.20.after_ref.own_mid, s32[2]{0:T(128)S(1)} %pad_add_fusion.par_ref.refs_0_, bf16[2,10,64,128]{3,2,1,0:T(8,128)(2,1)S(1)} %get-tuple-element.21.own_ref.refs_1_, ...), custom_call_target="tpu_custom_call" | custom-call | flops 10000000000 | bytes 10000000 | tf_op jit(solution)/shard_map/pallas_call | solution.py:362
  29.1 0.0 collective-permute-done.3.refs_2_.refs_3_
  29.1 0.0 collective-permute-done.4.refs_3_.refs_4_
  29.1 3.6 %shard_map.122 = (f32[2,8,32,512]{3,2,1,0:T(8,128)S(1)}, bf16[2,4,32,512]{3,2,1,0:T(8,128)(2,1)S(1)}) custom-call(f32[2,4,48,512]{3,2,1,0:T(8,128)S(1)} %shard_map.121.after_ref.outer_mid, s32[2]{0:T(128)S(1)} %pad_add_fusion.par_ref.refs_0_, bf16[2,10,64,128]{3,2,1,0:T(8,128)(2,1)S(1)} %get-tuple-element.21.own_ref.refs_1_, ...), custom_call_target="tpu_custom_call" | custom-call | flops 10000000000 | bytes 10000000 | tf_op jit(solution)/shard_map/pallas_call | solution.py:362
  32.7 2.3 %collective-permute-start.6 = (bf16[2,4,32,512]{3,2,1,0:T(8,128)(2,1)S(1)}, bf16[2,4,32,512]{3,2,1,0:T(8,128)(2,1)S(1)}, u32[]{:S(2)}, u32[]{:S(2)}) collective-permute-start(bf16[2,4,32,512]{3,2,1,0:T(8,128)(2,1)S(1)} %get-tuple-element.28), channel_id=1, source_target_pairs={{0,16},{16,0},{32,48},{48,32},{64,80},{80,64},{96,112},{112,96},{1... | collective-permute-start | bytes 786440 | tf_op jit(solution)/shard_map/ppermute | solution.py:505
  35.1 0.0 copy-start
  35.1 0.0 copy-start.4
  35.1 3.4 %shard_map.123.outer_edge = f32[2,4,32,512]{3,2,1,0:T(8,128)S(1)} custom-call(f32[2,8,32,512]{3,2,1,0:T(8,128)S(1)} %get-tuple-element.26.after_ref.own_edge, s32[2]{0:T(128)S(1)} %pad_add_fusion.par_ref.refs_0_, bf16[2,10,64,128]{3,2,1,0:T(8,128)(2,1)S(1)} %get-tuple-element.21.own_ref.refs_1_, bf16[2,8,64,128]{3,2,1,0:T(8,128)(2,1)S(1)} %get-tuple-element.23.refs_2_, ...), custom_call_target="tpu_custom_call" | custom-call | flops 10000000000 | bytes 10000000 | tf_op jit(solution)/shard_map/pallas_call | solution.py:362
  38.5 0.0 collective-permute-done.5.near_mid_ref
  38.5 0.0 collective-permute-done.6.near_edge_ref
  38.5 0.0 copy-done
  38.5 0.0 copy-done.4
  38.6 11.0 %shard_map.124 = bf16[2,4,32,1024]{3,2,1,0:T(8,128)(2,1)} custom-call(s32[2]{0:T(128)S(1)} %pad_add_fusion.par_ref.refs_0_, f32[2,8,48,512]{3,2,1,0:T(8,128)S(1)} %get-tuple-element.20.after_ref.own_mid, f32[2,4,48,512]{3,2,1,0:T(8,128)S(1)} %shard_map.121.after_ref.outer_mid, f32[2,8,32,512]{3,2,1,0:T(8,128)S(1)} %get-tuple-element.26.after_ref.own_edge, ...), custom_call_target="tpu_custom_call" | custom-call | flops 10000000000 | bytes 10000000 | tf_op jit(solution)/shard_map/pallas_call | solution.py:468
  (4 shorter events, 0.0 us)
Async XLA Ops:
  0.1 7.8 %copy-start.8 = (f32[512]{0:T(512)S(1)}, f32[512]{0:T(512)}, u32[]{:S(2)}) copy-start(f32[512]{0:T(512)} %param.17) | copy-start | bytes 6148
  0.1 7.9 %copy-start.7 = (bf16[12,12,6,512]{3,2,1,0:T(8,128)(2,1)S(1)}, bf16[12,12,6,512]{3,2,1,0:T(8,128)(2,1)}, u32[]{:S(2)}) copy-start(bf16[12,12,6,512]{3,2,1,0:T(8,128)(2,1)} %param.15) | copy-start | bytes 2654212
  2.6 6.1 %collective-permute-start = (bf16[1,96,128]{2,1,0:T(8,128)(2,1)S(1)}, bf16[1,96,128]{2,1,0:T(8,128)(2,1)S(1)}, u32[]{:S(2)}, u32[]{:S(2)}) collective-permute-start(bf16[1,96,128]{2,1,0:T(8,128)(2,1)S(1)} %get-tuple-element.17), channel_id=1, source_target_pairs={{0,16},{16,0},{32,48},{48,32},{64,80},{80,64},{96,112},{112,96},{1... | collective-permute-start | bytes 73736 | tf_op jit(solution)/shard_map/ppermute | solution.py:505
  3.3 7.9 %collective-permute-start.1 = (bf16[1,96,128]{2,1,0:T(8,128)(2,1)S(1)}, bf16[1,96,128]{2,1,0:T(8,128)(2,1)S(1)}, u32[]{:S(2)}, u32[]{:S(2)}) collective-permute-start(bf16[1,96,128]{2,1,0:T(8,128)(2,1)S(1)} %get-tuple-element.19), channel_id=1, source_target_pairs={{16,32},{32,16},{48,64},{64,48},{80,96},{96,80},{112,128},{128,112... | collective-permute-start | bytes 73736 | tf_op jit(solution)/shard_map/ppermute | solution.py:505
  8.2 3.0 %copy-start.5 = (f32[2,512]{1,0:T(2,128)S(1)}, f32[2,512]{1,0:T(2,128)}, u32[]{:S(2)}) copy-start(f32[2,512]{1,0:T(2,128)} %refs_6_.7) | copy-start | bytes 12292
  8.2 3.0 %copy-start.6 = (f32[2,512]{1,0:T(2,128)S(1)}, f32[2,512]{1,0:T(2,128)}, u32[]{:S(2)}) copy-start(f32[2,512]{1,0:T(2,128)} %gain_ref.1) | copy-start | bytes 12292
  8.7 8.9 %collective-permute-start.2 = (bf16[8,96,128]{2,1,0:T(8,128)(2,1)S(1)}, bf16[8,96,128]{2,1,0:T(8,128)(2,1)S(1)}, u32[]{:S(2)}, u32[]{:S(2)}) collective-permute-start(bf16[8,96,128]{2,1,0:T(8,128)(2,1)S(1)} %constant_dynamic-update-slice_fusion), channel_id=1, source_target_pairs={{16,32},{32,16},{48,64},{64,48},{80,96},{96,80},{112,128},{128,112... | collective-permute-start | bytes 589832 | tf_op jit(solution)/shard_map/ppermute | solution.py:505
  11.2 13.4 %copy-start.3 = (bf16[2,512,512]{2,1,0:T(8,128)(2,1)S(1)}, bf16[2,512,512]{2,1,0:T(8,128)(2,1)}, u32[]{:S(2)}) copy-start(bf16[2,512,512]{2,1,0:T(8,128)(2,1)} %wo_ref.1) | copy-start | bytes 3145732
  16.5 22.0 %collective-permute-start.5 = (bf16[2,4,48,512]{3,2,1,0:T(8,128)(2,1)S(1)}, bf16[2,4,48,512]{3,2,1,0:T(8,128)(2,1)S(1)}, u32[]{:S(2)}, u32[]{:S(2)}) collective-permute-start(bf16[2,4,48,512]{3,2,1,0:T(8,128)(2,1)S(1)} %get-tuple-element.27), channel_id=1, source_target_pairs={{0,16},{16,0},{32,48},{48,32},{64,80},{80,64},{96,112},{112,96},{1... | collective-permute-start | bytes 1179656 | tf_op jit(solution)/shard_map/ppermute | solution.py:505
  17.5 7.1 %copy-start.1 = (bf16[2,512,1024]{2,1,0:T(8,128)(2,1)S(1)}, bf16[2,512,1024]{2,1,0:T(8,128)(2,1)}, u32[]{:S(2)}) copy-start(bf16[2,512,1024]{2,1,0:T(8,128)(2,1)} %wkv_ref.1) | copy-start | bytes 6291460
  17.5 7.1 %copy-start.2 = (bf16[2,512,512]{2,1,0:T(8,128)(2,1)S(1)}, bf16[2,512,512]{2,1,0:T(8,128)(2,1)}, u32[]{:S(2)}) copy-start(bf16[2,512,512]{2,1,0:T(8,128)(2,1)} %wq_ref.1) | copy-start | bytes 3145732
  17.8 11.3 %collective-permute-start.3 = (bf16[21,16,128]{2,1,0:T(8,128)(2,1)S(1)}, bf16[21,16,128]{2,1,0:T(8,128)(2,1)S(1)}, u32[]{:S(2)}, u32[]{:S(2)}) collective-permute-start(bf16[21,16,128]{2,1,0:T(8,128)(2,1)S(1)} %get-tuple-element.24), channel_id=1, source_target_pairs={{0,1},{1,2},{2,3},{3,4},{4,5},{5,6},{6,7},{7,8},{8,9},{9,10},{10,1... | collective-permute-start | bytes 258056 | tf_op jit(solution)/shard_map/ppermute | solution.py:510
  19.5 9.6 %collective-permute-start.4 = (bf16[21,16,128]{2,1,0:T(8,128)(2,1)S(1)}, bf16[21,16,128]{2,1,0:T(8,128)(2,1)S(1)}, u32[]{:S(2)}, u32[]{:S(2)}) collective-permute-start(bf16[21,16,128]{2,1,0:T(8,128)(2,1)S(1)} %get-tuple-element.25), channel_id=1, source_target_pairs={{0,15},{1,0},{2,1},{3,2},{4,3},{5,4},{6,5},{7,6},{8,7},{9,8},{10,9... | collective-permute-start | bytes 258056 | tf_op jit(solution)/shard_map/ppermute | solution.py:510
  32.7 5.8 %collective-permute-start.6 = (bf16[2,4,32,512]{3,2,1,0:T(8,128)(2,1)S(1)}, bf16[2,4,32,512]{3,2,1,0:T(8,128)(2,1)S(1)}, u32[]{:S(2)}, u32[]{:S(2)}) collective-permute-start(bf16[2,4,32,512]{3,2,1,0:T(8,128)(2,1)S(1)} %get-tuple-element.28), channel_id=1, source_target_pairs={{0,16},{16,0},{32,48},{48,32},{64,80},{80,64},{96,112},{112,96},{1... | collective-permute-start | bytes 786440 | tf_op jit(solution)/shard_map/ppermute | solution.py:505
  35.1 3.5 %copy-start = (bf16[2048,1024]{1,0:T(8,128)(2,1)S(1)}, bf16[2048,1024]{1,0:T(8,128)(2,1)}, u32[]{:S(2)}) copy-start(bf16[2048,1024]{1,0:T(8,128)(2,1)} %wm_ref.1) | copy-start | bytes 12582916
  35.1 3.5 %copy-start.4 = (f32[2048]{0:T(1024)S(1)}, f32[2048]{0:T(1024)}, u32[]{:S(2)}) copy-start(f32[2048]{0:T(1024)} %param.22) | copy-start | bytes 24580

commit v8 on v7

--- a/solution.py
+++ b/solution.py
@@ -166,8 +166,9 @@
 
 def attend(q, k, v, bias):
     left = iota((128, 128), 1) < HEAD_DIM
-    ones_left, ones_right = one_hot(left), one_hot(~left)
+    ones_left, ones_right, ones = one_hot(left), one_hot(~left), jnp.ones((128, 128), BF)
     zero = jnp.zeros((128, 128), BF)
+    n = q.shape[0]
     out = []
     for pair in range(4):
         at = slice(pair * 128, pair * 128 + 128)
@@ -179,6 +180,13 @@
         s0, s1 = s[:, :128], s[:, 128:]
         p0 = jnp.exp2(s0 - jnp.max(s0, axis=-1, keepdims=True))
         p1 = jnp.exp2(s1 - jnp.max(s1, axis=-1, keepdims=True))
+        if n == 64:
+            p = jnp.concatenate([p0.astype(BF), p1.astype(BF)], axis=0)
+            o = mm(p, jnp.concatenate([vp, ones], axis=1))
+            values = jnp.where(left[:n], o[:n, :128], o[n:, :128])
+            total = jnp.where(left[:n], o[:n, 128:], o[n:, 128:])
+            out.append((values / total).astype(BF))
+            continue
         p = jnp.concatenate([p0, p1], axis=1).astype(BF)
         vals = jnp.concatenate(
             [

time: 49.7 us -> 49 us (0.986)
  Pallas kernels: 30.5 us -> 29.8 us
    pallas_call x1, Pallas kernels: 11 us -> 10.4 us  [second_block(): pl.pallas_call(second_kernel, out_shape=jax.ShapeDtypeStruct((2, 4, 32, 1...]
  transfers between devices with their start and end apart: 7 -> 7, of which waited for: 0 -> 0; matrix products, arithmetic and copies ran while one was open for 1% -> 1% of each run, Pallas kernels for 34% -> 35%
where the time goes in v8:
time: 49 us; the launch traced here: 48.8 us
  Pallas kernels  29.8 us (61%)
  starting transfers between devices  18 us (37%)
  other arithmetic  0.53 us (1%)
    pallas_call x4, Pallas kernels, first_block(): pl.pallas_call(functools.partial(first_kernel, parts, which), out_shape=t...  16.6 us
    ppermute x5, starting transfers between devices, swap(): return lax.ppermute(block, 'lat', pairs)  11.1 us
    pallas_call x1, Pallas kernels, second_block(): pl.pallas_call(second_kernel, out_shape=jax.ShapeDtypeStruct((2, 4, 32, 1...  10.4 us
    ppermute x2, starting transfers between devices, around(): lax.ppermute(block, 'lon', [(i, (i + distance) % count) for i in range(co...  6.85 us
    pallas_call x1, Pallas kernels, patches(): pl.pallas_call(patch_kernel, out_shape=tuple((jax.ShapeDtypeStruct((n, 96...  2.48 us
  transfers between devices with their start and end apart: 7, of which 0 were waited for; matrix products, arithmetic and copies ran while one was open for 1% of the time, Pallas kernels for 35%

profile of v8, /device:TPU:25, one launch (start us, length us, event | category | flops | bytes accessed | tf_op | source)
XLA Modules:
  0.0 48.8 jit_solution(1636272782036544728)
XLA Ops:
  0.0 0.1 pad_add_fusion.par_ref.refs_0_
  0.1 0.0 copy-start.8
  0.1 0.0 copy-start.7
  0.1 2.5 %shard_map.118 = (bf16[8,96,128]{2,1,0:T(8,128)(2,1)S(1)}, bf16[8,96,128]{2,1,0:T(8,128)(2,1)S(1)}, bf16[1,96,128]{2,1,0:T(8,128)(2,1)S(1)}, bf16[1,96,128]{2,1,0:T(8,128)(2,1)S(1)}) custom-call(s32[2]{0:T(128)S(1)} %pad_add_fusion.par_ref.refs_0_, bf16[2,5,32,256]{3,2,1,0:T(8,128)(2,1)} %atmos_any.1, bf16[32,256]{1,0:T(8,128)(2,1)} %oro_any.1, ...), custom_call_target="tpu_custom_call" | custom-call | flops 1000000000 | bytes 1000000 | tf_op jit(solution)/shard_map/pallas_call | solution.py:87
  2.6 0.8 %collective-permute-start = (bf16[1,96,128]{2,1,0:T(8,128)(2,1)S(1)}, bf16[1,96,128]{2,1,0:T(8,128)(2,1)S(1)}, u32[]{:S(2)}, u32[]{:S(2)}) collective-permute-start(bf16[1,96,128]{2,1,0:T(8,128)(2,1)S(1)} %get-tuple-element.17), channel_id=1, source_target_pairs={{0,16},{16,0},{32,48},{48,32},{64,80},{80,64},{96,112},{112,96},{1... | collective-permute-start | bytes 73736 | tf_op jit(solution)/shard_map/ppermute | solution.py:513
  3.3 4.5 %collective-permute-start.1 = (bf16[1,96,128]{2,1,0:T(8,128)(2,1)S(1)}, bf16[1,96,128]{2,1,0:T(8,128)(2,1)S(1)}, u32[]{:S(2)}, u32[]{:S(2)}) collective-permute-start(bf16[1,96,128]{2,1,0:T(8,128)(2,1)S(1)} %get-tuple-element.19), channel_id=1, source_target_pairs={{16,32},{32,16},{48,64},{64,48},{80,96},{96,80},{112,128},{128,112... | collective-permute-start | bytes 73736 | tf_op jit(solution)/shard_map/ppermute | solution.py:513
  7.9 0.0 copy-done.8
  7.9 0.0 copy-done.7
  7.9 0.2 pad.4
  8.2 0.0 copy-start.5
  8.2 0.0 copy-start.6
  8.2 0.4 fusion
  8.7 0.0 collective-permute-done.after_ref.refs_2_
  8.7 2.5 %collective-permute-start.2 = (bf16[8,96,128]{2,1,0:T(8,128)(2,1)S(1)}, bf16[8,96,128]{2,1,0:T(8,128)(2,1)S(1)}, u32[]{:S(2)}, u32[]{:S(2)}) collective-permute-start(bf16[8,96,128]{2,1,0:T(8,128)(2,1)S(1)} %constant_dynamic-update-slice_fusion), channel_id=1, source_target_pairs={{16,32},{32,16},{48,64},{64,48},{80,96},{96,80},{112,128},{128,112... | collective-permute-start | bytes 589832 | tf_op jit(solution)/shard_map/ppermute | solution.py:513
  11.2 0.0 collective-permute-done.1.refs_3_
  11.2 0.0 copy-done.5
  11.2 0.0 copy-done.6
  11.2 0.0 copy-start.3
  11.2 5.3 %shard_map.119 = (f32[2,8,48,512]{3,2,1,0:T(8,128)S(1)}, bf16[2,4,48,512]{3,2,1,0:T(8,128)(2,1)S(1)}, bf16[2,10,64,128]{3,2,1,0:T(8,128)(2,1)S(1)}) custom-call(bf16[1,96,128]{2,1,0:T(8,128)(2,1)S(1)} %collective-permute-done.after_ref.refs_2_, s32[2]{0:T(128)S(1)} %pad_add_fusion.par_ref.refs_0_, bf16[8,96,128]{2,1,0:T(8,128)(2,1)S(1)} %get-tuple-element.18.refs_1_, ...), custom_call_target="tpu_custom_call" | custom-call | flops 10000000000 | bytes 10000000 | tf_op jit(solution)/shard_map/pallas_call | solution.py:370
  16.5 1.0 %collective-permute-start.5 = (bf16[2,4,48,512]{3,2,1,0:T(8,128)(2,1)S(1)}, bf16[2,4,48,512]{3,2,1,0:T(8,128)(2,1)S(1)}, u32[]{:S(2)}, u32[]{:S(2)}) collective-permute-start(bf16[2,4,48,512]{3,2,1,0:T(8,128)(2,1)S(1)} %get-tuple-element.27), channel_id=1, source_target_pairs={{0,16},{16,0},{32,48},{48,32},{64,80},{80,64},{96,112},{112,96},{1... | collective-permute-start | bytes 1179656 | tf_op jit(solution)/shard_map/ppermute | solution.py:513
  17.5 0.0 collective-permute-done.2.packed_ref
  17.5 0.0 copy-start.1
  17.5 0.0 copy-start.2
  17.5 0.3 shard_map.120
  17.8 1.7 %collective-permute-start.3 = (bf16[21,16,128]{2,1,0:T(8,128)(2,1)S(1)}, bf16[21,16,128]{2,1,0:T(8,128)(2,1)S(1)}, u32[]{:S(2)}, u32[]{:S(2)}) collective-permute-start(bf16[21,16,128]{2,1,0:T(8,128)(2,1)S(1)} %get-tuple-element.24), channel_id=1, source_target_pairs={{0,1},{1,2},{2,3},{3,4},{4,5},{5,6},{6,7},{7,8},{8,9},{9,10},{10,1... | collective-permute-start | bytes 258056 | tf_op jit(solution)/shard_map/ppermute | solution.py:518
  19.5 5.1 %collective-permute-start.4 = (bf16[21,16,128]{2,1,0:T(8,128)(2,1)S(1)}, bf16[21,16,128]{2,1,0:T(8,128)(2,1)S(1)}, u32[]{:S(2)}, u32[]{:S(2)}) collective-permute-start(bf16[21,16,128]{2,1,0:T(8,128)(2,1)S(1)} %get-tuple-element.25), channel_id=1, source_target_pairs={{0,15},{1,0},{2,1},{3,2},{4,3},{5,4},{6,5},{7,6},{8,7},{9,8},{10,9... | collective-permute-start | bytes 258056 | tf_op jit(solution)/shard_map/ppermute | solution.py:518
  24.7 0.0 copy-done.3
  24.7 0.0 copy-done.1
  24.7 0.0 copy-done.2
  24.7 4.3 %shard_map.121.after_ref.outer_mid = f32[2,4,48,512]{3,2,1,0:T(8,128)S(1)} custom-call(f32[2,8,48,512]{3,2,1,0:T(8,128)S(1)} %get-tuple-element.20.after_ref.own_mid, s32[2]{0:T(128)S(1)} %pad_add_fusion.par_ref.refs_0_, bf16[2,10,64,128]{3,2,1,0:T(8,128)(2,1)S(1)} %get-tuple-element.21.own_ref.refs_1_, ...), custom_call_target="tpu_custom_call" | custom-call | flops 10000000000 | bytes 10000000 | tf_op jit(solution)/shard_map/pallas_call | solution.py:370
  29.0 0.0 collective-permute-done.3.refs_2_.refs_3_
  29.0 0.0 collective-permute-done.4.refs_3_.refs_4_
  29.0 3.6 %shard_map.122 = (f32[2,8,32,512]{3,2,1,0:T(8,128)S(1)}, bf16[2,4,32,512]{3,2,1,0:T(8,128)(2,1)S(1)}) custom-call(f32[2,4,48,512]{3,2,1,0:T(8,128)S(1)} %shard_map.121.after_ref.outer_mid, s32[2]{0:T(128)S(1)} %pad_add_fusion.par_ref.refs_0_, bf16[2,10,64,128]{3,2,1,0:T(8,128)(2,1)S(1)} %get-tuple-element.21.own_ref.refs_1_, ...), custom_call_target="tpu_custom_call" | custom-call | flops 10000000000 | bytes 10000000 | tf_op jit(solution)/shard_map/pallas_call | solution.py:370
  32.6 2.3 %collective-permute-start.6 = (bf16[2,4,32,512]{3,2,1,0:T(8,128)(2,1)S(1)}, bf16[2,4,32,512]{3,2,1,0:T(8,128)(2,1)S(1)}, u32[]{:S(2)}, u32[]{:S(2)}) collective-permute-start(bf16[2,4,32,512]{3,2,1,0:T(8,128)(2,1)S(1)} %get-tuple-element.28), channel_id=1, source_target_pairs={{0,16},{16,0},{32,48},{48,32},{64,80},{80,64},{96,112},{112,96},{1... | collective-permute-start | bytes 786440 | tf_op jit(solution)/shard_map/ppermute | solution.py:513
  35.0 0.0 copy-start
  35.0 0.0 copy-start.4
  35.0 3.4 %shard_map.123.outer_edge = f32[2,4,32,512]{3,2,1,0:T(8,128)S(1)} custom-call(f32[2,8,32,512]{3,2,1,0:T(8,128)S(1)} %get-tuple-element.26.after_ref.own_edge, s32[2]{0:T(128)S(1)} %pad_add_fusion.par_ref.refs_0_, bf16[2,10,64,128]{3,2,1,0:T(8,128)(2,1)S(1)} %get-tuple-element.21.own_ref.refs_1_, bf16[2,8,64,128]{3,2,1,0:T(8,128)(2,1)S(1)} %get-tuple-element.23.refs_2_, ...), custom_call_target="tpu_custom_call" | custom-call | flops 10000000000 | bytes 10000000 | tf_op jit(solution)/shard_map/pallas_call | solution.py:370
  38.3 0.0 collective-permute-done.5.near_mid_ref
  38.3 0.0 collective-permute-done.6.near_edge_ref
  38.4 0.0 copy-done
  38.4 0.0 copy-done.4
  38.4 10.4 %shard_map.124 = bf16[2,4,32,1024]{3,2,1,0:T(8,128)(2,1)} custom-call(s32[2]{0:T(128)S(1)} %pad_add_fusion.par_ref.refs_0_, f32[2,8,48,512]{3,2,1,0:T(8,128)S(1)} %get-tuple-element.20.after_ref.own_mid, f32[2,4,48,512]{3,2,1,0:T(8,128)S(1)} %shard_map.121.after_ref.outer_mid, f32[2,8,32,512]{3,2,1,0:T(8,128)S(1)} %get-tuple-element.26.after_ref.own_edge, ...), custom_call_target="tpu_custom_call" | custom-call | flops 10000000000 | bytes 10000000 | tf_op jit(solution)/shard_map/pallas_call | solution.py:476
  (4 shorter events, 0.0 us)
Async XLA Ops:
  0.1 7.8 %copy-start.8 = (f32[512]{0:T(512)S(1)}, f32[512]{0:T(512)}, u32[]{:S(2)}) copy-start(f32[512]{0:T(512)} %param.17) | copy-start | bytes 6148
  0.1 7.9 %copy-start.7 = (bf16[12,12,6,512]{3,2,1,0:T(8,128)(2,1)S(1)}, bf16[12,12,6,512]{3,2,1,0:T(8,128)(2,1)}, u32[]{:S(2)}) copy-start(bf16[12,12,6,512]{3,2,1,0:T(8,128)(2,1)} %param.15) | copy-start | bytes 2654212
  2.6 6.1 %collective-permute-start = (bf16[1,96,128]{2,1,0:T(8,128)(2,1)S(1)}, bf16[1,96,128]{2,1,0:T(8,128)(2,1)S(1)}, u32[]{:S(2)}, u32[]{:S(2)}) collective-permute-start(bf16[1,96,128]{2,1,0:T(8,128)(2,1)S(1)} %get-tuple-element.17), channel_id=1, source_target_pairs={{0,16},{16,0},{32,48},{48,32},{64,80},{80,64},{96,112},{112,96},{1... | collective-permute-start | bytes 73736 | tf_op jit(solution)/shard_map/ppermute | solution.py:513
  3.3 7.9 %collective-permute-start.1 = (bf16[1,96,128]{2,1,0:T(8,128)(2,1)S(1)}, bf16[1,96,128]{2,1,0:T(8,128)(2,1)S(1)}, u32[]{:S(2)}, u32[]{:S(2)}) collective-permute-start(bf16[1,96,128]{2,1,0:T(8,128)(2,1)S(1)} %get-tuple-element.19), channel_id=1, source_target_pairs={{16,32},{32,16},{48,64},{64,48},{80,96},{96,80},{112,128},{128,112... | collective-permute-start | bytes 73736 | tf_op jit(solution)/shard_map/ppermute | solution.py:513
  8.2 3.0 %copy-start.5 = (f32[2,512]{1,0:T(2,128)S(1)}, f32[2,512]{1,0:T(2,128)}, u32[]{:S(2)}) copy-start(f32[2,512]{1,0:T(2,128)} %refs_6_.7) | copy-start | bytes 12292
  8.2 3.0 %copy-start.6 = (f32[2,512]{1,0:T(2,128)S(1)}, f32[2,512]{1,0:T(2,128)}, u32[]{:S(2)}) copy-start(f32[2,512]{1,0:T(2,128)} %gain_ref.1) | copy-start | bytes 12292
  8.7 8.9 %collective-permute-start.2 = (bf16[8,96,128]{2,1,0:T(8,128)(2,1)S(1)}, bf16[8,96,128]{2,1,0:T(8,128)(2,1)S(1)}, u32[]{:S(2)}, u32[]{:S(2)}) collective-permute-start(bf16[8,96,128]{2,1,0:T(8,128)(2,1)S(1)} %constant_dynamic-update-slice_fusion), channel_id=1, source_target_pairs={{16,32},{32,16},{48,64},{64,48},{80,96},{96,80},{112,128},{128,112... | collective-permute-start | bytes 589832 | tf_op jit(solution)/shard_map/ppermute | solution.py:513
  11.2 13.4 %copy-start.3 = (bf16[2,512,512]{2,1,0:T(8,128)(2,1)S(1)}, bf16[2,512,512]{2,1,0:T(8,128)(2,1)}, u32[]{:S(2)}) copy-start(bf16[2,512,512]{2,1,0:T(8,128)(2,1)} %wo_ref.1) | copy-start | bytes 3145732
  16.5 21.8 %collective-permute-start.5 = (bf16[2,4,48,512]{3,2,1,0:T(8,128)(2,1)S(1)}, bf16[2,4,48,512]{3,2,1,0:T(8,128)(2,1)S(1)}, u32[]{:S(2)}, u32[]{:S(2)}) collective-permute-start(bf16[2,4,48,512]{3,2,1,0:T(8,128)(2,1)S(1)} %get-tuple-element.27), channel_id=1, source_target_pairs={{0,16},{16,0},{32,48},{48,32},{64,80},{80,64},{96,112},{112,96},{1... | collective-permute-start | bytes 1179656 | tf_op jit(solution)/shard_map/ppermute | solution.py:513
  17.5 7.1 %copy-start.1 = (bf16[2,512,1024]{2,1,0:T(8,128)(2,1)S(1)}, bf16[2,512,1024]{2,1,0:T(8,128)(2,1)}, u32[]{:S(2)}) copy-start(bf16[2,512,1024]{2,1,0:T(8,128)(2,1)} %wkv_ref.1) | copy-start | bytes 6291460
  17.5 7.1 %copy-start.2 = (bf16[2,512,512]{2,1,0:T(8,128)(2,1)S(1)}, bf16[2,512,512]{2,1,0:T(8,128)(2,1)}, u32[]{:S(2)}) copy-start(bf16[2,512,512]{2,1,0:T(8,128)(2,1)} %wq_ref.1) | copy-start | bytes 3145732
  17.8 11.2 %collective-permute-start.3 = (bf16[21,16,128]{2,1,0:T(8,128)(2,1)S(1)}, bf16[21,16,128]{2,1,0:T(8,128)(2,1)S(1)}, u32[]{:S(2)}, u32[]{:S(2)}) collective-permute-start(bf16[21,16,128]{2,1,0:T(8,128)(2,1)S(1)} %get-tuple-element.24), channel_id=1, source_target_pairs={{0,1},{1,2},{2,3},{3,4},{4,5},{5,6},{6,7},{7,8},{8,9},{9,10},{10,1... | collective-permute-start | bytes 258056 | tf_op jit(solution)/shard_map/ppermute | solution.py:518
  19.5 9.5 %collective-permute-start.4 = (bf16[21,16,128]{2,1,0:T(8,128)(2,1)S(1)}, bf16[21,16,128]{2,1,0:T(8,128)(2,1)S(1)}, u32[]{:S(2)}, u32[]{:S(2)}) collective-permute-start(bf16[21,16,128]{2,1,0:T(8,128)(2,1)S(1)} %get-tuple-element.25), channel_id=1, source_target_pairs={{0,15},{1,0},{2,1},{3,2},{4,3},{5,4},{6,5},{7,6},{8,7},{9,8},{10,9... | collective-permute-start | bytes 258056 | tf_op jit(solution)/shard_map/ppermute | solution.py:518
  32.6 5.7 %collective-permute-start.6 = (bf16[2,4,32,512]{3,2,1,0:T(8,128)(2,1)S(1)}, bf16[2,4,32,512]{3,2,1,0:T(8,128)(2,1)S(1)}, u32[]{:S(2)}, u32[]{:S(2)}) collective-permute-start(bf16[2,4,32,512]{3,2,1,0:T(8,128)(2,1)S(1)} %get-tuple-element.28), channel_id=1, source_target_pairs={{0,16},{16,0},{32,48},{48,32},{64,80},{80,64},{96,112},{112,96},{1... | collective-permute-start | bytes 786440 | tf_op jit(solution)/shard_map/ppermute | solution.py:513
  35.0 3.4 %copy-start = (bf16[2048,1024]{1,0:T(8,128)(2,1)S(1)}, bf16[2048,1024]{1,0:T(8,128)(2,1)}, u32[]{:S(2)}) copy-start(bf16[2048,1024]{1,0:T(8,128)(2,1)} %wm_ref.1) | copy-start | bytes 12582916
  35.0 3.4 %copy-start.4 = (f32[2048]{0:T(1024)S(1)}, f32[2048]{0:T(1024)}, u32[]{:S(2)}) copy-start(f32[2048]{0:T(1024)} %param.22) | copy-start | bytes 24580

commit v9 on v8

--- a/solution.py
+++ b/solution.py
@@ -215,6 +215,8 @@
         far_ref, refs = refs[0], refs[1:]
     if which == EDGES:
         low_ref, high_ref, refs = refs[0], refs[1], refs[2:]
+        if 0 in parts:
+            middle_ref, refs = refs[0], refs[1:]
     wemb_ref, lev_ref, gain_ref, wq_ref, wkv_ref, wo_ref, *refs = refs
     x1_refs, refs = refs[: len(parts)], refs[len(parts) :]
     if 0 in parts:
@@ -333,7 +335,12 @@
 
     pipelined([embed, norm, project, attention, project_out], list(parts))
     if 0 in parts:
-        send_ref[...] = x1_refs[0][:, 4:8].astype(BF)
+        if which == EDGES:
+            send_ref[:, :, 0:16, :] = x1_refs[0][:, 4:8, 0:16, :].astype(BF)
+            send_ref[:, :, 16:64, :] = middle_ref[...]
+            send_ref[:, :, 64:80, :] = x1_refs[0][:, 4:8, 16:32, :].astype(BF)
+        else:
+            send_ref[...] = x1_refs[0][:, 4:8].astype(BF)
 
 
 def first_block(parts, which, after, par, patch_arrays, wemb, level_embed, norm_gain, w_query, w_keyval, w_out):
@@ -342,7 +349,7 @@
     leading = parts == (0,) and which == MIDDLE
     outs = [jax.ShapeDtypeStruct((2, 4 if part else 8, width, D), F32) for part in parts]
     if 0 in parts:
-        outs.append(jax.ShapeDtypeStruct((2, 4, width, D), BF))
+        outs.append(jax.ShapeDtypeStruct((2, 4, 80 if which == EDGES else width, D), BF))
     scratch = [
         pltpu.VMEM((2, 2, 10, 96, 128), F32),
         pltpu.VMEM((2, 48, 128), F32),
@@ -383,15 +390,13 @@
 
 
 def second_kernel(
-    par_ref, own_mid, outer_mid, own_edge, outer_edge, near_mid_ref, near_edge_ref, gain_ref, mgain_ref,
+    par_ref, own_mid, outer_mid, own_edge, outer_edge, near_ref, gain_ref, mgain_ref,
     wq_ref, wkv_ref, wo_ref, wm_ref,
     out_ref,
     near, x2, normed, query, keyval, heads,
 ):
     par, pole = par_ref[0], par_ref[1]
-    near[:, :, 0:16, :] = near_edge_ref[:, :, 0:16, :].astype(F32)
-    near[:, :, 16:64, :] = near_mid_ref[...].astype(F32)
-    near[:, :, 64:80, :] = near_edge_ref[:, :, 16:32, :].astype(F32)
+    near[...] = near_ref[...].astype(F32)
     gain = gain_ref[1:2, :]
     upper = iota((8, D), 0) >= 4
     key_row = (iota((1, 256), 1) // 8) % 8
@@ -468,7 +473,7 @@
     pipelined([norm, project, attention, project_out, merge], [0, 1])
 
 
-def second_block(par, x1_parts, near_mid, near_edge, norm_gain, merge_gain, w_query, w_keyval, w_out, merge_weight):
+def second_block(par, x1_parts, near, norm_gain, merge_gain, w_query, w_keyval, w_out, merge_weight):
     vmem = pl.BlockSpec(memory_space=pltpu.VMEM)
     weights = [
         pltpu.with_memory_space_constraint(w, pltpu.VMEM) for w in (w_query, w_keyval, w_out, merge_weight)
@@ -476,7 +481,7 @@
     return pl.pallas_call(
         second_kernel,
         out_shape=jax.ShapeDtypeStruct((2, 4, 32, 1024), BF),
-        in_specs=[pl.BlockSpec(memory_space=pltpu.SMEM)] + [vmem] * 12,
+        in_specs=[pl.BlockSpec(memory_space=pltpu.SMEM)] + [vmem] * 11,
         out_specs=vmem,
         scratch_shapes=[
             pltpu.VMEM((2, 4, 80, D), F32),
@@ -489,7 +494,7 @@
         compiler_params=params(),
         cost_estimate=pl.CostEstimate(flops=10**10, bytes_accessed=10**7, transcendentals=0),
     )(
-        par, *x1_parts, near_mid, near_edge, norm_gain, merge_gain, *weights
+        par, *x1_parts, near, norm_gain, merge_gain, *weights
     )
 
 
@@ -534,19 +539,18 @@
     wemb = embedding_matrix(embed_weight, land_embed)
     weights = wemb, level_embed, norm_gain, w_query, w_keyval, w_out
     own_mid, send_mid, own = first_block((0,), MIDDLE, edge, place, (own, edge, near), *weights)
-    near_mid = swap(send_mid, 0)
     far, low, high = unpack_far(own_mid, far, own)
     from_low, from_high = around(high, 1), around(low, -1)
     (outer_mid,) = first_block((1,), MIDDLE, own_mid, place, (own, far), *weights)
-    own_edge, send_edge = first_block(
-        (0,), EDGES, outer_mid, place, (own, from_low, from_high), *weights
+    own_edge, send = first_block(
+        (0,), EDGES, outer_mid, place, (own, from_low, from_high, send_mid), *weights
     )
-    near_edge = swap(send_edge, 0)
+    near = swap(send, 0)
     (outer_edge,) = first_block(
         (1,), EDGES, own_edge, place, (own, far, from_low, from_high), *weights
     )
     return second_block(
-        place, (own_mid, outer_mid, own_edge, outer_edge), near_mid, near_edge, norm_gain,
+        place, (own_mid, outer_mid, own_edge, outer_edge), near, norm_gain,
         merge_gain.reshape(1, -1), w_query, w_keyval, w_out, merge_weight,
     )
 

time: 49 us -> 49 us (level)
  starting transfers between devices: 18 us -> 17 us
  waiting for transfers between devices: 0.02 us -> 0.96 us
    ppermute x5 -> x4, waiting for transfers between devices: 0.01 us -> 0.95 us  [swap(): return lax.ppermute(block, 'lat', pairs)]
    ppermute x2, starting transfers between devices: 6.85 us -> 5.96 us  [around(): lax.ppermute(block, 'lon', [(i, (i + distance) % count) for i in range(co...]
    ppermute x5 -> x4, starting transfers between devices: 11.1 us -> 11.1 us  [swap(): return lax.ppermute(block, 'lat', pairs)]
  transfers between devices with their start and end apart: 7 -> 6, of which waited for: 0 -> 1; matrix products, arithmetic and copies ran while one was open for 1% -> 1% of each run, Pallas kernels for 35% -> 27%
where the time goes in v9:
time: 49 us; the launch traced here: 48.8 us
  Pallas kernels  29.8 us (61%)
  starting transfers between devices  17 us (35%)
  waiting for transfers between devices  0.96 us (2%)
  other arithmetic  0.53 us (1%)
    pallas_call x4, Pallas kernels, first_block(): pl.pallas_call(functools.partial(first_kernel, parts, which), out_shape=t...  16.6 us
    ppermute x4, starting transfers between devices, swap(): return lax.ppermute(block, 'lat', pairs)  11.1 us
    pallas_call x1, Pallas kernels, second_block(): pl.pallas_call(second_kernel, out_shape=jax.ShapeDtypeStruct((2, 4, 32, 1...  10.4 us
    ppermute x2, starting transfers between devices, around(): lax.ppermute(block, 'lon', [(i, (i + distance) % count) for i in range(co...  5.96 us
    pallas_call x1, Pallas kernels, patches(): pl.pallas_call(patch_kernel, out_shape=tuple((jax.ShapeDtypeStruct((n, 96...  2.48 us
  transfers between devices with their start and end apart: 6, of which 1 were waited for; matrix products, arithmetic and copies ran while one was open for 1% of the time, Pallas kernels for 27%

profile of v9, /device:TPU:25, one launch (start us, length us, event | category | flops | bytes accessed | tf_op | source)
XLA Modules:
  0.0 48.8 jit_solution(2754304935856305416)
XLA Ops:
  0.0 0.1 pad_add_fusion.par_ref.refs_0_
  0.1 0.0 copy-start.8
  0.1 0.0 copy-start.7
  0.1 2.5 %shard_map.118 = (bf16[8,96,128]{2,1,0:T(8,128)(2,1)S(1)}, bf16[8,96,128]{2,1,0:T(8,128)(2,1)S(1)}, bf16[1,96,128]{2,1,0:T(8,128)(2,1)S(1)}, bf16[1,96,128]{2,1,0:T(8,128)(2,1)S(1)}) custom-call(s32[2]{0:T(128)S(1)} %pad_add_fusion.par_ref.refs_0_, bf16[2,5,32,256]{3,2,1,0:T(8,128)(2,1)} %atmos_any.1, bf16[32,256]{1,0:T(8,128)(2,1)} %oro_any.1, ...), custom_call_target="tpu_custom_call" | custom-call | flops 1000000000 | bytes 1000000 | tf_op jit(solution)/shard_map/pallas_call | solution.py:87
  2.6 0.8 %collective-permute-start = (bf16[1,96,128]{2,1,0:T(8,128)(2,1)S(1)}, bf16[1,96,128]{2,1,0:T(8,128)(2,1)S(1)}, u32[]{:S(2)}, u32[]{:S(2)}) collective-permute-start(bf16[1,96,128]{2,1,0:T(8,128)(2,1)S(1)} %get-tuple-element.17), channel_id=1, source_target_pairs={{0,16},{16,0},{32,48},{48,32},{64,80},{80,64},{96,112},{112,96},{1... | collective-permute-start | bytes 73736 | tf_op jit(solution)/shard_map/ppermute | solution.py:518
  3.3 4.5 %collective-permute-start.1 = (bf16[1,96,128]{2,1,0:T(8,128)(2,1)S(1)}, bf16[1,96,128]{2,1,0:T(8,128)(2,1)S(1)}, u32[]{:S(2)}, u32[]{:S(2)}) collective-permute-start(bf16[1,96,128]{2,1,0:T(8,128)(2,1)S(1)} %get-tuple-element.19), channel_id=1, source_target_pairs={{16,32},{32,16},{48,64},{64,48},{80,96},{96,80},{112,128},{128,112... | collective-permute-start | bytes 73736 | tf_op jit(solution)/shard_map/ppermute | solution.py:518
  7.9 0.0 copy-done.8
  7.9 0.0 copy-done.7
  7.9 0.2 pad.4
  8.2 0.0 copy-start.5
  8.2 0.0 copy-start.6
  8.2 0.4 fusion
  8.7 0.0 collective-permute-done.after_ref.refs_2_
  8.7 2.5 %collective-permute-start.2 = (bf16[8,96,128]{2,1,0:T(8,128)(2,1)S(1)}, bf16[8,96,128]{2,1,0:T(8,128)(2,1)S(1)}, u32[]{:S(2)}, u32[]{:S(2)}) collective-permute-start(bf16[8,96,128]{2,1,0:T(8,128)(2,1)S(1)} %constant_dynamic-update-slice_fusion), channel_id=1, source_target_pairs={{16,32},{32,16},{48,64},{64,48},{80,96},{96,80},{112,128},{128,112... | collective-permute-start | bytes 589832 | tf_op jit(solution)/shard_map/ppermute | solution.py:518
  11.2 0.0 collective-permute-done.1.refs_3_
  11.2 0.0 copy-done.5
  11.2 0.0 copy-done.6
  11.2 0.0 copy-start.3
  11.2 5.3 %shard_map.119 = (f32[2,8,48,512]{3,2,1,0:T(8,128)S(1)}, bf16[2,4,48,512]{3,2,1,0:T(8,128)(2,1)S(1)}, bf16[2,10,64,128]{3,2,1,0:T(8,128)(2,1)S(1)}) custom-call(bf16[1,96,128]{2,1,0:T(8,128)(2,1)S(1)} %collective-permute-done.after_ref.refs_2_, s32[2]{0:T(128)S(1)} %pad_add_fusion.par_ref.refs_0_, bf16[8,96,128]{2,1,0:T(8,128)(2,1)S(1)} %get-tuple-element.18.refs_1_, ...), custom_call_target="tpu_custom_call" | custom-call | flops 10000000000 | bytes 10000000 | tf_op jit(solution)/shard_map/pallas_call | solution.py:377
  16.5 0.9 %collective-permute-done.2.packed_ref = bf16[8,96,128]{2,1,0:T(8,128)(2,1)S(1)} collective-permute-done((bf16[8,96,128]{2,1,0:T(8,128)(2,1)S(1)}, bf16[8,96,128]{2,1,0:T(8,128)(2,1)S(1)}, u32[]{:S(2)}, u32[]{:S(2)}) %collective-permute-start.2) | collective-permute-done | bytes 196640 | tf_op jit(solution)/shard_map/ppermute | solution.py:518
  17.5 0.0 copy-start.1
  17.5 0.0 copy-start.2
  17.5 0.3 shard_map.120
  17.7 1.7 %collective-permute-start.3 = (bf16[21,16,128]{2,1,0:T(8,128)(2,1)S(1)}, bf16[21,16,128]{2,1,0:T(8,128)(2,1)S(1)}, u32[]{:S(2)}, u32[]{:S(2)}) collective-permute-start(bf16[21,16,128]{2,1,0:T(8,128)(2,1)S(1)} %get-tuple-element.24), channel_id=1, source_target_pairs={{0,1},{1,2},{2,3},{3,4},{4,5},{5,6},{6,7},{7,8},{8,9},{9,10},{10,1... | collective-permute-start | bytes 258056 | tf_op jit(solution)/shard_map/ppermute | solution.py:523
  19.5 4.2 %collective-permute-start.4 = (bf16[21,16,128]{2,1,0:T(8,128)(2,1)S(1)}, bf16[21,16,128]{2,1,0:T(8,128)(2,1)S(1)}, u32[]{:S(2)}, u32[]{:S(2)}) collective-permute-start(bf16[21,16,128]{2,1,0:T(8,128)(2,1)S(1)} %get-tuple-element.25), channel_id=1, source_target_pairs={{0,15},{1,0},{2,1},{3,2},{4,3},{5,4},{6,5},{7,6},{8,7},{9,8},{10,9... | collective-permute-start | bytes 258056 | tf_op jit(solution)/shard_map/ppermute | solution.py:523
  23.7 0.0 copy-done.3
  23.7 0.0 copy-done.1
  23.7 0.0 copy-done.2
  23.7 4.3 %shard_map.121.after_ref.outer_mid = f32[2,4,48,512]{3,2,1,0:T(8,128)S(1)} custom-call(f32[2,8,48,512]{3,2,1,0:T(8,128)S(1)} %get-tuple-element.20.after_ref.own_mid, s32[2]{0:T(128)S(1)} %pad_add_fusion.par_ref.refs_0_, bf16[2,10,64,128]{3,2,1,0:T(8,128)(2,1)S(1)} %get-tuple-element.21.own_ref.refs_1_, ...), custom_call_target="tpu_custom_call" | custom-call | flops 10000000000 | bytes 10000000 | tf_op jit(solution)/shard_map/pallas_call | solution.py:377
  28.0 0.0 collective-permute-done.3.refs_2_.refs_3_
  28.1 0.0 collective-permute-done.4.refs_3_.refs_4_
  28.1 3.6 %shard_map.122 = (f32[2,8,32,512]{3,2,1,0:T(8,128)S(1)}, bf16[2,4,80,512]{3,2,1,0:T(8,128)(2,1)S(1)}) custom-call(f32[2,4,48,512]{3,2,1,0:T(8,128)S(1)} %shard_map.121.after_ref.outer_mid, s32[2]{0:T(128)S(1)} %pad_add_fusion.par_ref.refs_0_, bf16[2,10,64,128]{3,2,1,0:T(8,128)(2,1)S(1)} %get-tuple-element.21.own_ref.refs_1_, ...), custom_call_target="tpu_custom_call" | custom-call | flops 10000000000 | bytes 10000000 | tf_op jit(solution)/shard_map/pallas_call | solution.py:377
  31.7 3.3 %collective-permute-start.5 = (bf16[2,4,80,512]{3,2,1,0:T(8,128)(2,1)S(1)}, bf16[2,4,80,512]{3,2,1,0:T(8,128)(2,1)S(1)}, u32[]{:S(2)}, u32[]{:S(2)}) collective-permute-start(bf16[2,4,80,512]{3,2,1,0:T(8,128)(2,1)S(1)} %get-tuple-element.28), channel_id=1, source_target_pairs={{0,16},{16,0},{32,48},{48,32},{64,80},{80,64},{96,112},{112,96},{1... | collective-permute-start | bytes 1966088 | tf_op jit(solution)/shard_map/ppermute | solution.py:518
  35.0 0.0 copy-start
  35.0 0.0 copy-start.4
  35.0 3.4 %shard_map.123.outer_edge = f32[2,4,32,512]{3,2,1,0:T(8,128)S(1)} custom-call(f32[2,8,32,512]{3,2,1,0:T(8,128)S(1)} %get-tuple-element.27.after_ref.own_edge, s32[2]{0:T(128)S(1)} %pad_add_fusion.par_ref.refs_0_, bf16[2,10,64,128]{3,2,1,0:T(8,128)(2,1)S(1)} %get-tuple-element.21.own_ref.refs_1_, bf16[2,8,64,128]{3,2,1,0:T(8,128)(2,1)S(1)} %get-tuple-element.23.refs_2_, ...), custom_call_target="tpu_custom_call" | custom-call | flops 10000000000 | bytes 10000000 | tf_op jit(solution)/shard_map/pallas_call | solution.py:377
  38.3 0.0 collective-permute-done.5.near_ref
  38.4 0.0 copy-done
  38.4 0.0 copy-done.4
  38.4 10.4 %shard_map.124 = bf16[2,4,32,1024]{3,2,1,0:T(8,128)(2,1)} custom-call(s32[2]{0:T(128)S(1)} %pad_add_fusion.par_ref.refs_0_, f32[2,8,48,512]{3,2,1,0:T(8,128)S(1)} %get-tuple-element.20.after_ref.own_mid, f32[2,4,48,512]{3,2,1,0:T(8,128)S(1)} %shard_map.121.after_ref.outer_mid, f32[2,8,32,512]{3,2,1,0:T(8,128)S(1)} %get-tuple-element.27.after_ref.own_edge, ...), custom_call_target="tpu_custom_call" | custom-call | flops 10000000000 | bytes 10000000 | tf_op jit(solution)/shard_map/pallas_call | solution.py:481
  (4 shorter events, 0.0 us)
Async XLA Ops:
  0.1 7.8 %copy-start.8 = (f32[512]{0:T(512)S(1)}, f32[512]{0:T(512)}, u32[]{:S(2)}) copy-start(f32[512]{0:T(512)} %param.17) | copy-start | bytes 6148
  0.1 7.9 %copy-start.7 = (bf16[12,12,6,512]{3,2,1,0:T(8,128)(2,1)S(1)}, bf16[12,12,6,512]{3,2,1,0:T(8,128)(2,1)}, u32[]{:S(2)}) copy-start(bf16[12,12,6,512]{3,2,1,0:T(8,128)(2,1)} %param.15) | copy-start | bytes 2654212
  2.6 6.1 %collective-permute-start = (bf16[1,96,128]{2,1,0:T(8,128)(2,1)S(1)}, bf16[1,96,128]{2,1,0:T(8,128)(2,1)S(1)}, u32[]{:S(2)}, u32[]{:S(2)}) collective-permute-start(bf16[1,96,128]{2,1,0:T(8,128)(2,1)S(1)} %get-tuple-element.17), channel_id=1, source_target_pairs={{0,16},{16,0},{32,48},{48,32},{64,80},{80,64},{96,112},{112,96},{1... | collective-permute-start | bytes 73736 | tf_op jit(solution)/shard_map/ppermute | solution.py:518
  3.3 7.9 %collective-permute-start.1 = (bf16[1,96,128]{2,1,0:T(8,128)(2,1)S(1)}, bf16[1,96,128]{2,1,0:T(8,128)(2,1)S(1)}, u32[]{:S(2)}, u32[]{:S(2)}) collective-permute-start(bf16[1,96,128]{2,1,0:T(8,128)(2,1)S(1)} %get-tuple-element.19), channel_id=1, source_target_pairs={{16,32},{32,16},{48,64},{64,48},{80,96},{96,80},{112,128},{128,112... | collective-permute-start | bytes 73736 | tf_op jit(solution)/shard_map/ppermute | solution.py:518
  8.2 3.0 %copy-start.5 = (f32[2,512]{1,0:T(2,128)S(1)}, f32[2,512]{1,0:T(2,128)}, u32[]{:S(2)}) copy-start(f32[2,512]{1,0:T(2,128)} %refs_6_.7) | copy-start | bytes 12292
  8.2 3.0 %copy-start.6 = (f32[2,512]{1,0:T(2,128)S(1)}, f32[2,512]{1,0:T(2,128)}, u32[]{:S(2)}) copy-start(f32[2,512]{1,0:T(2,128)} %gain_ref.1) | copy-start | bytes 12292
  8.7 8.8 %collective-permute-start.2 = (bf16[8,96,128]{2,1,0:T(8,128)(2,1)S(1)}, bf16[8,96,128]{2,1,0:T(8,128)(2,1)S(1)}, u32[]{:S(2)}, u32[]{:S(2)}) collective-permute-start(bf16[8,96,128]{2,1,0:T(8,128)(2,1)S(1)} %constant_dynamic-update-slice_fusion), channel_id=1, source_target_pairs={{16,32},{32,16},{48,64},{64,48},{80,96},{96,80},{112,128},{128,112... | collective-permute-start | bytes 589832 | tf_op jit(solution)/shard_map/ppermute | solution.py:518
  11.2 12.5 %copy-start.3 = (bf16[2,512,512]{2,1,0:T(8,128)(2,1)S(1)}, bf16[2,512,512]{2,1,0:T(8,128)(2,1)}, u32[]{:S(2)}) copy-start(bf16[2,512,512]{2,1,0:T(8,128)(2,1)} %wo_ref.1) | copy-start | bytes 3145732
  17.5 6.2 %copy-start.1 = (bf16[2,512,1024]{2,1,0:T(8,128)(2,1)S(1)}, bf16[2,512,1024]{2,1,0:T(8,128)(2,1)}, u32[]{:S(2)}) copy-start(bf16[2,512,1024]{2,1,0:T(8,128)(2,1)} %wkv_ref.1) | copy-start | bytes 6291460
  17.5 6.2 %copy-start.2 = (bf16[2,512,512]{2,1,0:T(8,128)(2,1)S(1)}, bf16[2,512,512]{2,1,0:T(8,128)(2,1)}, u32[]{:S(2)}) copy-start(bf16[2,512,512]{2,1,0:T(8,128)(2,1)} %wq_ref.1) | copy-start | bytes 3145732
  17.7 10.3 %collective-permute-start.3 = (bf16[21,16,128]{2,1,0:T(8,128)(2,1)S(1)}, bf16[21,16,128]{2,1,0:T(8,128)(2,1)S(1)}, u32[]{:S(2)}, u32[]{:S(2)}) collective-permute-start(bf16[21,16,128]{2,1,0:T(8,128)(2,1)S(1)} %get-tuple-element.24), channel_id=1, source_target_pairs={{0,1},{1,2},{2,3},{3,4},{4,5},{5,6},{6,7},{7,8},{8,9},{9,10},{10,1... | collective-permute-start | bytes 258056 | tf_op jit(solution)/shard_map/ppermute | solution.py:523
  19.5 8.6 %collective-permute-start.4 = (bf16[21,16,128]{2,1,0:T(8,128)(2,1)S(1)}, bf16[21,16,128]{2,1,0:T(8,128)(2,1)S(1)}, u32[]{:S(2)}, u32[]{:S(2)}) collective-permute-start(bf16[21,16,128]{2,1,0:T(8,128)(2,1)S(1)} %get-tuple-element.25), channel_id=1, source_target_pairs={{0,15},{1,0},{2,1},{3,2},{4,3},{5,4},{6,5},{7,6},{8,7},{9,8},{10,9... | collective-permute-start | bytes 258056 | tf_op jit(solution)/shard_map/ppermute | solution.py:523
  31.7 6.7 %collective-permute-start.5 = (bf16[2,4,80,512]{3,2,1,0:T(8,128)(2,1)S(1)}, bf16[2,4,80,512]{3,2,1,0:T(8,128)(2,1)S(1)}, u32[]{:S(2)}, u32[]{:S(2)}) collective-permute-start(bf16[2,4,80,512]{3,2,1,0:T(8,128)(2,1)S(1)} %get-tuple-element.28), channel_id=1, source_target_pairs={{0,16},{16,0},{32,48},{48,32},{64,80},{80,64},{96,112},{112,96},{1... | collective-permute-start | bytes 1966088 | tf_op jit(solution)/shard_map/ppermute | solution.py:518
  35.0 3.4 %copy-start = (bf16[2048,1024]{1,0:T(8,128)(2,1)S(1)}, bf16[2048,1024]{1,0:T(8,128)(2,1)}, u32[]{:S(2)}) copy-start(bf16[2048,1024]{1,0:T(8,128)(2,1)} %wm_ref.1) | copy-start | bytes 12582916
  35.0 3.4 %copy-start.4 = (f32[2048]{0:T(1024)S(1)}, f32[2048]{0:T(1024)}, u32[]{:S(2)}) copy-start(f32[2048]{0:T(1024)} %param.22) | copy-start | bytes 24580
